TPU v7x, 32 devices: a whole 2x2x4 slice. The times are simulated.
32 devices in a mesh: pb: 2 (over x), ka: 4 (over z), ha: 4 (over y, core).
Axes of the slice: x: 2, y: 2, z: 4, core: 2. Of those that a mesh axis runs over, the one named last changes fastest.
Arguments:
- queries: bfloat16 [768, 64, 128], P('pb', 'ha'), may hold values from -6 to 6
- key_codes: bfloat16 [768, 8, 128], P('ka', 'ha'), may hold values from -4 to 4
- key_scale_powers: int32 [12, 8], P('ka', 'ha'), may hold values from -1 to 1
- values: bfloat16 [768, 8, 128], P('ka', 'ha'), may hold values from -6 to 6
- grad_out: bfloat16 [768, 64, 128], P('pb', 'ha'), may hold values from -1.5 to 1.5
- grad_dot: float32 [768, 64], P('pb', 'ha'), may hold values from -6 to 6
- log_totals: float32 [768, 64], P('pb', 'ha')
Outputs:
- grad_queries: bfloat16 [768, 64, 128], P(('pb', 'ka'), 'ha')
- grad_keys: bfloat16 [768, 8, 128], P('ka', 'ha')
- grad_values: bfloat16 [768, 8, 128], P('ka', 'ha')
All inputs are finite; a program needn't handle non-finite values.
Results may differ from a plain program's by a relative error of at most 0.012.
Values may be sent and summed in bfloat16 or wider, within the bound.
No kernel may reach another device: no remote copies, remote signals or barrier semaphores. Data moves between devices by JAX's collectives and lax.ppermute only.
A program may use at most 64 MiB of HBM per device.

v0:
```python
import jax
import jax.numpy as jnp
from jax import lax
from jax.sharding import PartitionSpec as P

KEYS_PER_SCALE = 64


def head_grads(
    query_block, grad_block, dot_block, total_block, key_block, value_block, query_pos, key_pos
):
    inverse_root = query_block.shape[-1] ** (-0.5)
    scores = (
        jnp.einsum("igd,jd->gij", query_block, key_block, preferred_element_type=jnp.float32)
        * inverse_root
    )
    visible = key_pos[None, :] <= query_pos[:, None]
    weights = jnp.where(visible[None], jnp.exp(scores - total_block.T[:, :, None]), 0.0)
    weights_low = weights.astype(jnp.bfloat16)
    grad_values = jnp.einsum(
        "gij,igd->jd", weights_low, grad_block, preferred_element_type=jnp.float32
    )
    grad_weights = jnp.einsum(
        "igd,jd->gij", grad_block, value_block, preferred_element_type=jnp.float32
    )
    grad_scores = (weights * (grad_weights - dot_block.T[:, :, None])).astype(jnp.bfloat16)
    grad_query = (
        jnp.einsum("gij,jd->igd", grad_scores, key_block, preferred_element_type=jnp.float32)
        * inverse_root
    )
    grad_keys = (
        jnp.einsum("gij,igd->jd", grad_scores, query_block, preferred_element_type=jnp.float32)
        * inverse_root
    )
    return (grad_query, grad_keys, grad_values)


def per_device(queries, key_codes, key_scale_powers, values, grad_out, grad_dot, log_totals):
    query_count, head_count, head_width = queries.shape
    key_count, kv_heads, _ = key_codes.shape
    queries_per_group = head_count // kv_heads
    key_devices = lax.axis_size("ka")
    factor = jnp.exp2(key_scale_powers.astype(jnp.float32))
    dequantized = (
        key_codes.astype(jnp.float32) * jnp.repeat(factor, KEYS_PER_SCALE, axis=0)[:, :, None]
    )
    key_total = lax.psum(jnp.sum(dequantized, axis=0), "ka")
    smoothed = (dequantized - key_total / (key_count * key_devices)).astype(jnp.bfloat16)
    query_in, grads_in, dots_in, totals_in = (queries, grad_out, grad_dot, log_totals)
    keys_in, values_in = (smoothed, values)
    query_pos = lax.axis_index("pb") * query_count + lax.iota(jnp.int32, query_count)
    key_pos = lax.axis_index("ka") * key_count + lax.iota(jnp.int32, key_count)
    blocks = ((0, 0),)
    halves = 1
    outer = 1
    query_step = query_count // halves
    key_step = key_count // halves
    query_parts = []
    key_parts = []
    value_parts = []
    for kv_head in range(kv_heads):
        chosen = slice(kv_head * queries_per_group, (kv_head + 1) * queries_per_group)
        query_sums = [None] * halves
        key_sums_local = [None] * halves
        value_sums = [None] * halves
        query_half, key_half = blocks[0]
        query_range = slice(query_half * query_step, (query_half + 1) * query_step)
        key_range = slice(key_half * key_step, (key_half + 1) * key_step)
        part_query, part_keys, part_values = head_grads(
            query_in[query_range, chosen],
            grads_in[query_range, chosen],
            dots_in[query_range, chosen],
            totals_in[query_range, chosen],
            keys_in[key_range, kv_head],
            values_in[key_range, kv_head],
            query_pos,
            key_pos,
        )
        query_sums[query_half] = part_query
        key_sums_local[key_half] = part_keys
        value_sums[key_half] = part_values
        query_parts.append(query_sums[0])
        key_parts.append(key_sums_local[0])
        value_parts.append(value_sums[0])
    grad_query = jnp.concatenate(query_parts, axis=1)
    grad_keys = jnp.stack(key_parts, axis=1)
    grad_values = jnp.stack(value_parts, axis=1)
    share = query_count // key_devices
    summed = lax.psum_scatter(
        grad_query.reshape(outer, key_devices, share // outer, head_count, head_width),
        "ka",
        scatter_dimension=1,
        tiled=True,
    )
    key_sum, value_sum = lax.psum((grad_keys, grad_values), "pb")
    query_out = summed.reshape(share, head_count, head_width).astype(jnp.bfloat16)
    keys_out = key_sum.astype(jnp.bfloat16)
    values_out = value_sum.astype(jnp.bfloat16)
    return (query_out, keys_out, values_out)


def solution(mesh):
    in_specs = (
        P("pb", "ha", None),
        P("ka", "ha", None),
        P("ka", "ha"),
        P("ka", "ha", None),
        P("pb", "ha", None),
        P("pb", "ha"),
        P("pb", "ha"),
    )
    out_specs = (P(("pb", "ka"), "ha", None), P("ka", "ha", None), P("ka", "ha", None))
    return jax.shard_map(
        per_device, mesh=mesh, in_specs=in_specs, out_specs=out_specs, check_vma=False
    )
```

profile of v0, /device:TPU:0, one launch (start us, length us, event | category | flops | bytes accessed | tf_op | source)
XLA Modules:
  0.0 102.8 jit_solution(17560217914583388102)
XLA Ops:
  7.2 0.8 multiply_exponential_fusion
  8.2 1.0 fusion.36
  9.2 13.5 %psum.21 = f32[2,128]{1,0:T(2,128)S(1)} all-reduce(f32[2,128]{1,0:T(2,128)S(1)} %fusion.36), channel_id=1, replica_groups=mesh['pb'=2,'ka'=4,'ha'=4] {'ka'}, use_global_device_ids=true, to_apply=%region_1.0 | all-reduce | flops 256 | bytes 2048 | tf_op jit(solution)/shard_map/psum | solution.py:47
  22.7 1.0 subtract_convert_fusion
  23.7 1.1 %fusion.43 = (bf16[192,1,128]{2,1,0:T(2,128)(2,1)S(1)}, bf16[192,1,128]{2,1,0:T(2,128)(2,1)S(1)}) fusion(bf16[192,2,128]{2,1,0:T(2,128)(2,1)} %param.10), kind=kLoop, calls=%fused_computation.64 | loop fusion | bytes 196608 | tf_op jit(solution)/shard_map/slice | solution.py:75
  24.9 1.5 %fusion.42 = (bf16[384,8,128]{2,1,0:T(8,128)(2,1)S(1)}, bf16[384,8,128]{2,1,0:T(8,128)(2,1)S(1)}) fusion(bf16[384,16,128]{2,1,0:T(8,128)(2,1)} %param.7), kind=kLoop, calls=%fused_computation.63 | loop fusion | bytes 3145728 | tf_op jit(solution)/shard_map/slice | solution.py:70
  27.3 0.9 fusion.5
  28.2 0.5 copy-done.4
  29.1 0.5 fusion.29
  29.8 0.9 fusion.1
  30.7 0.5 copy-done.6
  31.2 1.1 %copy-done.11 = bf16[8,384,192]{1,2,0:T(8,128)(2,1)} copy-done((bf16[8,384,192]{1,2,0:T(8,128)(2,1)}, bf16[8,384,192]{1,2,0:T(8,128)(2,1)S(1)}, u32[]{:S(2)}) %copy-start.11) | copy-done | bytes 1179672
  33.0 2.4 %copy.27 = f32[384,16,128]{2,1,0:T(8,128)} copy(f32[384,16,128]{0,2,1:T(8,128)S(1)} %pad_maximum_fusion) | data formatting | bytes 6291456 | tf_op jit(solution)/shard_map/concatenate | solution.py:85
  35.4 1.1 %copy-done.3 = bf16[384,8,128]{2,1,0:T(8,128)(2,1)S(1)} copy-done((bf16[384,8,128]{2,1,0:T(8,128)(2,1)S(1)}, bf16[384,8,128]{2,1,0:T(8,128)(2,1)}, u32[]{:S(2)}) %copy-start.3) | copy-done | bytes 786456
  36.9 0.5 fusion.25
  37.4 2.0 %fusion.23 = f32[192,1,128]{2,0,1:T(8,128)S(1)} fusion(bf16[8,384,192]{1,2,0:T(8,128)(2,1)} %copy-done.11, bf16[384,8,128]{2,1,0:T(8,128)(2,1)S(1)} %copy-done.1), kind=kOutput, calls=%fused_computation.25 | convolution fusion | flops 151019520 | bytes 2064384 | tf_op jit(solution)/shard_map/gij,igd->jd/dot_general | solution.py:32
  39.4 0.7 fusion.16
  40.1 1.2 %copy-done.7 = f32[192,384,8]{1,0,2:T(8,128)S(1)} copy-done((f32[192,384,8]{1,0,2:T(8,128)S(1)}, f32[192,384,8]{1,0,2:T(8,128)}, u32[]{:S(2)}) %copy-start.7) | copy-done | bytes 2359320
  41.5 0.7 fusion.19
  42.2 15.1 %all-reduce.2 = (bf16[192,2,128]{2,0,1:T(8,128)(2,1)S(1)}, bf16[192,2,128]{2,0,1:T(8,128)(2,1)S(1)}) all-reduce(f32[192,2,128]{2,0,1:T(8,128)S(1)} %pad_maximum_fusion.1, f32[192,2,128]{2,0,1:T(8,128)S(1)} %pad_maximum_fusion.2), channel_id=1, replica_groups=mesh['pb'=2,'ka'=4,'ha'=4] {'pb'}, use_global_device_ids=true, to_apply=%region_3.4 | all-reduce | flops 98304 | bytes 589824 | tf_op jit(solution)/shard_map/psum | solution.py:95
  57.3 0.7 copy.28
  58.0 0.7 copy.29
  58.7 35.3 %reduce-scatter.2.cloned.1.call-done = f32[1,1,96,16,128]{4,3,2,1,0:T(8,128)} async-done(((f32[1,4,96,16,128]{4,3,2,1,0:T(8,128)}), f32[1,1,96,16,128]{4,3,2,1,0:T(8,128)}) %reduce-scatter.2.cloned.1.call-update) | async-done | bytes 786448 | tf_op jit(solution)/shard_map/reduce_scatter | solution.py:89
  94.0 1.9 %convert_bitcast_fusion = bf16[96,16,128]{2,1,0:T(8,128)(2,1)} fusion(f32[1,1,96,16,128]{4,3,2,1,0:T(8,128)} %reduce-scatter.2.cloned.1.call-done), kind=kLoop, calls=%fused_computation.39 | loop fusion | flops 196608 | bytes 1179648 | tf_op jit(solution)/shard_map/convert_element_type | solution.py:96
  (47 shorter events, 2.9 us)
Async XLA Ops:
  7.2 19.2 %copy-start.8 = (bf16[384,16,128]{2,1,0:T(8,128)(2,1)S(1)}, bf16[384,16,128]{2,1,0:T(8,128)(2,1)}, u32[]{:S(2)}) copy-start(bf16[384,16,128]{2,1,0:T(8,128)(2,1)} %param.11) | copy-start | bytes 4718596
  7.2 86.8 %reduce-scatter.2.cloned.1.call-start = ((), (), s32[]{:S(2)}) async-start(), calls=%async_computation.1 | async-start | bytes 3932160 | tf_op jit(solution)/shard_map/reduce_scatter | solution.py:89
  24.8 1.7 %copy-start.16 = (f32[384,16]{0,1:T(8,128)S(1)}, f32[384,16]{0,1:T(8,128)}, u32[]{:S(2)}) copy-start(f32[384,16]{0,1:T(8,128)} %param.12) | copy-start | bytes 73732
  24.9 1.7 %copy-start.17 = (f32[384,16]{0,1:T(8,128)S(1)}, f32[384,16]{0,1:T(8,128)}, u32[]{:S(2)}) copy-start(f32[384,16]{0,1:T(8,128)} %param.13) | copy-start | bytes 73732
  26.4 0.9 copy-start.2
  26.4 2.8 %copy-start = (bf16[384,8,128]{2,1,0:T(8,128)(2,1)}, bf16[384,8,128]{2,1,0:T(8,128)(2,1)S(1)}, u32[]{:S(2)}) copy-start(bf16[384,8,128]{2,1,0:T(8,128)(2,1)S(1)} %get-tuple-element.14) | copy-start | bytes 2359300
  26.5 1.7 %copy-start.14 = (bf16[384,8,128]{2,1,0:T(8,128)(2,1)}, bf16[384,8,128]{2,1,0:T(8,128)(2,1)S(1)}, u32[]{:S(2)}) copy-start(bf16[384,8,128]{2,1,0:T(8,128)(2,1)S(1)} %get-tuple-element.11) | copy-start | bytes 2359300
  26.5 3.2 %copy-start.12 = (bf16[384,8,128]{2,1,0:T(8,128)(2,1)}, bf16[384,8,128]{2,1,0:T(8,128)(2,1)S(1)}, u32[]{:S(2)}) copy-start(bf16[384,8,128]{2,1,0:T(8,128)(2,1)S(1)} %get-tuple-element.12) | copy-start | bytes 2359300
  27.2 1.5 %copy-start.4 = (f32[192,384,8]{1,0,2:T(8,128)}, f32[192,384,8]{1,0,2:T(8,128)S(1)}, u32[]{:S(2)}) copy-start(f32[192,384,8]{1,0,2:T(8,128)S(1)} %fusion.34) | copy-start | bytes 7077892
  28.7 1.0 copy-start.9
  29.8 1.5 %copy-start.6 = (f32[192,384,8]{1,0,2:T(8,128)}, f32[192,384,8]{1,0,2:T(8,128)S(1)}, u32[]{:S(2)}) copy-start(f32[192,384,8]{1,0,2:T(8,128)S(1)} %fusion.29) | copy-start | bytes 7077892
  31.2 1.1 %copy-start.11 = (bf16[8,384,192]{1,2,0:T(8,128)(2,1)}, bf16[8,384,192]{1,2,0:T(8,128)(2,1)S(1)}, u32[]{:S(2)}) copy-start(bf16[8,384,192]{1,2,0:T(8,128)(2,1)S(1)} %fusion.1) | copy-start | bytes 3538948
  35.3 1.1 %copy-start.3 = (bf16[384,8,128]{2,1,0:T(8,128)(2,1)S(1)}, bf16[384,8,128]{2,1,0:T(8,128)(2,1)}, u32[]{:S(2)}) copy-start(bf16[384,8,128]{2,1,0:T(8,128)(2,1)} %copy-done.2) | copy-start | bytes 2359300
  35.3 1.5 %copy-start.10 = (bf16[8,384,192]{1,2,0:T(8,128)(2,1)S(1)}, bf16[8,384,192]{1,2,0:T(8,128)(2,1)}, u32[]{:S(2)}) copy-start(bf16[8,384,192]{1,2,0:T(8,128)(2,1)} %copy-done.9) | copy-start | bytes 3538948
  35.3 2.0 %copy-start.1 = (bf16[384,8,128]{2,1,0:T(8,128)(2,1)S(1)}, bf16[384,8,128]{2,1,0:T(8,128)(2,1)}, u32[]{:S(2)}) copy-start(bf16[384,8,128]{2,1,0:T(8,128)(2,1)} %copy-done) | copy-start | bytes 2359300
  36.9 2.5 %copy-start.5 = (f32[192,384,8]{1,0,2:T(8,128)S(1)}, f32[192,384,8]{1,0,2:T(8,128)}, u32[]{:S(2)}) copy-start(f32[192,384,8]{1,0,2:T(8,128)} %copy-done.4) | copy-start | bytes 7077892
  36.9 2.5 %copy-start.15 = (bf16[384,8,128]{2,1,0:T(8,128)(2,1)S(1)}, bf16[384,8,128]{2,1,0:T(8,128)(2,1)}, u32[]{:S(2)}) copy-start(bf16[384,8,128]{2,1,0:T(8,128)(2,1)} %copy-done.14) | copy-start | bytes 2359300
  39.3 2.0 %copy-start.7 = (f32[192,384,8]{1,0,2:T(8,128)S(1)}, f32[192,384,8]{1,0,2:T(8,128)}, u32[]{:S(2)}) copy-start(f32[192,384,8]{1,0,2:T(8,128)} %copy-done.6) | copy-start | bytes 7077892
  39.3 2.1 %copy-start.13 = (bf16[384,8,128]{2,1,0:T(8,128)(2,1)S(1)}, bf16[384,8,128]{2,1,0:T(8,128)(2,1)}, u32[]{:S(2)}) copy-start(bf16[384,8,128]{2,1,0:T(8,128)(2,1)} %copy-done.12) | copy-start | bytes 2359300
Sparse Core Ops, SparseCore 0:
  35.5 58.4 reduce-scatter.1
where the time goes:
time: 103 us
  waiting for transfers between devices  35.3 us (34%)
  blocking collectives  28.5 us (28%)
  between operations  14.3 us (14%)
  local copies, waits for them, and re-layouts  12.1 us (12%)
  matrix products  7.34 us (7%)
  other arithmetic  5.18 us (5%)
    reduce_scatter x1, waiting for transfers between devices, per_device(): lax.psum_scatter(grad_query.reshape(outer, key_devices, share // outer, h...  35.3 us
    psum x1, blocking collectives, per_device(): key_sum, value_sum = lax.psum((grad_keys, grad_values), 'pb')  15.1 us
    psum x1, blocking collectives, per_device(): key_total = lax.psum(jnp.sum(dequantized, axis=0), 'ka')  13.5 us
    unnamed x38, local copies, waits for them, and re-layouts  6.83 us
    dot_general x2, matrix products, head_grads(): jnp.einsum('gij,igd->jd', grad_scores, query_block, preferred_element_typ...  2.45 us
    concatenate x1, local copies, waits for them, and re-layouts, per_device(): grad_query = jnp.concatenate(query_parts, axis=1)  2.38 us
  transfers between devices with their start and end apart: 1, of which 1 were waited for; matrix products, arithmetic and copies ran while one was open for 5% of the time, Pallas kernels for 0%

commit v1 on v0

v1 whole, which is shorter than its diff:
```python
import functools
import math

import jax
import jax.numpy as jnp
from jax import lax
from jax.experimental import pallas as pl
from jax.experimental.pallas import tpu as pltpu
from jax.sharding import PartitionSpec as P

KEYS_PER_SCALE = 64
LOG2E = math.log2(math.e)
VMEM = pl.BlockSpec(memory_space=pltpu.VMEM)
SMEM = pl.BlockSpec(memory_space=pltpu.SMEM)
NT = (((1,), (1,)), ((), ()))
SUM_ROWS = 8


def prep_kernel(powers_ref, codes_ref, values_ref, packed_ref, sums_ref):
    key_count, kv_heads, width = codes_ref.shape
    rows = lax.broadcasted_iota(jnp.int32, (key_count, width), 0) // KEYS_PER_SCALE
    sums_ref[...] = jnp.zeros_like(sums_ref)
    codes = codes_ref[...].astype(jnp.float32)
    values = values_ref[...].astype(jnp.float32)
    for g in range(kv_heads):
        factor = jnp.zeros((key_count, width), jnp.float32)
        for b in range(key_count // KEYS_PER_SCALE):
            power = jnp.left_shift(1, powers_ref[b, g] + 8).astype(jnp.float32) * 2.0**-8
            factor = jnp.where(rows == b, power, factor)
        wide = codes[:, g, :] * factor
        packed_ref[g] = wide.astype(jnp.bfloat16)
        packed_ref[kv_heads + g] = values[:, g, :].astype(jnp.bfloat16)
        sums_ref[pl.ds(g, 1)] = jnp.sum(wide, axis=0, keepdims=True)


def rows_kernel(
    shifts, share, kv_heads, key_devices, first,
    q_ref, do_ref, stats_ref, own_ref, got_ref, *refs,
):
    if first:
        sums_ref, dq_ref, acc_ref, smooth_ref = refs
    else:
        smooth_ref, acc_in_ref, dq_ref, keep_ref, send_ref = refs
    ka, pb = lax.axis_index("ka"), lax.axis_index("pb")
    key_count, width = own_ref.shape[1:]
    heads = q_ref.shape[1]
    group = heads // kv_heads
    cols = share * group
    root = width**-0.5
    own_base, got_base = ka * key_count, (ka ^ 1) * key_count
    line = lax.broadcasted_iota(jnp.int32, (2 * key_count, cols), 0)
    key_pos = line + jnp.where(line < key_count, own_base, got_base - key_count)
    lead = key_pos - lax.broadcasted_iota(jnp.int32, (2 * key_count, cols), 1) // group
    smooth, turned, vals = [], [], []
    for g in range(kv_heads):
        if first:
            own = own_ref[g].astype(jnp.float32)
            got = got_ref[g].astype(jnp.float32)
            total = jnp.sum(own, axis=0, keepdims=True) + jnp.sum(got, axis=0, keepdims=True)
            total = total + sums_ref[pl.ds(g, 1)]
            mean = total / (key_count * key_devices)
            k = jnp.concatenate([own - mean, got - mean], axis=0).astype(jnp.bfloat16)
            smooth_ref[g] = k
        else:
            k = smooth_ref[g]
        smooth.append(k)
        turned.append(k.astype(jnp.float32).T.astype(jnp.bfloat16))
        vals.append(jnp.concatenate([own_ref[kv_heads + g], got_ref[kv_heads + g]], axis=0))
    dks = [None] * kv_heads
    dvs = [None] * kv_heads
    for at, shift in enumerate(shifts):
        block = lax.rem(ka + shift, key_devices)
        q_all = q_ref[pl.ds(block * share, share)].astype(jnp.float32)
        do_all = do_ref[pl.ds(block * share, share)].astype(jnp.float32)
        visible = lead <= pb * (share * key_devices) + block * share
        outs = []
        for g in range(kv_heads):
            chosen = slice(g * group, (g + 1) * group)
            q = q_all[:, chosen].reshape(cols, width).astype(jnp.bfloat16)
            do = do_all[:, chosen].reshape(cols, width).astype(jnp.bfloat16)
            log_total = stats_ref[block, pl.ds(g, 1), :]
            dot = stats_ref[block, pl.ds(kv_heads + g, 1), :]
            scores = lax.dot_general(smooth[g], q, NT, preferred_element_type=jnp.float32)
            weights = jnp.where(visible, jnp.exp2(scores * (root * LOG2E) - log_total), 0.0)
            dp = lax.dot_general(vals[g], do, NT, preferred_element_type=jnp.float32)
            ds = (weights * (dp - dot)).astype(jnp.bfloat16)
            dv = jnp.dot(weights.astype(jnp.bfloat16), do, preferred_element_type=jnp.float32)
            dk = jnp.dot(ds, q, preferred_element_type=jnp.float32)
            dvs[g] = dv if dvs[g] is None else dvs[g] + dv
            dks[g] = dk if dks[g] is None else dks[g] + dk
            dq = jnp.dot(turned[g], ds, preferred_element_type=jnp.float32).T * root
            outs.append(dq.reshape(share, group, width))
        dq_ref[at] = jnp.concatenate(outs, axis=1).astype(dq_ref.dtype)
    for g in range(kv_heads):
        if first:
            acc_ref[g] = dks[g]
            acc_ref[kv_heads + g] = dvs[g]
        else:
            dk = (acc_in_ref[g] + dks[g]) * root
            dv = acc_in_ref[kv_heads + g] + dvs[g]
            for j, whole in ((g, dk), (kv_heads + g, dv)):
                keep_ref[j] = whole[:key_count]
                send_ref[j] = whole[key_count:].astype(jnp.bfloat16)


def finish_kernel(mine_ref, other_ref, dk_ref, dv_ref):
    kv_heads = mine_ref.shape[0] // 2
    total = mine_ref[...].astype(jnp.float32) + other_ref[...].astype(jnp.float32)
    for ref, base in ((dk_ref, 0), (dv_ref, kv_heads)):
        for g in range(kv_heads):
            ref[:, g, :] = total[base + g]


def cost(flops, size):
    return pl.CostEstimate(flops=int(flops), bytes_accessed=int(size), transcendentals=0)


def per_device(queries, key_codes, key_scale_powers, values, grad_out, grad_dot, log_totals):
    query_count, head_count, width = queries.shape
    key_count, kv_heads, _ = key_codes.shape
    group = head_count // kv_heads
    key_devices = lax.axis_size("ka")
    query_devices = lax.axis_size("pb")
    share = query_count // key_devices
    params = pltpu.CompilerParams(vmem_limit_bytes=40 * 2**20)

    def turn(x, by):
        return lax.ppermute(x, "ka", [((i + by) % key_devices, i) for i in range(key_devices)])

    def swap(x, by):
        return lax.ppermute(x, "ka", [(i, i ^ by) for i in range(key_devices)])

    packed, sums = pl.pallas_call(
        prep_kernel,
        out_shape=(
            jax.ShapeDtypeStruct((2 * kv_heads, key_count, width), jnp.bfloat16),
            jax.ShapeDtypeStruct((SUM_ROWS, width), jnp.float32),
        ),
        in_specs=[SMEM, VMEM, VMEM],
        out_specs=(VMEM, VMEM),
        compiler_params=params,
        name="prep",
    )(key_scale_powers, key_codes, values)
    got = swap(packed, 1)
    others = sum(swap(sums, by) for by in range(2, key_devices))

    def by_head(x):
        x = x.reshape(key_devices, share, kv_heads, group)
        return x.transpose(0, 2, 1, 3).reshape(key_devices, kv_heads, share * group)

    stats = jnp.concatenate([by_head(log_totals * LOG2E), by_head(grad_dot)], axis=1)

    even = list(range(2, key_devices, 2))
    acc_shape = jax.ShapeDtypeStruct((2 * kv_heads, 2 * key_count, width), jnp.float32)
    smooth_shape = jax.ShapeDtypeStruct((kv_heads, 2 * key_count, width), jnp.bfloat16)
    half = 10 * key_count * 2 * width * share * head_count

    sent, acc, smooth = pl.pallas_call(
        functools.partial(rows_kernel, even, share, kv_heads, key_devices, True),
        out_shape=(
            jax.ShapeDtypeStruct((len(even), share, head_count, width), jnp.bfloat16),
            acc_shape,
            smooth_shape,
        ),
        in_specs=[VMEM] * 6,
        out_specs=(VMEM,) * 3,
        compiler_params=params,
        cost_estimate=cost(half * len(even), 4 * 2**20),
        name="cross_rows",
    )(queries, grad_out, stats, packed, got, others)
    back = [turn(sent[at], key_devices - by) for at, by in enumerate(even)]

    own_dq, keep, send = pl.pallas_call(
        functools.partial(rows_kernel, [0], share, kv_heads, key_devices, False),
        out_shape=(
            jax.ShapeDtypeStruct((1, share, head_count, width), jnp.float32),
            jax.ShapeDtypeStruct((2 * kv_heads, key_count, width), jnp.float32),
            jax.ShapeDtypeStruct((2 * kv_heads, key_count, width), jnp.bfloat16),
        ),
        in_specs=[VMEM] * 7,
        out_specs=(VMEM,) * 3,
        compiler_params=params,
        cost_estimate=cost(half, 4 * 2**20),
        name="own_rows",
    )(queries, grad_out, stats, packed, got, smooth, acc)
    mine = (keep + swap(send, 1).astype(jnp.float32)).astype(jnp.bfloat16)
    if query_devices == 2:
        other = lax.ppermute(mine, "pb", [(0, 1), (1, 0)])
    else:
        other = lax.psum(mine.astype(jnp.float32), "pb") - mine.astype(jnp.float32)
    total = mine.astype(jnp.float32) + other.astype(jnp.float32)
    total = total.reshape(2, kv_heads, key_count, width).swapaxes(1, 2).astype(jnp.bfloat16)
    query_out = own_dq[0]
    for piece in back:
        query_out = query_out + piece.astype(jnp.float32)
    return query_out.astype(jnp.bfloat16), total[0], total[1]


def solution(mesh):
    in_specs = (
        P("pb", "ha", None),
        P("ka", "ha", None),
        P("ka", "ha"),
        P("ka", "ha", None),
        P("pb", "ha", None),
        P("pb", "ha"),
        P("pb", "ha"),
    )
    out_specs = (P(("pb", "ka"), "ha", None), P("ka", "ha", None), P("ka", "ha", None))
    return jax.shard_map(
        per_device, mesh=mesh, in_specs=in_specs, out_specs=out_specs, check_vma=False
    )
```

time: 103 us -> 47.2 us (0.46)
  blocking collectives: 28.5 us -> 0 us
  between operations: 14.3 us -> 0.73 us
  waiting for transfers between devices: 35.3 us -> 21.8 us
  starting transfers between devices: 0.04 us -> 11 us
  matrix products: 7.34 us -> 0 us
  local copies, waits for them, and re-layouts: 12.1 us -> 6.8 us
  Pallas kernels: 0 us -> 4.82 us
  other arithmetic: 5.18 us -> 1.69 us
    reduce_scatter x1 -> x0, waiting for transfers between devices: 35.3 us -> none  [per_device(): lax.psum_scatter(grad_query.reshape(outer, key_devices, share // outer, h...]
    psum x2 -> x0, blocking collectives: 28.5 us -> none  [the longest x1 15.1 us: per_device(): key_sum, value_sum = lax.psum((grad_keys, grad_values), 'pb')]
    ppermute x0 -> x6, waiting for transfers between devices: none -> 21.8 us  [the longest x1 12.3 us: turn(): lax.ppermute(x, 'ka', [((i + by) % key_devices, i) for i in range(key_dev...]
    ppermute x0 -> x6, starting transfers between devices: none -> 11 us  [the longest x4 6.47 us: swap(): return lax.ppermute(x, 'ka', [(i, i ^ by) for i in range(key_devices)])]
    dot_general x10 -> x0, matrix products: 7.34 us -> none  [the longest x2 2.45 us: head_grads(): jnp.einsum('gij,igd->jd', grad_scores, query_block, preferred_element_typ...]
    pallas_call x0 -> x3, Pallas kernels: none -> 4.82 us  [the longest x1 1.96 us: per_device(): pl.pallas_call(functools.partial(rows_kernel, [0], share, kv_heads, key_d...]
    unnamed x38 -> x9, local copies, waits for them, and re-layouts: 6.83 us -> 4.08 us
    slice x3 -> x0, local copies, waits for them, and re-layouts: 2.73 us -> none  [the longest x1 1.48 us: per_device(): query_in[query_range, chosen]]
  transfers between devices with their start and end apart: 1 -> 6, of which waited for: 1 -> 5; matrix products, arithmetic and copies ran while one was open for 5% -> 8% of each run, Pallas kernels for 0% -> 0%
where the time goes in v1:
time: 47.2 us; the launch traced here: 46.9 us
  waiting for transfers between devices  21.8 us (46%)
  starting transfers between devices  11 us (23%)
  local copies, waits for them, and re-layouts  6.8 us (14%)
  Pallas kernels  4.82 us (10%)
  other arithmetic  1.69 us (4%)
  between operations  0.73 us (2%)
    ppermute x1, waiting for transfers between devices, turn(): lax.ppermute(x, 'ka', [((i + by) % key_devices, i) for i in range(key_dev...  12.3 us
    ppermute x4, waiting for transfers between devices, swap(): return lax.ppermute(x, 'ka', [(i, i ^ by) for i in range(key_devices)])  8.31 us
    ppermute x4, starting transfers between devices, swap(): return lax.ppermute(x, 'ka', [(i, i ^ by) for i in range(key_devices)])  6.47 us
    unnamed x9, local copies, waits for them, and re-layouts  4.08 us
    ppermute x1, starting transfers between devices, turn(): lax.ppermute(x, 'ka', [((i + by) % key_devices, i) for i in range(key_dev...  2.96 us
    pallas_call x1, Pallas kernels, per_device(): pl.pallas_call(functools.partial(rows_kernel, [0], share, kv_heads, key_d...  1.96 us
    pallas_call x1, Pallas kernels, per_device(): pl.pallas_call(functools.partial(rows_kernel, even, share, kv_heads, key_...  1.9 us
    ppermute x1, starting transfers between devices, per_device(): other = lax.ppermute(mine, 'pb', [(0, 1), (1, 0)])  1.55 us
  transfers between devices with their start and end apart: 6, of which 5 were waited for; matrix products, arithmetic and copies ran while one was open for 8% of the time, Pallas kernels for 0%

profile of v1, /device:TPU:0, one launch (start us, length us, event | category | flops | bytes accessed | tf_op | source)
XLA Modules:
  0.0 46.9 jit_solution(16379502530672001544)
XLA Ops:
  0.6 0.9 %copy.16.powers_ref = s32[3,2]{1,0:T(4,128)S(1)} copy(s32[3,2]{0,1:T(2,128)} %param.9) | data formatting | bytes 48 | tf_op args[2]
  1.5 0.9 %copy-done.2 = bf16[192,2,128]{2,1,0:T(2,128)(2,1)S(1)} copy-done((bf16[192,2,128]{2,1,0:T(2,128)(2,1)S(1)}, bf16[192,2,128]{2,1,0:T(2,128)(2,1)}, u32[]{:S(2)}) %copy-start.2) | copy-done | bytes 98328
  2.4 0.9 %copy-done.3 = bf16[192,2,128]{2,1,0:T(2,128)(2,1)S(1)} copy-done((bf16[192,2,128]{2,1,0:T(2,128)(2,1)S(1)}, bf16[192,2,128]{2,1,0:T(2,128)(2,1)}, u32[]{:S(2)}) %copy-start.3) | copy-done | bytes 98328
  3.3 1.0 %prep.1 = (bf16[4,192,128]{2,1,0:T(8,128)(2,1)S(1)}, f32[8,128]{1,0:T(8,128)S(1)}) custom-call(s32[3,2]{1,0:T(4,128)S(1)} %copy.16.powers_ref, bf16[192,2,128]{2,1,0:T(2,128)(2,1)S(1)} %copy-done.2, bf16[192,2,128]{2,1,0:T(2,128)(2,1)S(1)} %copy-done.3), custom_call_target="tpu_custom_call" | custom-call | tf_op jit(solution)/shard_map/prep/pallas_call | solution.py:133
  4.3 5.1 %collective-permute-start.2 = (f32[8,128]{1,0:T(8,128)S(1)}, f32[8,128]{1,0:T(8,128)S(1)}, u32[]{:S(2)}, u32[]{:S(2)}) collective-permute-start(f32[8,128]{1,0:T(8,128)S(1)} %get-tuple-element.12), channel_id=1, source_target_pairs={{0,12},{4,8},{8,4},{12,0},{1,13},{5,9},{9,5},{13,1},{2,14},{6,10},... | collective-permute-start | bytes 12296 | tf_op jit(solution)/shard_map/ppermute | solution.py:131
  9.4 0.6 %collective-permute-start = (bf16[4,192,128]{2,1,0:T(8,128)(2,1)S(1)}, bf16[4,192,128]{2,1,0:T(8,128)(2,1)S(1)}, u32[]{:S(2)}, u32[]{:S(2)}) collective-permute-start(bf16[4,192,128]{2,1,0:T(8,128)(2,1)S(1)} %get-tuple-element.11.own_ref), channel_id=1, source_target_pairs={{0,4},{4,0},{8,12},{12,8},{1,5},{5,1},{9,13},{13,9},{2,6},{6,2},{1... | collective-permute-start | bytes 589832 | tf_op jit(solution)/shard_map/ppermute | solution.py:131
  10.0 0.7 %broadcast_multiply_fusion = f32[384,16]{0,1:T(8,128)S(1)} fusion(f32[384,16]{0,1:T(8,128)} %param.13), kind=kLoop, calls=%fused_computation.8 | loop fusion | flops 6144 | bytes 49152 | tf_op jit(solution)/shard_map/mul | solution.py:151
  10.9 0.8 %reshape.22 = f32[4,96,2,8]{1,0,3,2:T(4,128)S(1)} reshape(f32[384,16]{0,1:T(8,128)} %param.12) | data formatting | bytes 49152 | tf_op jit(solution)/shard_map/reshape | solution.py:148
  11.9 0.2 reshape.23
  12.3 0.2 reshape.21
  12.5 1.5 %collective-permute-done.1 = f32[8,128]{1,0:T(8,128)S(1)} collective-permute-done((f32[8,128]{1,0:T(8,128)S(1)}, f32[8,128]{1,0:T(8,128)S(1)}, u32[]{:S(2)}, u32[]{:S(2)}) %collective-permute-start.1) | collective-permute-done | bytes 4128 | tf_op jit(solution)/shard_map/ppermute | solution.py:131
  14.0 1.8 %collective-permute-done.got_ref = bf16[4,192,128]{2,1,0:T(8,128)(2,1)S(1)} collective-permute-done((bf16[4,192,128]{2,1,0:T(8,128)(2,1)S(1)}, bf16[4,192,128]{2,1,0:T(8,128)(2,1)S(1)}, u32[]{:S(2)}, u32[]{:S(2)}) %collective-permute-start) | collective-permute-done | bytes 196640 | tf_op jit(solution)/shard_map/ppermute | solution.py:131
  15.8 1.4 %copy-done.1 = bf16[384,16,128]{2,1,0:T(8,128)(2,1)S(1)} copy-done((bf16[384,16,128]{2,1,0:T(8,128)(2,1)S(1)}, bf16[384,16,128]{2,1,0:T(8,128)(2,1)}, u32[]{:S(2)}) %copy-start.1) | copy-done | bytes 1572888
  17.3 1.9 %cross_rows.1 = (bf16[1,96,16,128]{3,2,1,0:T(8,128)(2,1)S(1)}, f32[4,384,128]{2,1,0:T(8,128)S(1)}, bf16[2,384,128]{2,1,0:T(8,128)(2,1)S(1)}) custom-call(bf16[384,16,128]{2,1,0:T(8,128)(2,1)S(1)} %copy-done, bf16[384,16,128]{2,1,0:T(8,128)(2,1)S(1)} %copy-done.1, f32[4,4,768]{2,1,0:T(4,128)S(1)} %pad_maximum_fusion.stats_ref, ...), custom_call_target="tpu_custom_call" | custom-call | flops 754974720 | bytes 4194304 | tf_op jit(solution)/shard_map/cross_rows/pallas_call | solution.py:158
  19.2 2.0 %own_rows.1 = (f32[1,96,16,128]{3,2,1,0:T(8,128)S(1)}, f32[4,192,128]{2,1,0:T(8,128)S(1)}, bf16[4,192,128]{2,1,0:T(8,128)(2,1)S(1)}) custom-call(bf16[384,16,128]{2,1,0:T(8,128)(2,1)S(1)} %copy-done, bf16[384,16,128]{2,1,0:T(8,128)(2,1)S(1)} %copy-done.1, f32[4,4,768]{2,1,0:T(4,128)S(1)} %pad_maximum_fusion.stats_ref, ...), custom_call_target="tpu_custom_call" | custom-call | flops 754974720 | bytes 4194304 | tf_op jit(solution)/shard_map/own_rows/pallas_call | solution.py:173
  21.1 0.7 %collective-permute-start.4 = (bf16[4,192,128]{2,1,0:T(8,128)(2,1)S(1)}, bf16[4,192,128]{2,1,0:T(8,128)(2,1)S(1)}, u32[]{:S(2)}, u32[]{:S(2)}) collective-permute-start(bf16[4,192,128]{2,1,0:T(8,128)(2,1)S(1)} %get-tuple-element.18), channel_id=1, source_target_pairs={{0,4},{4,0},{8,12},{12,8},{1,5},{5,1},{9,13},{13,9},{2,6},{6,2},{1... | collective-permute-start | bytes 589832 | tf_op jit(solution)/shard_map/ppermute | solution.py:131
  21.9 5.0 %collective-permute-done.4 = bf16[4,192,128]{2,1,0:T(8,128)(2,1)S(1)} collective-permute-done((bf16[4,192,128]{2,1,0:T(8,128)(2,1)S(1)}, bf16[4,192,128]{2,1,0:T(8,128)(2,1)S(1)}, u32[]{:S(2)}, u32[]{:S(2)}) %collective-permute-start.4) | collective-permute-done | bytes 196640 | tf_op jit(solution)/shard_map/ppermute | solution.py:131
  26.9 1.6 %collective-permute-start.5 = (bf16[4,192,128]{2,1,0:T(8,128)(2,1)S(1)}, bf16[4,192,128]{2,1,0:T(8,128)(2,1)S(1)}, u32[]{:S(2)}, u32[]{:S(2)}) collective-permute-start(bf16[4,192,128]{2,1,0:T(8,128)(2,1)S(1)} %add_convert_fusion.1), channel_id=1, source_target_pairs={{0,16},{16,0},{1,17},{17,1},{2,18},{18,2},{3,19},{19,3},{4,20},{20... | collective-permute-start | bytes 589832 | tf_op jit(solution)/shard_map/ppermute | solution.py:188
  28.5 3.0 %collective-permute-start.3 = (bf16[96,16,128]{2,1,0:T(8,128)(2,1)S(1)}, bf16[96,16,128]{2,1,0:T(8,128)(2,1)S(1)}, u32[]{:S(2)}, u32[]{:S(2)}) collective-permute-start(bf16[96,16,128]{2,1,0:T(8,128)(2,1)S(1)} %bitcast.23), channel_id=1, source_target_pairs={{8,0},{12,4},{0,8},{4,12},{9,1},{13,5},{1,9},{5,13},{10,2},{14,6},... | collective-permute-start | bytes 1179656 | tf_op jit(solution)/shard_map/ppermute | solution.py:128
  31.4 1.2 %collective-permute-done.5 = bf16[4,192,128]{2,1,0:T(8,128)(2,1)S(1)} collective-permute-done((bf16[4,192,128]{2,1,0:T(8,128)(2,1)S(1)}, bf16[4,192,128]{2,1,0:T(8,128)(2,1)S(1)}, u32[]{:S(2)}, u32[]{:S(2)}) %collective-permute-start.5) | collective-permute-done | bytes 196640 | tf_op jit(solution)/shard_map/ppermute | solution.py:188
  32.7 0.2 copy.19
  32.9 0.8 %slice_bitcast_fusion = (bf16[192,2,128]{2,1,0:T(2,128)(2,1)}, bf16[192,2,128]{2,1,0:T(2,128)(2,1)}) fusion(bf16[2,192,2,128]{3,2,1,0:T(2,128)(2,1)S(1)} %bitcast.26), kind=kLoop, calls=%fused_computation.5 | loop fusion | bytes 393216 | tf_op jit(solution)/shard_map/squeeze | solution.py:196
  33.7 12.3 %collective-permute-done.3 = bf16[96,16,128]{2,1,0:T(8,128)(2,1)S(1)} collective-permute-done((bf16[96,16,128]{2,1,0:T(8,128)(2,1)S(1)}, bf16[96,16,128]{2,1,0:T(8,128)(2,1)S(1)}, u32[]{:S(2)}, u32[]{:S(2)}) %collective-permute-start.3) | collective-permute-done | bytes 393248 | tf_op jit(solution)/shard_map/ppermute | solution.py:128
  46.0 0.8 %fusion = bf16[96,16,128]{2,1,0:T(8,128)(2,1)} fusion(f32[1,96,16,128]{3,2,1,0:T(8,128)S(1)} %get-tuple-element.15, bf16[96,16,128]{2,1,0:T(8,128)(2,1)S(1)} %collective-permute-done.3), kind=kLoop, calls=%fused_computation.1 | loop fusion | flops 589824 | bytes 1572864 | tf_op jit(solution)/shard_map/convert_element_type | solution.py:196
  (14 shorter events, 0.6 us)
Async XLA Ops:
  0.6 15.2 %copy-start = (bf16[384,16,128]{2,1,0:T(8,128)(2,1)S(1)}, bf16[384,16,128]{2,1,0:T(8,128)(2,1)}, u32[]{:S(2)}) copy-start(bf16[384,16,128]{2,1,0:T(8,128)(2,1)} %q_ref.3) | copy-start | bytes 4718596
  1.5 0.9 %copy-start.2 = (bf16[192,2,128]{2,1,0:T(2,128)(2,1)S(1)}, bf16[192,2,128]{2,1,0:T(2,128)(2,1)}, u32[]{:S(2)}) copy-start(bf16[192,2,128]{2,1,0:T(2,128)(2,1)} %codes_ref.1) | copy-start | bytes 294916
  2.4 0.9 %copy-start.3 = (bf16[192,2,128]{2,1,0:T(2,128)(2,1)S(1)}, bf16[192,2,128]{2,1,0:T(2,128)(2,1)}, u32[]{:S(2)}) copy-start(bf16[192,2,128]{2,1,0:T(2,128)(2,1)} %values_ref.1) | copy-start | bytes 294916
  4.3 8.3 %collective-permute-start.2 = (f32[8,128]{1,0:T(8,128)S(1)}, f32[8,128]{1,0:T(8,128)S(1)}, u32[]{:S(2)}, u32[]{:S(2)}) collective-permute-start(f32[8,128]{1,0:T(8,128)S(1)} %get-tuple-element.12), channel_id=1, source_target_pairs={{0,12},{4,8},{8,4},{12,0},{1,13},{5,9},{9,5},{13,1},{2,14},{6,10},... | collective-permute-start | bytes 12296 | tf_op jit(solution)/shard_map/ppermute | solution.py:131
  9.4 4.6 %collective-permute-start.1 = (f32[8,128]{1,0:T(8,128)S(1)}, f32[8,128]{1,0:T(8,128)S(1)}, u32[]{:S(2)}, u32[]{:S(2)}) collective-permute-start(f32[8,128]{1,0:T(8,128)S(1)} %get-tuple-element.12), channel_id=1, source_target_pairs={{0,8},{4,12},{8,0},{12,4},{1,9},{5,13},{9,1},{13,5},{2,10},{6,14},... | collective-permute-start | bytes 12296 | tf_op jit(solution)/shard_map/ppermute | solution.py:131
  9.4 6.4 %collective-permute-start = (bf16[4,192,128]{2,1,0:T(8,128)(2,1)S(1)}, bf16[4,192,128]{2,1,0:T(8,128)(2,1)S(1)}, u32[]{:S(2)}, u32[]{:S(2)}) collective-permute-start(bf16[4,192,128]{2,1,0:T(8,128)(2,1)S(1)} %get-tuple-element.11.own_ref), channel_id=1, source_target_pairs={{0,4},{4,0},{8,12},{12,8},{1,5},{5,1},{9,13},{13,9},{2,6},{6,2},{1... | collective-permute-start | bytes 589832 | tf_op jit(solution)/shard_map/ppermute | solution.py:131
  15.8 1.4 %copy-start.1 = (bf16[384,16,128]{2,1,0:T(8,128)(2,1)S(1)}, bf16[384,16,128]{2,1,0:T(8,128)(2,1)}, u32[]{:S(2)}) copy-start(bf16[384,16,128]{2,1,0:T(8,128)(2,1)} %do_ref.3) | copy-start | bytes 4718596
  21.1 5.7 %collective-permute-start.4 = (bf16[4,192,128]{2,1,0:T(8,128)(2,1)S(1)}, bf16[4,192,128]{2,1,0:T(8,128)(2,1)S(1)}, u32[]{:S(2)}, u32[]{:S(2)}) collective-permute-start(bf16[4,192,128]{2,1,0:T(8,128)(2,1)S(1)} %get-tuple-element.18), channel_id=1, source_target_pairs={{0,4},{4,0},{8,12},{12,8},{1,5},{5,1},{9,13},{13,9},{2,6},{6,2},{1... | collective-permute-start | bytes 589832 | tf_op jit(solution)/shard_map/ppermute | solution.py:131
  26.9 5.7 %collective-permute-start.5 = (bf16[4,192,128]{2,1,0:T(8,128)(2,1)S(1)}, bf16[4,192,128]{2,1,0:T(8,128)(2,1)S(1)}, u32[]{:S(2)}, u32[]{:S(2)}) collective-permute-start(bf16[4,192,128]{2,1,0:T(8,128)(2,1)S(1)} %add_convert_fusion.1), channel_id=1, source_target_pairs={{0,16},{16,0},{1,17},{17,1},{2,18},{18,2},{3,19},{19,3},{4,20},{20... | collective-permute-start | bytes 589832 | tf_op jit(solution)/shard_map/ppermute | solution.py:188
  28.5 17.6 %collective-permute-start.3 = (bf16[96,16,128]{2,1,0:T(8,128)(2,1)S(1)}, bf16[96,16,128]{2,1,0:T(8,128)(2,1)S(1)}, u32[]{:S(2)}, u32[]{:S(2)}) collective-permute-start(bf16[96,16,128]{2,1,0:T(8,128)(2,1)S(1)} %bitcast.23), channel_id=1, source_target_pairs={{8,0},{12,4},{0,8},{4,12},{9,1},{13,5},{1,9},{5,13},{10,2},{14,6},... | collective-permute-start | bytes 1179656 | tf_op jit(solution)/shard_map/ppermute | solution.py:128

commit v2 on v0

v2 whole, which is shorter than its diff:
```python
import functools
import math

import jax
import jax.numpy as jnp
from jax import lax
from jax.experimental import pallas as pl
from jax.experimental.pallas import tpu as pltpu
from jax.sharding import PartitionSpec as P

KEYS_PER_SCALE = 64
LOG2E = math.log2(math.e)
VMEM = pl.BlockSpec(memory_space=pltpu.VMEM)
SMEM = pl.BlockSpec(memory_space=pltpu.SMEM)
HBM = pl.BlockSpec(memory_space=pltpu.HBM)
NT = (((1,), (1,)), ((), ()))
SUM_ROWS = 16


def prep_kernel(powers_ref, codes_hbm, values_hbm, *refs):
    *message_refs, sums_ref, codes_ref, values_ref, sems = refs
    key_count, kv_heads, width = codes_ref.shape
    load_codes = pltpu.make_async_copy(codes_hbm, codes_ref, sems.at[0])
    load_values = pltpu.make_async_copy(values_hbm, values_ref, sems.at[1])
    load_codes.start()
    load_values.start()
    rows = lax.broadcasted_iota(jnp.int32, (key_count, width), 0) // KEYS_PER_SCALE
    factors = []
    for g in range(kv_heads):
        factor = jnp.zeros((key_count, width), jnp.float32)
        for b in range(key_count // KEYS_PER_SCALE):
            power = jnp.left_shift(1, powers_ref[g, b] + 8).astype(jnp.float32) * 2.0**-8
            factor = jnp.where(rows == b, power, factor)
        factors.append(factor)
    load_codes.wait()
    load_values.wait()
    codes = codes_ref[...].astype(jnp.float32)
    values = values_ref[...].astype(jnp.float32)
    sums = []
    for g in range(kv_heads):
        wide = codes[:, g, :] * factors[g]
        message_refs[g][0:key_count] = wide.astype(jnp.bfloat16)
        message_refs[g][key_count : 2 * key_count] = values[:, g, :].astype(jnp.bfloat16)
        sums.append(jnp.sum(wide, axis=0, keepdims=True))
    line = lax.broadcasted_iota(jnp.int32, (SUM_ROWS, width), 0)
    parts = jnp.zeros((SUM_ROWS, width), jnp.float32)
    whole = jnp.zeros((SUM_ROWS, width), jnp.float32)
    for g in range(kv_heads):
        rest = sums[g]
        whole = jnp.where(line == g, rest, whole)
        for j in range(3):
            piece = rest.astype(jnp.bfloat16).astype(jnp.float32)
            parts = jnp.where(line == 3 * g + j, piece, parts)
            rest = rest - piece
    sums_ref[...] = whole
    for ref in message_refs:
        ref[2 * key_count : 2 * key_count + SUM_ROWS] = parts.astype(jnp.bfloat16)


def gather_kernel(row_sets, share, q_hbm, do_hbm, q_out, do_out, q_ref, do_ref, sems):
    ka = lax.axis_index("ka")
    kv_heads = len(row_sets)
    group = q_ref.shape[2] // kv_heads
    cols, width = share * group, q_ref.shape[3]
    needed = sorted({m for sets in row_sets for m in sets})
    loads = []
    for at, m in enumerate(needed):
        for j, (src, dst) in enumerate(((q_hbm, q_ref), (do_hbm, do_ref))):
            load = pltpu.make_async_copy(
                src.at[pl.ds((ka ^ m) * share, share)], dst.at[at], sems.at[2 * at + j]
            )
            load.start()
            loads.append(load)
    for at, m in enumerate(needed):
        for j, (src, dst) in enumerate(((q_ref, q_out), (do_ref, do_out))):
            loads[2 * at + j].wait()
            wide = src[at].astype(jnp.float32)
            for g in range(kv_heads):
                if m in row_sets[g]:
                    rows = wide[:, g * group : (g + 1) * group].reshape(cols, width)
                    dst[g, row_sets[g].index(m)] = rows.astype(jnp.bfloat16)


def rows_kernel(key_devices, share, partners, row_sets, *refs):
    kv_heads = len(partners)
    q_ref, do_ref, stats_ref = refs[:3]
    own_refs, got_refs = refs[3 : 3 + kv_heads], refs[3 + kv_heads : 3 + 2 * kv_heads]
    dq_ref, cross_ref, keep_ref = refs[-3:]
    send_refs = refs[-3 - kv_heads : -3]
    sum_refs = refs[3 + 2 * kv_heads : -3 - kv_heads]
    ka, pb = lax.axis_index("ka"), lax.axis_index("pb")
    cols, width = q_ref.shape[2:]
    key_count = (own_refs[0].shape[0] - SUM_ROWS) // 2
    group = cols // share
    root = width**-0.5
    line = lax.broadcasted_iota(jnp.int32, (2 * key_count, cols), 0)
    step = lax.broadcasted_iota(jnp.int32, (2 * key_count, cols), 1) // group
    parts = own_refs[0][2 * key_count :].astype(jnp.float32)
    for partner in dict(zip(partners, range(kv_heads))).values():
        parts = parts + got_refs[partner][2 * key_count :].astype(jnp.float32)
    whole = jnp.zeros((SUM_ROWS, width), jnp.float32)
    for ref in sum_refs:
        whole = whole + ref[...]
    for g in range(kv_heads):
        own, got = own_refs[g], got_refs[g]
        total = jnp.sum(parts[3 * g : 3 * g + 3], axis=0, keepdims=True) + whole[g : g + 1]
        mean = total / (key_count * key_devices)
        k = jnp.concatenate([own[0:key_count], got[0:key_count]], axis=0).astype(jnp.float32)
        k = k - mean
        turned = k.T.astype(jnp.bfloat16)
        k = k.astype(jnp.bfloat16)
        v = jnp.concatenate(
            [own[key_count : 2 * key_count], got[key_count : 2 * key_count]], axis=0
        )
        base = jnp.where(line < key_count, ka * key_count, ((ka ^ partners[g]) - 1) * key_count)
        lead = line + base - step
        dk = dv = None
        for at, m in enumerate(row_sets[g]):
            block = ka ^ m
            q, do = q_ref[g, at], do_ref[g, at]
            log_total = stats_ref[block, pl.ds(g, 1), :]
            dot = stats_ref[block, pl.ds(kv_heads + g, 1), :]
            visible = lead <= pb * (share * key_devices) + block * share
            scores = lax.dot_general(k, q, NT, preferred_element_type=jnp.float32)
            weights = jnp.where(visible, jnp.exp2(scores * (root * LOG2E) - log_total), 0.0)
            dp = lax.dot_general(v, do, NT, preferred_element_type=jnp.float32)
            ds = (weights * (dp - dot)).astype(jnp.bfloat16)
            dv_now = jnp.dot(weights.astype(jnp.bfloat16), do, preferred_element_type=jnp.float32)
            dk_now = jnp.dot(ds, q, preferred_element_type=jnp.float32)
            dv = dv_now if dv is None else dv + dv_now
            dk = dk_now if dk is None else dk + dk_now
            dq = jnp.dot(turned, ds, preferred_element_type=jnp.float32).T * root
            if m == 0:
                dq_ref[g] = dq
            else:
                others = [other for other in row_sets[g] if other]
                send_refs[g][others.index(m)] = dq.astype(jnp.bfloat16)
        for j, grad in ((2 * g, dk * root), (2 * g + 1, dv)):
            keep_ref[j] = grad[:key_count].astype(jnp.bfloat16)
            cross_ref[j] = grad[key_count:].astype(jnp.bfloat16)


def across_kernel(*refs):
    *in_refs, out_a, out_b = refs
    total = in_refs[0][...].astype(jnp.float32)
    for ref in in_refs[1:]:
        total = total + ref[...].astype(jnp.float32)
    half = out_a.shape[0]
    out_a[...] = total[:half].astype(jnp.bfloat16)
    out_b[...] = total[half:].astype(jnp.bfloat16)


def finish_kernel(kv_heads, keep_count, own_dq_ref, *refs):
    *refs, dq_ref, dk_ref, dv_ref = refs
    keep_refs, refs = refs[:keep_count], refs[keep_count:]
    z_refs, back_refs = refs[:2], refs[2:]
    share, heads, width = dq_ref.shape
    group = heads // kv_heads
    outs = []
    for g in range(kv_heads):
        dq = own_dq_ref[g]
        for ref in back_refs[g :: kv_heads]:
            dq = dq + ref[...].astype(jnp.float32)
        outs.append(dq.reshape(share, group, width))
    dq_ref[...] = jnp.concatenate(outs, axis=1).astype(jnp.bfloat16)
    total = keep_refs[0][...].astype(jnp.float32)
    for ref in keep_refs[1:]:
        total = total + ref[...].astype(jnp.float32)
    total = total + jnp.concatenate([ref[...] for ref in z_refs], axis=0).astype(jnp.float32)
    for j, ref in enumerate((dk_ref, dv_ref)):
        grads = jnp.stack([total[2 * g + j] for g in range(kv_heads)], axis=1)
        ref[...] = grads.astype(jnp.bfloat16)


def per_device(queries, key_codes, key_scale_powers, values, grad_out, grad_dot, log_totals):
    query_count, head_count, width = queries.shape
    key_count, kv_heads, _ = key_codes.shape
    group = head_count // kv_heads
    key_devices = lax.axis_size("ka")
    query_devices = lax.axis_size("pb")
    share = query_count // key_devices
    cols = share * group
    params = pltpu.CompilerParams(vmem_limit_bytes=24 * 2**20)
    top = key_devices // 2
    partners = [1 if g < kv_heads // 2 else top for g in range(kv_heads)]
    row_sets = [[m for m in range(key_devices) if not m & p] for p in partners]
    shape = jax.ShapeDtypeStruct

    def swap(x, by):
        return lax.ppermute(x, "ka", [(i, i ^ by) for i in range(key_devices)])

    def pinned(x):
        return pltpu.with_memory_space_constraint(x, pltpu.HBM)

    *messages, sums = pl.pallas_call(
        prep_kernel,
        out_shape=(shape((2 * key_count + SUM_ROWS, width), jnp.bfloat16),) * kv_heads
        + (shape((SUM_ROWS, width), jnp.float32),),
        in_specs=[SMEM, HBM, HBM],
        out_specs=(VMEM,) * (kv_heads + 1),
        scratch_shapes=[
            pltpu.VMEM(key_codes.shape, key_codes.dtype),
            pltpu.VMEM(values.shape, values.dtype),
            pltpu.SemaphoreType.DMA((2,)),
        ],
        compiler_params=params,
        name="prep",
    )(key_scale_powers.T, pinned(key_codes), pinned(values))
    got = [swap(message, by) for message, by in zip(messages, partners)]
    others = [swap(sums, by) for by in range(1, key_devices) if by not in partners]

    needed = sorted({m for sets in row_sets for m in sets})
    laid = shape((kv_heads, key_devices // 2, cols, width), jnp.bfloat16)
    rows_q, rows_do = pl.pallas_call(
        functools.partial(gather_kernel, row_sets, share),
        out_shape=(laid, laid),
        in_specs=[HBM, HBM],
        out_specs=(VMEM, VMEM),
        scratch_shapes=[
            pltpu.VMEM((len(needed), share, head_count, width), queries.dtype),
            pltpu.VMEM((len(needed), share, head_count, width), grad_out.dtype),
            pltpu.SemaphoreType.DMA((2 * len(needed),)),
        ],
        compiler_params=params,
        name="gather",
    )(pinned(queries), pinned(grad_out))

    stats = jnp.concatenate([log_totals.T * LOG2E, grad_dot.T], axis=0)
    stats = stats.reshape(2 * kv_heads, group, key_devices, share)
    stats = stats.transpose(2, 0, 3, 1).reshape(key_devices, 2 * kv_heads, cols)

    part = shape((2 * kv_heads, key_count, width), jnp.bfloat16)
    sent = shape((key_devices // 2 - 1, cols, width), jnp.bfloat16)
    *sends, own_dq, cross, keep = pl.pallas_call(
        functools.partial(rows_kernel, key_devices, share, partners, row_sets),
        out_shape=(sent,) * kv_heads + (shape((kv_heads, cols, width), jnp.float32), part, part),
        in_specs=[VMEM] * (3 + 2 * kv_heads + len(others)),
        out_specs=(VMEM,) * (kv_heads + 3),
        compiler_params=params,
        name="rows",
    )(rows_q, rows_do, stats, *messages, *got, *others)

    def over_queries(x):
        if query_devices == 2:
            return [x, lax.ppermute(x, "pb", [(0, 1), (1, 0)])]
        return [lax.psum(x.astype(jnp.float32), "pb")]

    crossed = over_queries(cross)
    back = []
    for at in range(key_devices // 2 - 1):
        for g in range(kv_heads):
            back.append(swap(sends[g][at], [m for m in row_sets[g] if m][at]))
    kept = over_queries(keep)
    half = shape((kv_heads, key_count, width), jnp.bfloat16)
    z_a, z_b = pl.pallas_call(
        across_kernel,
        out_shape=(half, half),
        in_specs=[VMEM] * len(crossed),
        out_specs=(VMEM, VMEM),
        compiler_params=params,
        cost_estimate=pl.CostEstimate(
            flops=10**10, bytes_accessed=2**20, transcendentals=0
        ),
        name="across",
    )(*crossed)
    z = [swap(z_a, partners[0]), swap(z_b, partners[-1])]
    return pl.pallas_call(
        functools.partial(finish_kernel, kv_heads, len(kept)),
        out_shape=(
            shape((share, head_count, width), jnp.bfloat16),
            shape(key_codes.shape, jnp.bfloat16),
            shape(values.shape, jnp.bfloat16),
        ),
        in_specs=[VMEM] * (1 + len(kept) + len(z) + len(back)),
        out_specs=(VMEM,) * 3,
        compiler_params=params,
        name="finish",
    )(own_dq, *kept, *z, *back)


def solution(mesh):
    in_specs = (
        P("pb", "ha", None),
        P("ka", "ha", None),
        P("ka", "ha"),
        P("ka", "ha", None),
        P("pb", "ha", None),
        P("pb", "ha"),
        P("pb", "ha"),
    )
    out_specs = (P(("pb", "ka"), "ha", None), P("ka", "ha", None), P("ka", "ha", None))
    return jax.shard_map(
        per_device, mesh=mesh, in_specs=in_specs, out_specs=out_specs, check_vma=False
    )
```

time: 103 us -> 35.2 us (0.34)
  blocking collectives: 28.5 us -> 0 us
  waiting for transfers between devices: 35.3 us -> 11.3 us
  between operations: 14.3 us -> 0.71 us
  starting transfers between devices: 0.04 us -> 11.7 us
  local copies, waits for them, and re-layouts: 12.1 us -> 1.46 us
  Pallas kernels: 0 us -> 8.24 us
  matrix products: 7.34 us -> 0 us
  other arithmetic: 5.18 us -> 1.48 us
    reduce_scatter x1 -> x0, waiting for transfers between devices: 35.3 us -> none  [per_device(): lax.psum_scatter(grad_query.reshape(outer, key_devices, share // outer, h...]
    psum x2 -> x0, blocking collectives: 28.5 us -> none  [the longest x1 15.1 us: per_device(): key_sum, value_sum = lax.psum((grad_keys, grad_values), 'pb')]
    ppermute x0 -> x9, starting transfers between devices: none -> 11.7 us  [the longest x7 9.6 us: swap(): return lax.ppermute(x, 'ka', [(i, i ^ by) for i in range(key_devices)])]
    ppermute x0 -> x9, waiting for transfers between devices: none -> 11.3 us  [the longest x7 7.74 us: swap(): return lax.ppermute(x, 'ka', [(i, i ^ by) for i in range(key_devices)])]
    pallas_call x0 -> x5, Pallas kernels: none -> 8.24 us  [the longest x1 3.55 us: per_device(): pl.pallas_call(functools.partial(rows_kernel, key_devices, share, partner...]
    dot_general x10 -> x0, matrix products: 7.34 us -> none  [the longest x2 2.45 us: head_grads(): jnp.einsum('gij,igd->jd', grad_scores, query_block, preferred_element_typ...]
    unnamed x38 -> x2, local copies, waits for them, and re-layouts: 6.83 us -> 0.67 us
    convert_element_type x2 -> x0, other arithmetic: 2.94 us -> none  [the longest x1 1.93 us: per_device(): summed.reshape(share, head_count, head_width).astype(jnp.bfloat16)]
  transfers between devices with their start and end apart: 1 -> 9, of which waited for: 1 -> 5; matrix products, arithmetic and copies ran while one was open for 5% -> 7% of each run, Pallas kernels for 0% -> 5%
where the time goes in v2:
time: 35.2 us; the launch traced here: 34.9 us
  starting transfers between devices  11.7 us (33%)
  waiting for transfers between devices  11.3 us (32%)
  Pallas kernels  8.24 us (23%)
  other arithmetic  1.48 us (4%)
  local copies, waits for them, and re-layouts  1.46 us (4%)
  between operations  0.71 us (2%)
    ppermute x7, starting transfers between devices, swap(): return lax.ppermute(x, 'ka', [(i, i ^ by) for i in range(key_devices)])  9.6 us
    ppermute x7, waiting for transfers between devices, swap(): return lax.ppermute(x, 'ka', [(i, i ^ by) for i in range(key_devices)])  7.74 us
    ppermute x2, waiting for transfers between devices, over_queries(): return [x, lax.ppermute(x, 'pb', [(0, 1), (1, 0)])]  3.59 us
    pallas_call x1, Pallas kernels, per_device(): pl.pallas_call(functools.partial(rows_kernel, key_devices, share, partner...  3.55 us
    ppermute x2, starting transfers between devices, over_queries(): return [x, lax.ppermute(x, 'pb', [(0, 1), (1, 0)])]  2.09 us
    pallas_call x1, Pallas kernels, per_device(): pl.pallas_call(prep_kernel, out_shape=(shape((2 * key_count + SUM_ROWS, w...  1.87 us
    pallas_call x1, Pallas kernels, per_device(): pl.pallas_call(functools.partial(gather_kernel, row_sets, share), out_sha...  1.68 us
    pallas_call x1, Pallas kernels, per_device(): pl.pallas_call(functools.partial(finish_kernel, kv_heads, len(kept)), out...  1.09 us
  transfers between devices with their start and end apart: 9, of which 5 were waited for; matrix products, arithmetic and copies ran while one was open for 7% of the time, Pallas kernels for 5%

profile of v2, /device:TPU:0, one launch (start us, length us, event | category | flops | bytes accessed | tf_op | source)
XLA Modules:
  0.0 34.9 jit_solution(16249319940656665034)
XLA Ops:
  0.6 0.7 %copy-done = s32[3,2]{0,1:T(2,128)S(1)} copy-done((s32[3,2]{0,1:T(2,128)S(1)}, s32[3,2]{0,1:T(2,128)}, u32[]{:S(2)}) %copy-start) | copy-done | bytes 48
  1.3 1.9 %prep.1 = (bf16[400,128]{1,0:T(8,128)(2,1)S(1)}, bf16[400,128]{1,0:T(8,128)(2,1)S(1)}, f32[16,128]{1,0:T(8,128)S(1)}) custom-call(s32[2,3]{1,0:T(2,128)S(1)} %bitcast.9, bf16[192,2,128]{2,1,0:T(2,128)(2,1)} %codes_hbm.1, bf16[192,2,128]{2,1,0:T(2,128)(2,1)} %values_hbm.1), custom_call_target="tpu_custom_call" | custom-call | tf_op jit(solution)/shard_map/prep/pallas_call | solution.py:195
  3.2 5.1 %collective-permute-start.2 = (f32[16,128]{1,0:T(8,128)S(1)}, f32[16,128]{1,0:T(8,128)S(1)}, u32[]{:S(2)}, u32[]{:S(2)}) collective-permute-start(f32[16,128]{1,0:T(8,128)S(1)} %get-tuple-element.19), channel_id=1, source_target_pairs={{0,12},{4,8},{8,4},{12,0},{1,13},{5,9},{9,5},{13,1},{2,14},{6,10},... | collective-permute-start | bytes 24584 | tf_op jit(solution)/shard_map/ppermute | solution.py:190
  8.3 0.6 %collective-permute-start.1 = (bf16[400,128]{1,0:T(8,128)(2,1)S(1)}, bf16[400,128]{1,0:T(8,128)(2,1)S(1)}, u32[]{:S(2)}, u32[]{:S(2)}) collective-permute-start(bf16[400,128]{1,0:T(8,128)(2,1)S(1)} %get-tuple-element.18.refs_4_), channel_id=1, source_target_pairs={{0,8},{4,12},{8,0},{12,4},{1,9},{5,13},{9,1},{13,5},{2,10},{6,14},... | collective-permute-start | bytes 307208 | tf_op jit(solution)/shard_map/ppermute | solution.py:190
  8.9 0.7 %multiply_bitcast_fusion = f32[16,384]{1,0:T(8,128)S(1)} fusion(f32[384,16]{0,1:T(8,128)} %param.13), kind=kLoop, calls=%fused_computation.1 | loop fusion | flops 6144 | bytes 49152 | tf_op jit(solution)/shard_map/mul | solution.py:228
  9.7 0.7 %pad_maximum_fusion = f32[32,384]{1,0:T(8,128)S(1)} fusion(f32[16,384]{1,0:T(8,128)} %bitcast.13, f32[16,384]{1,0:T(8,128)S(1)} %multiply_bitcast_fusion), kind=kLoop, calls=%fused_computation | loop fusion | flops 12288 | bytes 98304 | tf_op jit(solution)/shard_map/concatenate | solution.py:228
  10.4 0.1 reshape.12
  10.5 0.3 copy.11
  10.8 0.4 %reshape.13.refs_2_ = f32[4,4,768]{2,1,0:T(4,128)S(1)} reshape(f32[4,4,96,8]{3,2,1,0:T(8,128)S(1)} %bitcast.12) | data formatting | bytes 98304 | tf_op jit(solution)/shard_map/reshape | solution.py:230
  11.2 1.7 %gather.1 = (bf16[2,2,768,128]{3,2,1,0:T(8,128)(2,1)S(1)}, bf16[2,2,768,128]{3,2,1,0:T(8,128)(2,1)S(1)}) custom-call(bf16[384,16,128]{2,1,0:T(8,128)(2,1)} %q_hbm.1, bf16[384,16,128]{2,1,0:T(8,128)(2,1)} %do_hbm.1), custom_call_target="tpu_custom_call" | custom-call | tf_op jit(solution)/shard_map/gather/pallas_call | solution.py:214
  12.9 1.5 %collective-permute-done.refs_5_ = bf16[400,128]{1,0:T(8,128)(2,1)S(1)} collective-permute-done((bf16[400,128]{1,0:T(8,128)(2,1)S(1)}, bf16[400,128]{1,0:T(8,128)(2,1)S(1)}, u32[]{:S(2)}, u32[]{:S(2)}) %collective-permute-start) | collective-permute-done | bytes 102432 | tf_op jit(solution)/shard_map/ppermute | solution.py:190
  14.4 1.4 %collective-permute-done.1.refs_6_ = bf16[400,128]{1,0:T(8,128)(2,1)S(1)} collective-permute-done((bf16[400,128]{1,0:T(8,128)(2,1)S(1)}, bf16[400,128]{1,0:T(8,128)(2,1)S(1)}, u32[]{:S(2)}, u32[]{:S(2)}) %collective-permute-start.1) | collective-permute-done | bytes 102432 | tf_op jit(solution)/shard_map/ppermute | solution.py:190
  15.8 3.5 %rows.1 = (bf16[1,768,128]{2,1,0:T(8,128)(2,1)S(1)}, bf16[1,768,128]{2,1,0:T(8,128)(2,1)S(1)}, f32[2,768,128]{2,1,0:T(8,128)S(1)}, bf16[4,192,128]{2,1,0:T(8,128)(2,1)S(1)}, bf16[4,192,128]{2,1,0:T(8,128)(2,1)S(1)}) custom-call(bf16[2,2,768,128]{3,2,1,0:T(8,128)(2,1)S(1)} %get-tuple-element.15.refs_0_, ...), custom_call_target="tpu_custom_call" | custom-call | tf_op jit(solution)/shard_map/rows/pallas_call | solution.py:234
  19.4 1.6 %collective-permute-start.4 = (bf16[4,192,128]{2,1,0:T(8,128)(2,1)S(1)}, bf16[4,192,128]{2,1,0:T(8,128)(2,1)S(1)}, u32[]{:S(2)}, u32[]{:S(2)}) collective-permute-start(bf16[4,192,128]{2,1,0:T(8,128)(2,1)S(1)} %get-tuple-element.22.refs_0_), channel_id=1, source_target_pairs={{0,16},{16,0},{1,17},{17,1},{2,18},{18,2},{3,19},{19,3},{4,20},{20... | collective-permute-start | bytes 589832 | tf_op jit(solution)/shard_map/ppermute | solution.py:245
  20.9 0.4 %collective-permute-start.7 = (bf16[768,128]{1,0:T(8,128)(2,1)S(1)}, bf16[768,128]{1,0:T(8,128)(2,1)S(1)}, u32[]{:S(2)}, u32[]{:S(2)}) collective-permute-start(bf16[768,128]{1,0:T(8,128)(2,1)S(1)} %bitcast.11), channel_id=1, source_target_pairs={{0,8},{4,12},{8,0},{12,4},{1,9},{5,13},{9,1},{13,5},{2,10},{6,14},... | collective-permute-start | bytes 589832 | tf_op jit(solution)/shard_map/ppermute | solution.py:190
  21.3 1.7 %collective-permute-start.8 = (bf16[768,128]{1,0:T(8,128)(2,1)S(1)}, bf16[768,128]{1,0:T(8,128)(2,1)S(1)}, u32[]{:S(2)}, u32[]{:S(2)}) collective-permute-start(bf16[768,128]{1,0:T(8,128)(2,1)S(1)} %bitcast.10), channel_id=1, source_target_pairs={{0,4},{4,0},{8,12},{12,8},{1,5},{5,1},{9,13},{13,9},{2,6},{6,2},{1... | collective-permute-start | bytes 589832 | tf_op jit(solution)/shard_map/ppermute | solution.py:190
  23.0 0.5 %collective-permute-start.3 = (bf16[4,192,128]{2,1,0:T(8,128)(2,1)S(1)}, bf16[4,192,128]{2,1,0:T(8,128)(2,1)S(1)}, u32[]{:S(2)}, u32[]{:S(2)}) collective-permute-start(bf16[4,192,128]{2,1,0:T(8,128)(2,1)S(1)} %get-tuple-element.21.refs_0_), channel_id=1, source_target_pairs={{0,16},{16,0},{1,17},{17,1},{2,18},{18,2},{3,19},{19,3},{4,20},{20... | collective-permute-start | bytes 589832 | tf_op jit(solution)/shard_map/ppermute | solution.py:245
  23.5 3.6 %collective-permute-done.4.refs_1_ = bf16[4,192,128]{2,1,0:T(8,128)(2,1)S(1)} collective-permute-done((bf16[4,192,128]{2,1,0:T(8,128)(2,1)S(1)}, bf16[4,192,128]{2,1,0:T(8,128)(2,1)S(1)}, u32[]{:S(2)}, u32[]{:S(2)}) %collective-permute-start.4) | collective-permute-done | bytes 196640 | tf_op jit(solution)/shard_map/ppermute | solution.py:245
  27.2 0.1 collective-permute-start.5
  27.2 1.7 %collective-permute-start.6 = (bf16[2,192,128]{2,1,0:T(8,128)(2,1)S(1)}, bf16[2,192,128]{2,1,0:T(8,128)(2,1)S(1)}, u32[]{:S(2)}, u32[]{:S(2)}) collective-permute-start(bf16[2,192,128]{2,1,0:T(8,128)(2,1)S(1)} %get-tuple-element.24), channel_id=1, source_target_pairs={{0,8},{4,12},{8,0},{12,4},{1,9},{5,13},{9,1},{13,5},{2,10},{6,14},... | collective-permute-start | bytes 294920 | tf_op jit(solution)/shard_map/ppermute | solution.py:190
  29.0 2.8 %collective-permute-done.7.refs_4_ = bf16[768,128]{1,0:T(8,128)(2,1)S(1)} collective-permute-done((bf16[768,128]{1,0:T(8,128)(2,1)S(1)}, bf16[768,128]{1,0:T(8,128)(2,1)S(1)}, u32[]{:S(2)}, u32[]{:S(2)}) %collective-permute-start.7) | collective-permute-done | bytes 196640 | tf_op jit(solution)/shard_map/ppermute | solution.py:190
  31.8 0.0 collective-permute-done.8.refs_5_
  31.8 2.1 %collective-permute-done.5.refs_2_ = bf16[2,192,128]{2,1,0:T(8,128)(2,1)S(1)} collective-permute-done((bf16[2,192,128]{2,1,0:T(8,128)(2,1)S(1)}, bf16[2,192,128]{2,1,0:T(8,128)(2,1)S(1)}, u32[]{:S(2)}, u32[]{:S(2)}) %collective-permute-start.5) | collective-permute-done | bytes 98336 | tf_op jit(solution)/shard_map/ppermute | solution.py:190
  33.8 1.1 %finish.1 = (bf16[96,16,128]{2,1,0:T(8,128)(2,1)}, bf16[192,2,128]{2,1,0:T(2,128)(2,1)}, bf16[192,2,128]{2,1,0:T(2,128)(2,1)}) custom-call(f32[2,768,128]{2,1,0:T(8,128)S(1)} %get-tuple-element.20.own_dq_ref, bf16[4,192,128]{2,1,0:T(8,128)(2,1)S(1)} %get-tuple-element.21.refs_0_, bf16[4,192,128]{2,1,0:T(8,128)(2,1)S(1)} %collective-permute-done.3.refs_1_, ...), custom_call_target="tpu_custom_call" | custom-call | tf_op jit(solution)/shard_map/finish/pallas_call | solution.py:267
  (6 shorter events, 0.1 us)
Async XLA Ops:
  0.6 0.7 %copy-start = (s32[3,2]{0,1:T(2,128)S(1)}, s32[3,2]{0,1:T(2,128)}, u32[]{:S(2)}) copy-start(s32[3,2]{0,1:T(2,128)} %param.9) | copy-start | bytes 76
  3.2 9.7 %collective-permute-start.2 = (f32[16,128]{1,0:T(8,128)S(1)}, f32[16,128]{1,0:T(8,128)S(1)}, u32[]{:S(2)}, u32[]{:S(2)}) collective-permute-start(f32[16,128]{1,0:T(8,128)S(1)} %get-tuple-element.19), channel_id=1, source_target_pairs={{0,12},{4,8},{8,4},{12,0},{1,13},{5,9},{9,5},{13,1},{2,14},{6,10},... | collective-permute-start | bytes 24584 | tf_op jit(solution)/shard_map/ppermute | solution.py:190
  8.3 6.1 %collective-permute-start = (bf16[400,128]{1,0:T(8,128)(2,1)S(1)}, bf16[400,128]{1,0:T(8,128)(2,1)S(1)}, u32[]{:S(2)}, u32[]{:S(2)}) collective-permute-start(bf16[400,128]{1,0:T(8,128)(2,1)S(1)} %get-tuple-element.17.refs_3_), channel_id=1, source_target_pairs={{0,4},{4,0},{8,12},{12,8},{1,5},{5,1},{9,13},{13,9},{2,6},{6,2},{1... | collective-permute-start | bytes 307208 | tf_op jit(solution)/shard_map/ppermute | solution.py:190
  8.3 7.5 %collective-permute-start.1 = (bf16[400,128]{1,0:T(8,128)(2,1)S(1)}, bf16[400,128]{1,0:T(8,128)(2,1)S(1)}, u32[]{:S(2)}, u32[]{:S(2)}) collective-permute-start(bf16[400,128]{1,0:T(8,128)(2,1)S(1)} %get-tuple-element.18.refs_4_), channel_id=1, source_target_pairs={{0,8},{4,12},{8,0},{12,4},{1,9},{5,13},{9,1},{13,5},{2,10},{6,14},... | collective-permute-start | bytes 307208 | tf_op jit(solution)/shard_map/ppermute | solution.py:190
  19.4 7.7 %collective-permute-start.4 = (bf16[4,192,128]{2,1,0:T(8,128)(2,1)S(1)}, bf16[4,192,128]{2,1,0:T(8,128)(2,1)S(1)}, u32[]{:S(2)}, u32[]{:S(2)}) collective-permute-start(bf16[4,192,128]{2,1,0:T(8,128)(2,1)S(1)} %get-tuple-element.22.refs_0_), channel_id=1, source_target_pairs={{0,16},{16,0},{1,17},{17,1},{2,18},{18,2},{3,19},{19,3},{4,20},{20... | collective-permute-start | bytes 589832 | tf_op jit(solution)/shard_map/ppermute | solution.py:245
  20.9 10.8 %collective-permute-start.7 = (bf16[768,128]{1,0:T(8,128)(2,1)S(1)}, bf16[768,128]{1,0:T(8,128)(2,1)S(1)}, u32[]{:S(2)}, u32[]{:S(2)}) collective-permute-start(bf16[768,128]{1,0:T(8,128)(2,1)S(1)} %bitcast.11), channel_id=1, source_target_pairs={{0,8},{4,12},{8,0},{12,4},{1,9},{5,13},{9,1},{13,5},{2,10},{6,14},... | collective-permute-start | bytes 589832 | tf_op jit(solution)/shard_map/ppermute | solution.py:190
  21.3 10.4 %collective-permute-start.8 = (bf16[768,128]{1,0:T(8,128)(2,1)S(1)}, bf16[768,128]{1,0:T(8,128)(2,1)S(1)}, u32[]{:S(2)}, u32[]{:S(2)}) collective-permute-start(bf16[768,128]{1,0:T(8,128)(2,1)S(1)} %bitcast.10), channel_id=1, source_target_pairs={{0,4},{4,0},{8,12},{12,8},{1,5},{5,1},{9,13},{13,9},{2,6},{6,2},{1... | collective-permute-start | bytes 589832 | tf_op jit(solution)/shard_map/ppermute | solution.py:190
  23.0 8.8 %collective-permute-start.3 = (bf16[4,192,128]{2,1,0:T(8,128)(2,1)S(1)}, bf16[4,192,128]{2,1,0:T(8,128)(2,1)S(1)}, u32[]{:S(2)}, u32[]{:S(2)}) collective-permute-start(bf16[4,192,128]{2,1,0:T(8,128)(2,1)S(1)} %get-tuple-element.21.refs_0_), channel_id=1, source_target_pairs={{0,16},{16,0},{1,17},{17,1},{2,18},{18,2},{3,19},{19,3},{4,20},{20... | collective-permute-start | bytes 589832 | tf_op jit(solution)/shard_map/ppermute | solution.py:245
  27.2 6.7 %collective-permute-start.5 = (bf16[2,192,128]{2,1,0:T(8,128)(2,1)S(1)}, bf16[2,192,128]{2,1,0:T(8,128)(2,1)S(1)}, u32[]{:S(2)}, u32[]{:S(2)}) collective-permute-start(bf16[2,192,128]{2,1,0:T(8,128)(2,1)S(1)} %get-tuple-element.23), channel_id=1, source_target_pairs={{0,4},{4,0},{8,12},{12,8},{1,5},{5,1},{9,13},{13,9},{2,6},{6,2},{1... | collective-permute-start | bytes 294920 | tf_op jit(solution)/shard_map/ppermute | solution.py:190
  27.2 6.6 %collective-permute-start.6 = (bf16[2,192,128]{2,1,0:T(8,128)(2,1)S(1)}, bf16[2,192,128]{2,1,0:T(8,128)(2,1)S(1)}, u32[]{:S(2)}, u32[]{:S(2)}) collective-permute-start(bf16[2,192,128]{2,1,0:T(8,128)(2,1)S(1)} %get-tuple-element.24), channel_id=1, source_target_pairs={{0,8},{4,12},{8,0},{12,4},{1,9},{5,13},{9,1},{13,5},{2,10},{6,14},... | collective-permute-start | bytes 294920 | tf_op jit(solution)/shard_map/ppermute | solution.py:190

commit v3 on v2

v3 whole, which is shorter than its diff:
```python
import functools
import math

import jax
import jax.numpy as jnp
from jax import lax
from jax.experimental import pallas as pl
from jax.experimental.pallas import tpu as pltpu
from jax.sharding import PartitionSpec as P

KEYS_PER_SCALE = 64
LOG2E = math.log2(math.e)
VMEM = pl.BlockSpec(memory_space=pltpu.VMEM)
HBM = pl.BlockSpec(memory_space=pltpu.HBM)
NT = (((1,), (1,)), ((), ()))
SUM_ROWS = 16


def prep_kernel(powers_hbm, codes_hbm, values_hbm, *refs):
    *message_refs, sums_ref, powers_ref, codes_ref, values_ref, sems = refs
    key_count, kv_heads, width = codes_ref.shape
    load_codes = pltpu.make_async_copy(codes_hbm, codes_ref, sems.at[0])
    load_values = pltpu.make_async_copy(values_hbm, values_ref, sems.at[1])
    load_powers = pltpu.make_async_copy(powers_hbm, powers_ref, sems.at[2])
    load_powers.start()
    load_codes.start()
    load_values.start()
    rows = lax.broadcasted_iota(jnp.int32, (key_count, width), 0) // KEYS_PER_SCALE
    factors = []
    load_powers.wait()
    for g in range(kv_heads):
        factor = jnp.zeros((key_count, width), jnp.float32)
        for b in range(key_count // KEYS_PER_SCALE):
            power = jnp.left_shift(1, powers_ref[g, b] + 8).astype(jnp.float32) * 2.0**-8
            factor = jnp.where(rows == b, power, factor)
        factors.append(factor)
    load_codes.wait()
    load_values.wait()
    codes = codes_ref[...].astype(jnp.float32)
    values = values_ref[...].astype(jnp.float32)
    sums = []
    for g in range(kv_heads):
        wide = codes[:, g, :] * factors[g]
        message_refs[g][0:key_count] = wide.astype(jnp.bfloat16)
        message_refs[g][key_count : 2 * key_count] = values[:, g, :].astype(jnp.bfloat16)
        sums.append(jnp.sum(wide, axis=0, keepdims=True))
    line = lax.broadcasted_iota(jnp.int32, (SUM_ROWS, width), 0)
    parts = jnp.zeros((SUM_ROWS, width), jnp.float32)
    whole = jnp.zeros((SUM_ROWS, width), jnp.float32)
    for g in range(kv_heads):
        rest = sums[g]
        whole = jnp.where(line == g, rest, whole)
        for j in range(3):
            piece = rest.astype(jnp.bfloat16).astype(jnp.float32)
            parts = jnp.where(line == 3 * g + j, piece, parts)
            rest = rest - piece
    sums_ref[...] = whole
    for ref in message_refs:
        ref[2 * key_count : 2 * key_count + SUM_ROWS] = parts.astype(jnp.bfloat16)


def gather_kernel(
    row_sets, share, q_hbm, do_hbm, totals_hbm, dots_hbm,
    q_out, do_out, q_ref, do_ref, stats_ref, turned_ref, sems,
):
    ka = lax.axis_index("ka")
    kv_heads = len(row_sets)
    heads, width = q_ref.shape[2:]
    group = heads // kv_heads
    cols = share * group
    loads = []
    for j, src in enumerate((totals_hbm, dots_hbm)):
        load = pltpu.make_async_copy(src, stats_ref.at[pl.ds(j * heads, heads)], sems.at[j])
        load.start()
        loads.append(load)
    needed = sorted({m for sets in row_sets for m in sets})
    for at, m in enumerate(needed):
        for j, (src, dst) in enumerate(((q_hbm, q_ref), (do_hbm, do_ref))):
            load = pltpu.make_async_copy(
                src.at[pl.ds((ka ^ m) * share, share)], dst.at[at], sems.at[2 + 2 * at + j]
            )
            load.start()
            loads.append(load)
    loads[0].wait()
    loads[1].wait()
    stats_ref[pl.ds(2 * heads, width - 2 * heads)] = jnp.zeros(
        (width - 2 * heads, stats_ref.shape[1]), jnp.float32
    )
    rest = stats_ref[...].T
    lane = lax.broadcasted_iota(jnp.int32, rest.shape, 1)
    rest = jnp.where(lane < heads, jnp.clip(rest * LOG2E, -1e38, 1e38), rest)
    terms = jnp.zeros_like(rest)
    for j in range(3):
        piece = rest.astype(jnp.bfloat16).astype(jnp.float32)
        terms = terms + (pltpu.roll(piece, 2 * heads * j, 1) if j else piece)
        rest = rest - piece
    turned_ref[...] = terms
    spot = lax.broadcasted_iota(jnp.int32, (share, group, width), 2) % (2 * heads)
    spot = spot - lax.broadcasted_iota(jnp.int32, (share, group, width), 1)
    for at, m in enumerate(needed):
        rows = turned_ref[pl.ds((ka ^ m) * share, share)]
        rows = jnp.broadcast_to(rows[:, None, :], (share, group, width))
        for j, (src, dst) in enumerate(((q_ref, q_out), (do_ref, do_out))):
            loads[2 + 2 * at + j].wait()
            wide = src[at].astype(jnp.float32)
            for g in range(kv_heads):
                if m in row_sets[g]:
                    to = row_sets[g].index(m)
                    part = wide[:, g * group : (g + 1) * group].reshape(cols, width)
                    dst[g, to, :, 0:width] = part.astype(jnp.bfloat16)
                    extra = jnp.where(spot == j * heads + g * group, rows, 0.0)
                    dst[g, to, :, width:] = extra.reshape(cols, width).astype(jnp.bfloat16)


def rows_kernel(key_devices, share, heads, partners, row_sets, *refs):
    kv_heads = len(partners)
    q_ref, do_ref = refs[:2]
    own_refs, got_refs = refs[2 : 2 + kv_heads], refs[2 + kv_heads : 2 + 2 * kv_heads]
    dq_ref, cross_ref, keep_ref = refs[-3:]
    send_refs = refs[-3 - kv_heads : -3]
    sum_refs = refs[2 + 2 * kv_heads : -3 - kv_heads]
    ka, pb = lax.axis_index("ka"), lax.axis_index("pb")
    cols, width = q_ref.shape[2], q_ref.shape[3] // 2
    key_count = (own_refs[0].shape[0] - SUM_ROWS) // 2
    group = cols // share
    root = width**-0.5
    line = lax.broadcasted_iota(jnp.int32, (2 * key_count, cols), 0)
    step = lax.broadcasted_iota(jnp.int32, (2 * key_count, cols), 1) // group
    lane = lax.broadcasted_iota(jnp.int32, (2 * key_count, width), 1)
    minus = jnp.where(lane < 6 * heads, -1.0, 0.0).astype(jnp.bfloat16)
    parts = own_refs[0][2 * key_count :].astype(jnp.float32)
    for partner in dict(zip(partners, range(kv_heads))).values():
        parts = parts + got_refs[partner][2 * key_count :].astype(jnp.float32)
    whole = jnp.zeros((SUM_ROWS, width), jnp.float32)
    for ref in sum_refs:
        whole = whole + ref[...]
    for g in range(kv_heads):
        own, got = own_refs[g], got_refs[g]
        total = jnp.sum(parts[3 * g : 3 * g + 3], axis=0, keepdims=True) + whole[g : g + 1]
        mean = total / (key_count * key_devices)
        k = jnp.concatenate([own[0:key_count], got[0:key_count]], axis=0).astype(jnp.float32)
        k = (k - mean) * (root * LOG2E)
        turned = k.T.astype(jnp.bfloat16)
        k = jnp.concatenate([k.astype(jnp.bfloat16), minus], axis=1)
        v = jnp.concatenate(
            [own[key_count : 2 * key_count], got[key_count : 2 * key_count]], axis=0
        )
        v = jnp.concatenate([v, minus], axis=1)
        base = jnp.where(line < key_count, ka * key_count, ((ka ^ partners[g]) - 1) * key_count)
        lead = line + base - step
        dk = dv = None
        for at, m in enumerate(row_sets[g]):
            q, do = q_ref[g, at], do_ref[g, at]
            visible = lead <= pb * (share * key_devices) + (ka ^ m) * share
            scores = lax.dot_general(k, q, NT, preferred_element_type=jnp.float32)
            weights = jnp.where(visible, jnp.exp2(scores), 0.0)
            dp = lax.dot_general(v, do, NT, preferred_element_type=jnp.float32)
            ds = (weights * dp).astype(jnp.bfloat16)
            dv_now = jnp.dot(
                weights.astype(jnp.bfloat16), do[:, :width], preferred_element_type=jnp.float32
            )
            dk_now = jnp.dot(ds, q[:, :width], preferred_element_type=jnp.float32)
            dv = dv_now if dv is None else dv + dv_now
            dk = dk_now if dk is None else dk + dk_now
            dq = jnp.dot(turned, ds, preferred_element_type=jnp.float32).T * (1.0 / LOG2E)
            if m == 0:
                dq_ref[g] = dq
            else:
                others = [other for other in row_sets[g] if other]
                send_refs[g][others.index(m)] = dq.astype(jnp.bfloat16)
        for j, grad in ((2 * g, dk * root), (2 * g + 1, dv)):
            keep_ref[j] = grad[:key_count].astype(jnp.bfloat16)
            cross_ref[j] = grad[key_count:].astype(jnp.bfloat16)


def across_kernel(*refs):
    *in_refs, out_a, out_b = refs
    total = in_refs[0][...].astype(jnp.float32)
    for ref in in_refs[1:]:
        total = total + ref[...].astype(jnp.float32)
    half = out_a.shape[0]
    out_a[...] = total[:half].astype(jnp.bfloat16)
    out_b[...] = total[half:].astype(jnp.bfloat16)


def finish_rows_kernel(kv_heads, own_ref, *refs):
    *back_refs, dq_ref = refs
    share, heads, width = dq_ref.shape
    outs = []
    for g in range(kv_heads):
        dq = own_ref[g]
        for ref in back_refs[kv_heads - 1 - g :: kv_heads]:
            dq = dq + ref[...].astype(jnp.float32)
        outs.append(dq.reshape(share, heads // kv_heads, width))
    dq_ref[...] = jnp.concatenate(outs, axis=1).astype(jnp.bfloat16)


def finish_keys_kernel(*refs):
    *keep_refs, z_a, z_b, dk_ref, dv_ref = refs
    total = keep_refs[0][...].astype(jnp.float32)
    for ref in keep_refs[1:]:
        total = total + ref[...].astype(jnp.float32)
    total = total + jnp.concatenate([z_a[...], z_b[...]], axis=0).astype(jnp.float32)
    for j, ref in enumerate((dk_ref, dv_ref)):
        grads = jnp.stack([total[2 * g + j] for g in range(ref.shape[1])], axis=1)
        ref[...] = grads.astype(jnp.bfloat16)


def per_device(queries, key_codes, key_scale_powers, values, grad_out, grad_dot, log_totals):
    query_count, head_count, width = queries.shape
    key_count, kv_heads, _ = key_codes.shape
    group = head_count // kv_heads
    key_devices = lax.axis_size("ka")
    query_devices = lax.axis_size("pb")
    share = query_count // key_devices
    cols = share * group
    params = pltpu.CompilerParams(vmem_limit_bytes=24 * 2**20)
    top = key_devices // 2
    partners = [top if g < kv_heads // 2 else 1 for g in range(kv_heads)]
    row_sets = [[m for m in range(key_devices) if not m & p] for p in partners]
    shape = jax.ShapeDtypeStruct

    def swap(x, by):
        return lax.ppermute(x, "ka", [(i, i ^ by) for i in range(key_devices)])

    def pinned(x):
        return pltpu.with_memory_space_constraint(x, pltpu.HBM)

    *messages, sums = pl.pallas_call(
        prep_kernel,
        out_shape=(shape((2 * key_count + SUM_ROWS, width), jnp.bfloat16),) * kv_heads
        + (shape((SUM_ROWS, width), jnp.float32),),
        in_specs=[HBM, HBM, HBM],
        out_specs=(VMEM,) * (kv_heads + 1),
        scratch_shapes=[
            pltpu.SMEM(key_scale_powers.shape[::-1], jnp.int32),
            pltpu.VMEM(key_codes.shape, key_codes.dtype),
            pltpu.VMEM(values.shape, values.dtype),
            pltpu.SemaphoreType.DMA((3,)),
        ],
        compiler_params=params,
        name="prep",
    )(pinned(key_scale_powers.T), pinned(key_codes), pinned(values))
    got = [swap(message, by) for message, by in zip(messages, partners)]

    others = [swap(sums, by) for by in range(1, key_devices) if by not in partners]
    needed = sorted({m for sets in row_sets for m in sets})
    laid = shape((kv_heads, key_devices // 2, cols, 2 * width), jnp.bfloat16)
    rows_q, rows_do = pl.pallas_call(
        functools.partial(gather_kernel, row_sets, share),
        out_shape=(laid, laid),
        in_specs=[HBM] * 4,
        out_specs=(VMEM,) * 2,
        scratch_shapes=[
            pltpu.VMEM((len(needed), share, head_count, width), queries.dtype),
            pltpu.VMEM((len(needed), share, head_count, width), grad_out.dtype),
            pltpu.VMEM((width, query_count), jnp.float32),
            pltpu.VMEM((query_count, width), jnp.float32),
            pltpu.SemaphoreType.DMA((2 + 2 * len(needed),)),
        ],
        compiler_params=params,
        name="gather",
    )(pinned(queries), pinned(grad_out), pinned(log_totals.T), pinned(grad_dot.T))

    part = shape((2 * kv_heads, key_count, width), jnp.bfloat16)
    sent = shape((key_devices // 2 - 1, cols, width), jnp.bfloat16)
    *sends, own_dq, cross, keep = pl.pallas_call(
        functools.partial(
            rows_kernel, key_devices, share, head_count, partners, row_sets
        ),
        out_shape=(sent,) * kv_heads + (shape((kv_heads, cols, width), jnp.float32), part, part),
        in_specs=[VMEM] * (2 + 2 * kv_heads + len(others)),
        out_specs=(VMEM,) * (kv_heads + 3),
        compiler_params=params,
        name="rows",
    )(rows_q, rows_do, *messages, *got, *others)

    def over_queries(x):
        if query_devices == 2:
            return [x, lax.ppermute(x, "pb", [(0, 1), (1, 0)])]
        return [lax.psum(x.astype(jnp.float32), "pb")]

    crossed = over_queries(cross)
    back = []
    for at in range(key_devices // 2 - 1):
        for g in reversed(range(kv_heads)):
            back.append(swap(sends[g][at], [m for m in row_sets[g] if m][at]))
    kept = over_queries(keep)
    half = shape((kv_heads, key_count, width), jnp.bfloat16)
    z_a, z_b = pl.pallas_call(
        across_kernel,
        out_shape=(half, half),
        in_specs=[VMEM] * len(crossed),
        out_specs=(VMEM, VMEM),
        compiler_params=params,
        cost_estimate=pl.CostEstimate(
            flops=10**10, bytes_accessed=2**20, transcendentals=0
        ),
        name="across",
    )(*crossed)
    z = [swap(z_a, partners[0]), swap(z_b, partners[-1])]
    dq = pl.pallas_call(
        functools.partial(finish_rows_kernel, kv_heads),
        out_shape=shape((share, head_count, width), jnp.bfloat16),
        in_specs=[VMEM] * (1 + len(back)),
        out_specs=VMEM,
        compiler_params=params,
        name="finish_rows",
    )(own_dq, *back)
    dk, dv = pl.pallas_call(
        finish_keys_kernel,
        out_shape=(
            shape(key_codes.shape, jnp.bfloat16),
            shape(values.shape, jnp.bfloat16),
        ),
        in_specs=[VMEM] * (len(kept) + len(z)),
        out_specs=(VMEM, VMEM),
        compiler_params=params,
        name="finish_keys",
    )(*kept, *z)
    return dq, dk, dv


def solution(mesh):
    in_specs = (
        P("pb", "ha", None),
        P("ka", "ha", None),
        P("ka", "ha"),
        P("ka", "ha", None),
        P("pb", "ha", None),
        P("pb", "ha"),
        P("pb", "ha"),
    )
    out_specs = (P(("pb", "ka"), "ha", None), P("ka", "ha", None), P("ka", "ha", None))
    return jax.shard_map(
        per_device, mesh=mesh, in_specs=in_specs, out_specs=out_specs, check_vma=False
    )
```

time: 35.2 us -> 34 us (0.966)
  starting transfers between devices: 11.7 us -> 14.8 us
  waiting for transfers between devices: 11.3 us -> 9.74 us
  other arithmetic: 1.48 us -> 0 us
  local copies, waits for them, and re-layouts: 1.46 us -> 0 us
  Pallas kernels: 8.24 us -> 8.63 us
    ppermute x7, starting transfers between devices: 9.6 us -> 12.7 us  [swap(): return lax.ppermute(x, 'ka', [(i, i ^ by) for i in range(key_devices)])]
    ppermute x2, waiting for transfers between devices: 3.59 us -> 1.32 us  [over_queries(): return [x, lax.ppermute(x, 'pb', [(0, 1), (1, 0)])]]
    pallas_call x2 -> x3, Pallas kernels: 4.64 us -> 5.48 us  [the longest x1 3.61 us: per_device(): pl.pallas_call(functools.partial(rows_kernel, key_devices, share, head_co...]
    reshape x3 -> x0, local copies, waits for them, and re-layouts: 0.79 us -> none  [the longest x1 0.41 us: per_device(): stats = stats.transpose(2, 0, 3, 1).reshape(key_devices, 2 * kv_heads, cols)]
    concatenate x1 -> x0, other arithmetic: 0.74 us -> none  [per_device(): stats = jnp.concatenate([log_totals.T * LOG2E, grad_dot.T], axis=0)]
    mul x1 -> x0, other arithmetic: 0.74 us -> none  [per_device(): stats = jnp.concatenate([log_totals.T * LOG2E, grad_dot.T], axis=0)]
    ppermute x7, waiting for transfers between devices: 7.74 us -> 8.43 us  [swap(): return lax.ppermute(x, 'ka', [(i, i ^ by) for i in range(key_devices)])]
    unnamed x2 -> x0, local copies, waits for them, and re-layouts: 0.67 us -> none
  transfers between devices with their start and end apart: 9 -> 9, of which waited for: 5 -> 5; matrix products, arithmetic and copies ran while one was open for 7% -> 0% of each run, Pallas kernels for 5% -> 8%
where the time goes in v3:
time: 34 us; the launch traced here: 33.8 us
  starting transfers between devices  14.8 us (44%)
  waiting for transfers between devices  9.74 us (29%)
  Pallas kernels  8.63 us (25%)
  between operations  0.67 us (2%)
    ppermute x7, starting transfers between devices, swap(): return lax.ppermute(x, 'ka', [(i, i ^ by) for i in range(key_devices)])  12.7 us
    ppermute x7, waiting for transfers between devices, swap(): return lax.ppermute(x, 'ka', [(i, i ^ by) for i in range(key_devices)])  8.43 us
    pallas_call x1, Pallas kernels, per_device(): pl.pallas_call(functools.partial(rows_kernel, key_devices, share, head_co...  3.61 us
    ppermute x2, starting transfers between devices, over_queries(): return [x, lax.ppermute(x, 'pb', [(0, 1), (1, 0)])]  2.09 us
    pallas_call x1, Pallas kernels, per_device(): pl.pallas_call(functools.partial(gather_kernel, row_sets, share), out_sha...  1.76 us
    pallas_call x1, Pallas kernels, per_device(): pl.pallas_call(prep_kernel, out_shape=(shape((2 * key_count + SUM_ROWS, w...  1.34 us
    ppermute x2, waiting for transfers between devices, over_queries(): return [x, lax.ppermute(x, 'pb', [(0, 1), (1, 0)])]  1.32 us
    pallas_call x1, Pallas kernels, per_device(): pl.pallas_call(finish_keys_kernel, out_shape=(shape(key_codes.shape, jnp....  1.02 us
  transfers between devices with their start and end apart: 9, of which 5 were waited for; matrix products, arithmetic and copies ran while one was open for 0% of the time, Pallas kernels for 8%

profile of v3, /device:TPU:0, one launch (start us, length us, event | category | flops | bytes accessed | tf_op | source)
XLA Modules:
  0.0 33.8 jit_solution(11093572923922192028)
XLA Ops:
  0.6 1.3 %prep.1 = (bf16[400,128]{1,0:T(8,128)(2,1)S(1)}, bf16[400,128]{1,0:T(8,128)(2,1)S(1)}, f32[16,128]{1,0:T(8,128)S(1)}) custom-call(s32[2,3]{1,0:T(2,128)} %bitcast.9, bf16[192,2,128]{2,1,0:T(2,128)(2,1)} %codes_hbm.1, bf16[192,2,128]{2,1,0:T(2,128)(2,1)} %values_hbm.1), custom_call_target="tpu_custom_call" | custom-call | tf_op jit(solution)/shard_map/prep/pallas_call | solution.py:229
  2.0 4.1 %collective-permute-start = (bf16[400,128]{1,0:T(8,128)(2,1)S(1)}, bf16[400,128]{1,0:T(8,128)(2,1)S(1)}, u32[]{:S(2)}, u32[]{:S(2)}) collective-permute-start(bf16[400,128]{1,0:T(8,128)(2,1)S(1)} %get-tuple-element.19.refs_2_), channel_id=1, source_target_pairs={{0,8},{4,12},{8,0},{12,4},{1,9},{5,13},{9,1},{13,5},{2,10},{6,14},... | collective-permute-start | bytes 307208 | tf_op jit(solution)/shard_map/ppermute | solution.py:224
  6.1 1.6 %collective-permute-start.1 = (bf16[400,128]{1,0:T(8,128)(2,1)S(1)}, bf16[400,128]{1,0:T(8,128)(2,1)S(1)}, u32[]{:S(2)}, u32[]{:S(2)}) collective-permute-start(bf16[400,128]{1,0:T(8,128)(2,1)S(1)} %get-tuple-element.20.refs_3_), channel_id=1, source_target_pairs={{0,4},{4,0},{8,12},{12,8},{1,5},{5,1},{9,13},{13,9},{2,6},{6,2},{1... | collective-permute-start | bytes 307208 | tf_op jit(solution)/shard_map/ppermute | solution.py:224
  7.7 0.0 collective-permute-start.2
  7.7 1.8 %gather.1 = (bf16[2,2,768,256]{3,2,1,0:T(8,128)(2,1)S(1)}, bf16[2,2,768,256]{3,2,1,0:T(8,128)(2,1)S(1)}) custom-call(bf16[384,16,128]{2,1,0:T(8,128)(2,1)} %q_hbm.1, bf16[384,16,128]{2,1,0:T(8,128)(2,1)} %do_hbm.1, f32[16,384]{1,0:T(8,128)} %bitcast.7, f32[16,384]{1,0:T(8,128)} %bitcast.8), custom_call_target="tpu_custom_call" | custom-call | tf_op jit(solution)/shard_map/gather/pallas_call | solution.py:249
  9.4 3.7 %collective-permute-done.2.refs_6_ = f32[16,128]{1,0:T(8,128)S(1)} collective-permute-done((f32[16,128]{1,0:T(8,128)S(1)}, f32[16,128]{1,0:T(8,128)S(1)}, u32[]{:S(2)}, u32[]{:S(2)}) %collective-permute-start.2) | collective-permute-done | bytes 8224 | tf_op jit(solution)/shard_map/ppermute | solution.py:224
  13.1 0.0 collective-permute-done.refs_4_
  13.1 0.0 collective-permute-done.1.refs_5_
  13.1 3.6 %rows.1 = (bf16[1,768,128]{2,1,0:T(8,128)(2,1)S(1)}, bf16[1,768,128]{2,1,0:T(8,128)(2,1)S(1)}, f32[2,768,128]{2,1,0:T(8,128)S(1)}, bf16[4,192,128]{2,1,0:T(8,128)(2,1)S(1)}, bf16[4,192,128]{2,1,0:T(8,128)(2,1)S(1)}) custom-call(bf16[2,2,768,256]{3,2,1,0:T(8,128)(2,1)S(1)} %get-tuple-element.17.refs_0_, ...), custom_call_target="tpu_custom_call" | custom-call | tf_op jit(solution)/shard_map/rows/pallas_call | solution.py:267
  16.7 1.6 %collective-permute-start.6 = (bf16[4,192,128]{2,1,0:T(8,128)(2,1)S(1)}, bf16[4,192,128]{2,1,0:T(8,128)(2,1)S(1)}, u32[]{:S(2)}, u32[]{:S(2)}) collective-permute-start(bf16[4,192,128]{2,1,0:T(8,128)(2,1)S(1)} %get-tuple-element.26.refs_0_), channel_id=1, source_target_pairs={{0,16},{16,0},{1,17},{17,1},{2,18},{18,2},{3,19},{19,3},{4,20},{20... | collective-permute-start | bytes 589832 | tf_op jit(solution)/shard_map/ppermute | solution.py:280
  18.3 1.0 %collective-permute-start.3 = (bf16[768,128]{1,0:T(8,128)(2,1)S(1)}, bf16[768,128]{1,0:T(8,128)(2,1)S(1)}, u32[]{:S(2)}, u32[]{:S(2)}) collective-permute-start(bf16[768,128]{1,0:T(8,128)(2,1)S(1)} %bitcast.6), channel_id=1, source_target_pairs={{0,8},{4,12},{8,0},{12,4},{1,9},{5,13},{9,1},{13,5},{2,10},{6,14},... | collective-permute-start | bytes 589832 | tf_op jit(solution)/shard_map/ppermute | solution.py:224
  19.3 1.4 %collective-permute-start.4 = (bf16[768,128]{1,0:T(8,128)(2,1)S(1)}, bf16[768,128]{1,0:T(8,128)(2,1)S(1)}, u32[]{:S(2)}, u32[]{:S(2)}) collective-permute-start(bf16[768,128]{1,0:T(8,128)(2,1)S(1)} %bitcast.5), channel_id=1, source_target_pairs={{0,4},{4,0},{8,12},{12,8},{1,5},{5,1},{9,13},{13,9},{2,6},{6,2},{1... | collective-permute-start | bytes 589832 | tf_op jit(solution)/shard_map/ppermute | solution.py:224
  20.8 0.5 %collective-permute-start.5 = (bf16[4,192,128]{2,1,0:T(8,128)(2,1)S(1)}, bf16[4,192,128]{2,1,0:T(8,128)(2,1)S(1)}, u32[]{:S(2)}, u32[]{:S(2)}) collective-permute-start(bf16[4,192,128]{2,1,0:T(8,128)(2,1)S(1)} %get-tuple-element.25.refs_0_), channel_id=1, source_target_pairs={{0,16},{16,0},{1,17},{17,1},{2,18},{18,2},{3,19},{19,3},{4,20},{20... | collective-permute-start | bytes 589832 | tf_op jit(solution)/shard_map/ppermute | solution.py:280
  21.3 1.3 %collective-permute-done.6.refs_1_ = bf16[4,192,128]{2,1,0:T(8,128)(2,1)S(1)} collective-permute-done((bf16[4,192,128]{2,1,0:T(8,128)(2,1)S(1)}, bf16[4,192,128]{2,1,0:T(8,128)(2,1)S(1)}, u32[]{:S(2)}, u32[]{:S(2)}) %collective-permute-start.6) | collective-permute-done | bytes 196640 | tf_op jit(solution)/shard_map/ppermute | solution.py:280
  22.6 0.1 across.1
  22.7 3.1 %collective-permute-start.7 = (bf16[2,192,128]{2,1,0:T(8,128)(2,1)S(1)}, bf16[2,192,128]{2,1,0:T(8,128)(2,1)S(1)}, u32[]{:S(2)}, u32[]{:S(2)}) collective-permute-start(bf16[2,192,128]{2,1,0:T(8,128)(2,1)S(1)} %get-tuple-element.27), channel_id=1, source_target_pairs={{0,8},{4,12},{8,0},{12,4},{1,9},{5,13},{9,1},{13,5},{2,10},{6,14},... | collective-permute-start | bytes 294920 | tf_op jit(solution)/shard_map/ppermute | solution.py:224
  25.8 1.4 %collective-permute-start.8 = (bf16[2,192,128]{2,1,0:T(8,128)(2,1)S(1)}, bf16[2,192,128]{2,1,0:T(8,128)(2,1)S(1)}, u32[]{:S(2)}, u32[]{:S(2)}) collective-permute-start(bf16[2,192,128]{2,1,0:T(8,128)(2,1)S(1)} %get-tuple-element.28), channel_id=1, source_target_pairs={{0,4},{4,0},{8,12},{12,8},{1,5},{5,1},{9,13},{13,9},{2,6},{6,2},{1... | collective-permute-start | bytes 294920 | tf_op jit(solution)/shard_map/ppermute | solution.py:224
  27.2 3.1 %collective-permute-done.3.refs_0_ = bf16[768,128]{1,0:T(8,128)(2,1)S(1)} collective-permute-done((bf16[768,128]{1,0:T(8,128)(2,1)S(1)}, bf16[768,128]{1,0:T(8,128)(2,1)S(1)}, u32[]{:S(2)}, u32[]{:S(2)}) %collective-permute-start.3) | collective-permute-done | bytes 196640 | tf_op jit(solution)/shard_map/ppermute | solution.py:224
  30.3 0.0 collective-permute-done.4.refs_1_
  30.3 0.8 %finish_rows.1 = bf16[96,16,128]{2,1,0:T(8,128)(2,1)} custom-call(f32[2,768,128]{2,1,0:T(8,128)S(1)} %get-tuple-element.22.own_ref, bf16[768,128]{1,0:T(8,128)(2,1)S(1)} %collective-permute-done.3.refs_0_, bf16[768,128]{1,0:T(8,128)(2,1)S(1)} %collective-permute-done.4.refs_1_), custom_call_target="tpu_custom_call" | custom-call | tf_op jit(solution)/shard_map/finish_rows/pallas_call | solution.py:302
  31.1 0.0 collective-permute-done.5.refs_1_
  31.1 1.4 %collective-permute-done.7.refs_2_ = bf16[2,192,128]{2,1,0:T(8,128)(2,1)S(1)} collective-permute-done((bf16[2,192,128]{2,1,0:T(8,128)(2,1)S(1)}, bf16[2,192,128]{2,1,0:T(8,128)(2,1)S(1)}, u32[]{:S(2)}, u32[]{:S(2)}) %collective-permute-start.7) | collective-permute-done | bytes 98336 | tf_op jit(solution)/shard_map/ppermute | solution.py:224
  32.6 0.2 collective-permute-done.8.refs_3_
  32.8 1.0 %finish_keys.1 = (bf16[192,2,128]{2,1,0:T(2,128)(2,1)}, bf16[192,2,128]{2,1,0:T(2,128)(2,1)}) custom-call(bf16[4,192,128]{2,1,0:T(8,128)(2,1)S(1)} %get-tuple-element.25.refs_0_, bf16[4,192,128]{2,1,0:T(8,128)(2,1)S(1)} %collective-permute-done.5.refs_1_, bf16[2,192,128]{2,1,0:T(8,128)(2,1)S(1)} %collective-permute-done.7.refs_2_, ...), custom_call_target="tpu_custom_call" | custom-call | tf_op jit(solution)/shard_map/finish_keys/pallas_call | solution.py:310
Async XLA Ops:
  2.0 11.1 %collective-permute-start = (bf16[400,128]{1,0:T(8,128)(2,1)S(1)}, bf16[400,128]{1,0:T(8,128)(2,1)S(1)}, u32[]{:S(2)}, u32[]{:S(2)}) collective-permute-start(bf16[400,128]{1,0:T(8,128)(2,1)S(1)} %get-tuple-element.19.refs_2_), channel_id=1, source_target_pairs={{0,8},{4,12},{8,0},{12,4},{1,9},{5,13},{9,1},{13,5},{2,10},{6,14},... | collective-permute-start | bytes 307208 | tf_op jit(solution)/shard_map/ppermute | solution.py:224
  6.1 7.0 %collective-permute-start.1 = (bf16[400,128]{1,0:T(8,128)(2,1)S(1)}, bf16[400,128]{1,0:T(8,128)(2,1)S(1)}, u32[]{:S(2)}, u32[]{:S(2)}) collective-permute-start(bf16[400,128]{1,0:T(8,128)(2,1)S(1)} %get-tuple-element.20.refs_3_), channel_id=1, source_target_pairs={{0,4},{4,0},{8,12},{12,8},{1,5},{5,1},{9,13},{13,9},{2,6},{6,2},{1... | collective-permute-start | bytes 307208 | tf_op jit(solution)/shard_map/ppermute | solution.py:224
  7.7 5.4 %collective-permute-start.2 = (f32[16,128]{1,0:T(8,128)S(1)}, f32[16,128]{1,0:T(8,128)S(1)}, u32[]{:S(2)}, u32[]{:S(2)}) collective-permute-start(f32[16,128]{1,0:T(8,128)S(1)} %get-tuple-element.21), channel_id=1, source_target_pairs={{0,12},{4,8},{8,4},{12,0},{1,13},{5,9},{9,5},{13,1},{2,14},{6,10},... | collective-permute-start | bytes 24584 | tf_op jit(solution)/shard_map/ppermute | solution.py:224
  16.7 5.9 %collective-permute-start.6 = (bf16[4,192,128]{2,1,0:T(8,128)(2,1)S(1)}, bf16[4,192,128]{2,1,0:T(8,128)(2,1)S(1)}, u32[]{:S(2)}, u32[]{:S(2)}) collective-permute-start(bf16[4,192,128]{2,1,0:T(8,128)(2,1)S(1)} %get-tuple-element.26.refs_0_), channel_id=1, source_target_pairs={{0,16},{16,0},{1,17},{17,1},{2,18},{18,2},{3,19},{19,3},{4,20},{20... | collective-permute-start | bytes 589832 | tf_op jit(solution)/shard_map/ppermute | solution.py:280
  18.3 12.0 %collective-permute-start.3 = (bf16[768,128]{1,0:T(8,128)(2,1)S(1)}, bf16[768,128]{1,0:T(8,128)(2,1)S(1)}, u32[]{:S(2)}, u32[]{:S(2)}) collective-permute-start(bf16[768,128]{1,0:T(8,128)(2,1)S(1)} %bitcast.6), channel_id=1, source_target_pairs={{0,8},{4,12},{8,0},{12,4},{1,9},{5,13},{9,1},{13,5},{2,10},{6,14},... | collective-permute-start | bytes 589832 | tf_op jit(solution)/shard_map/ppermute | solution.py:224
  19.3 11.0 %collective-permute-start.4 = (bf16[768,128]{1,0:T(8,128)(2,1)S(1)}, bf16[768,128]{1,0:T(8,128)(2,1)S(1)}, u32[]{:S(2)}, u32[]{:S(2)}) collective-permute-start(bf16[768,128]{1,0:T(8,128)(2,1)S(1)} %bitcast.5), channel_id=1, source_target_pairs={{0,4},{4,0},{8,12},{12,8},{1,5},{5,1},{9,13},{13,9},{2,6},{6,2},{1... | collective-permute-start | bytes 589832 | tf_op jit(solution)/shard_map/ppermute | solution.py:224
  20.8 10.4 %collective-permute-start.5 = (bf16[4,192,128]{2,1,0:T(8,128)(2,1)S(1)}, bf16[4,192,128]{2,1,0:T(8,128)(2,1)S(1)}, u32[]{:S(2)}, u32[]{:S(2)}) collective-permute-start(bf16[4,192,128]{2,1,0:T(8,128)(2,1)S(1)} %get-tuple-element.25.refs_0_), channel_id=1, source_target_pairs={{0,16},{16,0},{1,17},{17,1},{2,18},{18,2},{3,19},{19,3},{4,20},{20... | collective-permute-start | bytes 589832 | tf_op jit(solution)/shard_map/ppermute | solution.py:280
  22.7 9.9 %collective-permute-start.7 = (bf16[2,192,128]{2,1,0:T(8,128)(2,1)S(1)}, bf16[2,192,128]{2,1,0:T(8,128)(2,1)S(1)}, u32[]{:S(2)}, u32[]{:S(2)}) collective-permute-start(bf16[2,192,128]{2,1,0:T(8,128)(2,1)S(1)} %get-tuple-element.27), channel_id=1, source_target_pairs={{0,8},{4,12},{8,0},{12,4},{1,9},{5,13},{9,1},{13,5},{2,10},{6,14},... | collective-permute-start | bytes 294920 | tf_op jit(solution)/shard_map/ppermute | solution.py:224
  25.8 7.0 %collective-permute-start.8 = (bf16[2,192,128]{2,1,0:T(8,128)(2,1)S(1)}, bf16[2,192,128]{2,1,0:T(8,128)(2,1)S(1)}, u32[]{:S(2)}, u32[]{:S(2)}) collective-permute-start(bf16[2,192,128]{2,1,0:T(8,128)(2,1)S(1)} %get-tuple-element.28), channel_id=1, source_target_pairs={{0,4},{4,0},{8,12},{12,8},{1,5},{5,1},{9,13},{13,9},{2,6},{6,2},{1... | collective-permute-start | bytes 294920 | tf_op jit(solution)/shard_map/ppermute | solution.py:224

commit v4 on v3

--- a/solution.py
+++ b/solution.py
@@ -88,7 +88,7 @@
     )
     rest = stats_ref[...].T
     lane = lax.broadcasted_iota(jnp.int32, rest.shape, 1)
-    rest = jnp.where(lane < heads, jnp.clip(rest * LOG2E, -1e38, 1e38), rest)
+    rest = jnp.where(lane < heads, jnp.clip(rest, -1e36, 1e36) * width**0.5, rest)
     terms = jnp.zeros_like(rest)
     for j in range(3):
         piece = rest.astype(jnp.bfloat16).astype(jnp.float32)
@@ -112,13 +112,22 @@
                     dst[g, to, :, width:] = extra.reshape(cols, width).astype(jnp.bfloat16)
 
 
-def rows_kernel(key_devices, share, heads, partners, row_sets, *refs):
+def rows_kernel(key_devices, share, heads, partners, row_sets, tasks, first, *refs):
     kv_heads = len(partners)
-    q_ref, do_ref = refs[:2]
-    own_refs, got_refs = refs[2 : 2 + kv_heads], refs[2 + kv_heads : 2 + 2 * kv_heads]
-    dq_ref, cross_ref, keep_ref = refs[-3:]
-    send_refs = refs[-3 - kv_heads : -3]
-    sum_refs = refs[2 + 2 * kv_heads : -3 - kv_heads]
+    busy = [g for g in range(kv_heads) if tasks[g]]
+    pieces = 2 if first else 1
+    sending = [g for g in busy if any(tasks[g]) for _ in range(pieces)]
+    ends = [g for g in range(kv_heads) if partners[g] != partners[0]]
+    q_ref, do_ref, *refs = refs
+    own_refs, got_refs, refs = refs[:kv_heads], refs[kv_heads : 2 * kv_heads], refs[2 * kv_heads :]
+    if first:
+        *sum_refs, acc_ref = refs[: -len(sending)]
+        send_refs = list(zip(sending, refs[-len(sending) :]))
+    else:
+        dq_ref, keep_ref = refs[-2 - kv_heads : -kv_heads]
+        cross_refs, refs = refs[-kv_heads:], refs[: -2 - kv_heads]
+        send_refs = list(zip(sending, refs[-len(sending) :]))
+        *sum_refs, acc_ref = refs[: -len(sending)]
     ka, pb = lax.axis_index("ka"), lax.axis_index("pb")
     cols, width = q_ref.shape[2], q_ref.shape[3] // 2
     key_count = (own_refs[0].shape[0] - SUM_ROWS) // 2
@@ -134,14 +143,14 @@
     whole = jnp.zeros((SUM_ROWS, width), jnp.float32)
     for ref in sum_refs:
         whole = whole + ref[...]
-    for g in range(kv_heads):
+    for g in busy:
         own, got = own_refs[g], got_refs[g]
         total = jnp.sum(parts[3 * g : 3 * g + 3], axis=0, keepdims=True) + whole[g : g + 1]
         mean = total / (key_count * key_devices)
         k = jnp.concatenate([own[0:key_count], got[0:key_count]], axis=0).astype(jnp.float32)
-        k = (k - mean) * (root * LOG2E)
-        turned = k.T.astype(jnp.bfloat16)
-        k = jnp.concatenate([k.astype(jnp.bfloat16), minus], axis=1)
+        k = (k - mean).astype(jnp.bfloat16)
+        turned = k.astype(jnp.float32).T.astype(jnp.bfloat16)
+        k = jnp.concatenate([k, minus], axis=1)
         v = jnp.concatenate(
             [own[key_count : 2 * key_count], got[key_count : 2 * key_count]], axis=0
         )
@@ -149,11 +158,14 @@
         base = jnp.where(line < key_count, ka * key_count, ((ka ^ partners[g]) - 1) * key_count)
         lead = line + base - step
         dk = dv = None
-        for at, m in enumerate(row_sets[g]):
+        if not first and g in ends:
+            dk, dv = acc_ref[2 * ends.index(g)], acc_ref[2 * ends.index(g) + 1]
+        for m in tasks[g]:
+            at = row_sets[g].index(m)
             q, do = q_ref[g, at], do_ref[g, at]
             visible = lead <= pb * (share * key_devices) + (ka ^ m) * share
             scores = lax.dot_general(k, q, NT, preferred_element_type=jnp.float32)
-            weights = jnp.where(visible, jnp.exp2(scores), 0.0)
+            weights = jnp.where(visible, jnp.exp2(scores * (root * LOG2E)), 0.0)
             dp = lax.dot_general(v, do, NT, preferred_element_type=jnp.float32)
             ds = (weights * dp).astype(jnp.bfloat16)
             dv_now = jnp.dot(
@@ -162,45 +174,69 @@
             dk_now = jnp.dot(ds, q[:, :width], preferred_element_type=jnp.float32)
             dv = dv_now if dv is None else dv + dv_now
             dk = dk_now if dk is None else dk + dk_now
-            dq = jnp.dot(turned, ds, preferred_element_type=jnp.float32).T * (1.0 / LOG2E)
+            dq = jnp.dot(turned, ds, preferred_element_type=jnp.float32).T * root
             if m == 0:
                 dq_ref[g] = dq
             else:
                 others = [other for other in row_sets[g] if other]
-                send_refs[g][others.index(m)] = dq.astype(jnp.bfloat16)
-        for j, grad in ((2 * g, dk * root), (2 * g + 1, dv)):
-            keep_ref[j] = grad[:key_count].astype(jnp.bfloat16)
-            cross_ref[j] = grad[key_count:].astype(jnp.bfloat16)
-
-
-def across_kernel(*refs):
-    *in_refs, out_a, out_b = refs
+                for j, ref in enumerate(ref for to, ref in send_refs if to == g):
+                    piece = dq[j * cols // pieces : (j + 1) * cols // pieces]
+                    ref[others.index(m)] = piece.astype(jnp.bfloat16)
+        if first:
+            acc_ref[2 * ends.index(g)] = dk
+            acc_ref[2 * ends.index(g) + 1] = dv
+        else:
+            for j, grad in enumerate((dk * root, dv)):
+                keep_ref[2 * g + j] = grad[:key_count].astype(jnp.bfloat16)
+                cross_refs[g][j] = grad[key_count:].astype(jnp.bfloat16)
+
+
+def across_kernel(after_ref, *refs):
+    *in_refs, out_ref = refs
     total = in_refs[0][...].astype(jnp.float32)
     for ref in in_refs[1:]:
         total = total + ref[...].astype(jnp.float32)
-    half = out_a.shape[0]
-    out_a[...] = total[:half].astype(jnp.bfloat16)
-    out_b[...] = total[half:].astype(jnp.bfloat16)
-
-
-def finish_rows_kernel(kv_heads, own_ref, *refs):
+    out_ref[...] = total.astype(jnp.bfloat16)
+
+
+def far_rows_kernel(ends, own_ref, *refs):
+    *back_refs, sum_ref = refs
+    for j, g in enumerate(ends):
+        dq = own_ref[g, : own_ref.shape[1] // 2]
+        for ref in back_refs[j :: len(ends)]:
+            dq = dq + ref[...].astype(jnp.float32)
+        sum_ref[j] = dq
+
+
+def finish_rows_kernel(ends, late_count, own_ref, far_ref, *refs):
     *back_refs, dq_ref = refs
+    late_refs, back_refs = back_refs[:late_count], back_refs[late_count:]
     share, heads, width = dq_ref.shape
+    kv_heads = own_ref.shape[0]
+    near = [g for g in range(kv_heads) if g not in ends]
     outs = []
     for g in range(kv_heads):
-        dq = own_ref[g]
-        for ref in back_refs[kv_heads - 1 - g :: kv_heads]:
-            dq = dq + ref[...].astype(jnp.float32)
+        if g in ends:
+            late = own_ref[g, own_ref.shape[1] // 2 :]
+            for ref in late_refs[ends.index(g) :: len(ends)]:
+                late = late + ref[...].astype(jnp.float32)
+            dq = jnp.concatenate([far_ref[ends.index(g)], late], axis=0)
+        else:
+            dq = own_ref[g]
+            for ref in back_refs[near.index(g) :: len(near)]:
+                dq = dq + ref[...].astype(jnp.float32)
         outs.append(dq.reshape(share, heads // kv_heads, width))
     dq_ref[...] = jnp.concatenate(outs, axis=1).astype(jnp.bfloat16)
 
 
 def finish_keys_kernel(*refs):
-    *keep_refs, z_a, z_b, dk_ref, dv_ref = refs
+    *refs, dk_ref, dv_ref = refs
+    kv_heads = dk_ref.shape[1]
+    keep_refs, z_refs = refs[:-kv_heads], refs[-kv_heads:]
     total = keep_refs[0][...].astype(jnp.float32)
     for ref in keep_refs[1:]:
         total = total + ref[...].astype(jnp.float32)
-    total = total + jnp.concatenate([z_a[...], z_b[...]], axis=0).astype(jnp.float32)
+    total = total + jnp.concatenate([ref[...] for ref in z_refs], axis=0).astype(jnp.float32)
     for j, ref in enumerate((dk_ref, dv_ref)):
         grads = jnp.stack([total[2 * g + j] for g in range(ref.shape[1])], axis=1)
         ref[...] = grads.astype(jnp.bfloat16)
@@ -264,49 +300,87 @@
 
     part = shape((2 * kv_heads, key_count, width), jnp.bfloat16)
     sent = shape((key_devices // 2 - 1, cols, width), jnp.bfloat16)
-    *sends, own_dq, cross, keep = pl.pallas_call(
-        functools.partial(
-            rows_kernel, key_devices, share, head_count, partners, row_sets
-        ),
-        out_shape=(sent,) * kv_heads + (shape((kv_heads, cols, width), jnp.float32), part, part),
-        in_specs=[VMEM] * (2 + 2 * kv_heads + len(others)),
-        out_specs=(VMEM,) * (kv_heads + 3),
-        compiler_params=params,
-        name="rows",
-    )(rows_q, rows_do, *messages, *got, *others)
+    half_sent = shape((key_devices // 2 - 1, cols // 2, width), jnp.bfloat16)
+    near = [g for g in range(kv_heads) if partners[g] == partners[0]]
+    ends = [g for g in range(kv_heads) if partners[g] != partners[0]]
+    inputs = (rows_q, rows_do, *messages, *got, *others)
+
+    def rows(tasks, first, *extra, out_shape):
+        return pl.pallas_call(
+            functools.partial(
+                rows_kernel, key_devices, share, head_count, partners, row_sets, tasks, first
+            ),
+            out_shape=out_shape,
+            in_specs=[VMEM] * (len(inputs) + len(extra)),
+            out_specs=(VMEM,) * len(out_shape),
+            compiler_params=params,
+            name="far_rows" if first else "near_rows",
+        )(*inputs, *extra)
+
+    acc, *far_sends = rows(
+        [[m for m in row_sets[g] if m] if g in ends else [] for g in range(kv_heads)],
+        True,
+        out_shape=(shape((2 * len(ends), 2 * key_count, width), jnp.float32),)
+        + (half_sent,) * (2 * len(ends)),
+    )
+    one = shape((2, key_count, width), jnp.bfloat16)
+    results = rows(
+        [[0] if g in ends else row_sets[g] for g in range(kv_heads)],
+        False,
+        acc,
+        out_shape=(sent,) * len(near)
+        + (shape((kv_heads, cols, width), jnp.float32), part)
+        + (one,) * kv_heads,
+    )
+    near_sends, crosses = results[: len(near)], results[len(near) + 2 :]
+    own_dq, keep = results[len(near) : len(near) + 2]
+
+    def send_back(sends, heads):
+        return [
+            swap(send[at], [m for m in row_sets[g] if m][at])
+            for at in range(key_devices // 2 - 1)
+            for send, g in zip(sends, heads)
+        ]
+
+    far_back = send_back(far_sends[0::2], ends)
+    far_late = send_back(far_sends[1::2], ends)
+    near_back = send_back(near_sends, near)
 
     def over_queries(x):
         if query_devices == 2:
             return [x, lax.ppermute(x, "pb", [(0, 1), (1, 0)])]
         return [lax.psum(x.astype(jnp.float32), "pb")]
 
-    crossed = over_queries(cross)
-    back = []
-    for at in range(key_devices // 2 - 1):
-        for g in reversed(range(kv_heads)):
-            back.append(swap(sends[g][at], [m for m in row_sets[g] if m][at]))
+    far_dq = pl.pallas_call(
+        functools.partial(far_rows_kernel, ends),
+        out_shape=shape((len(ends), cols // 2, width), jnp.float32),
+        in_specs=[VMEM] * (1 + len(far_back)),
+        out_specs=VMEM,
+        compiler_params=params,
+        cost_estimate=pl.CostEstimate(flops=10**10, bytes_accessed=2**20, transcendentals=0),
+        name="far_dq",
+    )(own_dq, *far_back)
+    z = []
+    for cross, partner in zip(crosses, partners):
+        crossed = over_queries(cross)
+        summed = pl.pallas_call(
+            across_kernel,
+            out_shape=one,
+            in_specs=[pl.BlockSpec(memory_space=pl.ANY)] + [VMEM] * len(crossed),
+            out_specs=VMEM,
+            compiler_params=params,
+            name="across",
+        )(far_dq, *crossed)
+        z.append(swap(summed, partner))
     kept = over_queries(keep)
-    half = shape((kv_heads, key_count, width), jnp.bfloat16)
-    z_a, z_b = pl.pallas_call(
-        across_kernel,
-        out_shape=(half, half),
-        in_specs=[VMEM] * len(crossed),
-        out_specs=(VMEM, VMEM),
-        compiler_params=params,
-        cost_estimate=pl.CostEstimate(
-            flops=10**10, bytes_accessed=2**20, transcendentals=0
-        ),
-        name="across",
-    )(*crossed)
-    z = [swap(z_a, partners[0]), swap(z_b, partners[-1])]
     dq = pl.pallas_call(
-        functools.partial(finish_rows_kernel, kv_heads),
+        functools.partial(finish_rows_kernel, ends, len(far_late)),
         out_shape=shape((share, head_count, width), jnp.bfloat16),
-        in_specs=[VMEM] * (1 + len(back)),
+        in_specs=[VMEM] * (2 + len(far_late) + len(near_back)),
         out_specs=VMEM,
         compiler_params=params,
         name="finish_rows",
-    )(own_dq, *back)
+    )(own_dq, far_dq, *far_late, *near_back)
     dk, dv = pl.pallas_call(
         finish_keys_kernel,
         out_shape=(

time: 34 us -> 33.8 us (level)
  waiting for transfers between devices: 9.74 us -> 7.89 us
  starting transfers between devices: 14.8 us -> 15.9 us
  Pallas kernels: 8.63 us -> 9.08 us
    ppermute x2 -> x3, starting transfers between devices: 2.09 us -> 3.59 us  [over_queries(): return [x, lax.ppermute(x, 'pb', [(0, 1), (1, 0)])]]
    ppermute x2 -> x3, waiting for transfers between devices: 1.32 us -> 0.15 us  [over_queries(): return [x, lax.ppermute(x, 'pb', [(0, 1), (1, 0)])]]
    ppermute x7 -> x8, waiting for transfers between devices: 8.43 us -> 7.74 us  [swap(): return lax.ppermute(x, 'ka', [(i, i ^ by) for i in range(key_devices)])]
    pallas_call x3 -> x6, Pallas kernels: 4.5 us -> 4.95 us  [the longest x2 4.05 us: rows(): pl.pallas_call(functools.partial(rows_kernel, key_devices, share, head_co...]
    ppermute x7 -> x8, starting transfers between devices: 12.7 us -> 12.3 us  [swap(): return lax.ppermute(x, 'ka', [(i, i ^ by) for i in range(key_devices)])]
  transfers between devices with their start and end apart: 9 -> 11, of which waited for: 5 -> 4; matrix products, arithmetic and copies ran while one was open for 0% -> 0% of each run, Pallas kernels for 8% -> 16%
where the time goes in v4:
time: 33.8 us; the launch traced here: 33.6 us
  starting transfers between devices  15.9 us (47%)
  Pallas kernels  9.08 us (27%)
  waiting for transfers between devices  7.89 us (23%)
  between operations  0.68 us (2%)
    ppermute x8, starting transfers between devices, swap(): return lax.ppermute(x, 'ka', [(i, i ^ by) for i in range(key_devices)])  12.3 us
    ppermute x8, waiting for transfers between devices, swap(): return lax.ppermute(x, 'ka', [(i, i ^ by) for i in range(key_devices)])  7.74 us
    pallas_call x2, Pallas kernels, rows(): pl.pallas_call(functools.partial(rows_kernel, key_devices, share, head_co...  4.05 us
    ppermute x3, starting transfers between devices, over_queries(): return [x, lax.ppermute(x, 'pb', [(0, 1), (1, 0)])]  3.59 us
    pallas_call x1, Pallas kernels, per_device(): pl.pallas_call(functools.partial(gather_kernel, row_sets, share), out_sha...  1.76 us
    pallas_call x1, Pallas kernels, per_device(): pl.pallas_call(prep_kernel, out_shape=(shape((2 * key_count + SUM_ROWS, w...  1.34 us
    pallas_call x1, Pallas kernels, per_device(): pl.pallas_call(finish_keys_kernel, out_shape=(shape(key_codes.shape, jnp....  1.03 us
    pallas_call x1, Pallas kernels, per_device(): pl.pallas_call(functools.partial(finish_rows_kernel, ends, len(far_late))...  0.83 us
  transfers between devices with their start and end apart: 11, of which 4 were waited for; matrix products, arithmetic and copies ran while one was open for 0% of the time, Pallas kernels for 16%

profile of v4, /device:TPU:0, one launch (start us, length us, event | category | flops | bytes accessed | tf_op | source)
XLA Modules:
  0.0 33.6 jit_solution(5274153274150231703)
XLA Ops:
  0.6 1.3 %prep.1 = (bf16[400,128]{1,0:T(8,128)(2,1)S(1)}, bf16[400,128]{1,0:T(8,128)(2,1)S(1)}, f32[16,128]{1,0:T(8,128)S(1)}) custom-call(s32[2,3]{1,0:T(2,128)} %bitcast.11, bf16[192,2,128]{2,1,0:T(2,128)(2,1)} %codes_hbm.1, bf16[192,2,128]{2,1,0:T(2,128)(2,1)} %values_hbm.1), custom_call_target="tpu_custom_call" | custom-call | tf_op jit(solution)/shard_map/prep/pallas_call | solution.py:265
  2.0 4.1 %collective-permute-start = (bf16[400,128]{1,0:T(8,128)(2,1)S(1)}, bf16[400,128]{1,0:T(8,128)(2,1)S(1)}, u32[]{:S(2)}, u32[]{:S(2)}) collective-permute-start(bf16[400,128]{1,0:T(8,128)(2,1)S(1)} %get-tuple-element.20.refs_2_), channel_id=1, source_target_pairs={{0,8},{4,12},{8,0},{12,4},{1,9},{5,13},{9,1},{13,5},{2,10},{6,14},... | collective-permute-start | bytes 307208 | tf_op jit(solution)/shard_map/ppermute | solution.py:260
  6.1 1.6 %collective-permute-start.1 = (bf16[400,128]{1,0:T(8,128)(2,1)S(1)}, bf16[400,128]{1,0:T(8,128)(2,1)S(1)}, u32[]{:S(2)}, u32[]{:S(2)}) collective-permute-start(bf16[400,128]{1,0:T(8,128)(2,1)S(1)} %get-tuple-element.21.refs_3_), channel_id=1, source_target_pairs={{0,4},{4,0},{8,12},{12,8},{1,5},{5,1},{9,13},{13,9},{2,6},{6,2},{1... | collective-permute-start | bytes 307208 | tf_op jit(solution)/shard_map/ppermute | solution.py:260
  7.7 0.0 collective-permute-start.2
  7.7 1.8 %gather.1 = (bf16[2,2,768,256]{3,2,1,0:T(8,128)(2,1)S(1)}, bf16[2,2,768,256]{3,2,1,0:T(8,128)(2,1)S(1)}) custom-call(bf16[384,16,128]{2,1,0:T(8,128)(2,1)} %q_hbm.1, bf16[384,16,128]{2,1,0:T(8,128)(2,1)} %do_hbm.1, f32[16,384]{1,0:T(8,128)} %bitcast.9, f32[16,384]{1,0:T(8,128)} %bitcast.10), custom_call_target="tpu_custom_call" | custom-call | tf_op jit(solution)/shard_map/gather/pallas_call | solution.py:285
  9.4 3.7 %collective-permute-done.2.refs_6_ = f32[16,128]{1,0:T(8,128)S(1)} collective-permute-done((f32[16,128]{1,0:T(8,128)S(1)}, f32[16,128]{1,0:T(8,128)S(1)}, u32[]{:S(2)}, u32[]{:S(2)}) %collective-permute-start.2) | collective-permute-done | bytes 8224 | tf_op jit(solution)/shard_map/ppermute | solution.py:260
  13.1 0.0 collective-permute-done.1.refs_5_
  13.1 1.2 %far_rows.1 = (f32[2,384,128]{2,1,0:T(8,128)S(1)}, bf16[1,384,128]{2,1,0:T(8,128)(2,1)S(1)}, bf16[1,384,128]{2,1,0:T(8,128)(2,1)S(1)}) custom-call(bf16[2,2,768,256]{3,2,1,0:T(8,128)(2,1)S(1)} %get-tuple-element.18.refs_0_, bf16[2,2,768,256]{3,2,1,0:T(8,128)(2,1)S(1)} %get-tuple-element.19.refs_1_, bf16[400,128]{1,0:T(8,128)(2,1)S(1)} %get-tuple-element.20.refs_2_, ...), custom_call_target="tpu_custom_call" | custom-call | tf_op jit(solution)/shard_map/far_rows/pallas_call | solution.py:309
  14.3 1.1 %collective-permute-start.3 = (bf16[384,128]{1,0:T(8,128)(2,1)S(1)}, bf16[384,128]{1,0:T(8,128)(2,1)S(1)}, u32[]{:S(2)}, u32[]{:S(2)}) collective-permute-start(bf16[384,128]{1,0:T(8,128)(2,1)S(1)} %bitcast.8), channel_id=1, source_target_pairs={{0,8},{4,12},{8,0},{12,4},{1,9},{5,13},{9,1},{13,5},{2,10},{6,14},... | collective-permute-start | bytes 294920 | tf_op jit(solution)/shard_map/ppermute | solution.py:260
  15.4 2.9 %near_rows.1 = (bf16[1,768,128]{2,1,0:T(8,128)(2,1)S(1)}, f32[2,768,128]{2,1,0:T(8,128)S(1)}, bf16[4,192,128]{2,1,0:T(8,128)(2,1)S(1)}, bf16[2,192,128]{2,1,0:T(8,128)(2,1)S(1)}, bf16[2,192,128]{2,1,0:T(8,128)(2,1)S(1)}) custom-call(bf16[2,2,768,256]{3,2,1,0:T(8,128)(2,1)S(1)} %get-tuple-element.18.refs_0_, ...), custom_call_target="tpu_custom_call" | custom-call | tf_op jit(solution)/shard_map/near_rows/pallas_call | solution.py:309
  18.3 1.6 %collective-permute-start.7 = (bf16[2,192,128]{2,1,0:T(8,128)(2,1)S(1)}, bf16[2,192,128]{2,1,0:T(8,128)(2,1)S(1)}, u32[]{:S(2)}, u32[]{:S(2)}) collective-permute-start(bf16[2,192,128]{2,1,0:T(8,128)(2,1)S(1)} %get-tuple-element.29.refs_0_), channel_id=1, source_target_pairs={{0,16},{16,0},{1,17},{17,1},{2,18},{18,2},{3,19},{19,3},{4,20},{20... | collective-permute-start | bytes 294920 | tf_op jit(solution)/shard_map/ppermute | solution.py:351
  19.8 0.5 %collective-permute-start.9 = (bf16[2,192,128]{2,1,0:T(8,128)(2,1)S(1)}, bf16[2,192,128]{2,1,0:T(8,128)(2,1)S(1)}, u32[]{:S(2)}, u32[]{:S(2)}) collective-permute-start(bf16[2,192,128]{2,1,0:T(8,128)(2,1)S(1)} %get-tuple-element.30.refs_0_), channel_id=1, source_target_pairs={{0,16},{16,0},{1,17},{17,1},{2,18},{18,2},{3,19},{19,3},{4,20},{20... | collective-permute-start | bytes 294920 | tf_op jit(solution)/shard_map/ppermute | solution.py:351
  20.4 1.9 %collective-permute-start.4 = (bf16[384,128]{1,0:T(8,128)(2,1)S(1)}, bf16[384,128]{1,0:T(8,128)(2,1)S(1)}, u32[]{:S(2)}, u32[]{:S(2)}) collective-permute-start(bf16[384,128]{1,0:T(8,128)(2,1)S(1)} %bitcast.7), channel_id=1, source_target_pairs={{0,8},{4,12},{8,0},{12,4},{1,9},{5,13},{9,1},{13,5},{2,10},{6,14},... | collective-permute-start | bytes 294920 | tf_op jit(solution)/shard_map/ppermute | solution.py:260
  22.3 0.0 collective-permute-start.5
  22.3 0.0 collective-permute-done.3.refs_0_
  22.3 1.5 %collective-permute-start.6 = (bf16[4,192,128]{2,1,0:T(8,128)(2,1)S(1)}, bf16[4,192,128]{2,1,0:T(8,128)(2,1)S(1)}, u32[]{:S(2)}, u32[]{:S(2)}) collective-permute-start(bf16[4,192,128]{2,1,0:T(8,128)(2,1)S(1)} %get-tuple-element.28.refs_0_), channel_id=1, source_target_pairs={{0,16},{16,0},{1,17},{17,1},{2,18},{18,2},{3,19},{19,3},{4,20},{20... | collective-permute-start | bytes 589832 | tf_op jit(solution)/shard_map/ppermute | solution.py:351
  23.8 0.1 collective-permute-done.7.refs_1_
  24.0 2.4 %collective-permute-start.8 = (bf16[2,192,128]{2,1,0:T(8,128)(2,1)S(1)}, bf16[2,192,128]{2,1,0:T(8,128)(2,1)S(1)}, u32[]{:S(2)}, u32[]{:S(2)}) collective-permute-start(bf16[2,192,128]{2,1,0:T(8,128)(2,1)S(1)} %across.2), channel_id=1, source_target_pairs={{0,8},{4,12},{8,0},{12,4},{1,9},{5,13},{9,1},{13,5},{2,10},{6,14},... | collective-permute-start | bytes 294920 | tf_op jit(solution)/shard_map/ppermute | solution.py:260
  26.4 1.3 %collective-permute-start.10 = (bf16[2,192,128]{2,1,0:T(8,128)(2,1)S(1)}, bf16[2,192,128]{2,1,0:T(8,128)(2,1)S(1)}, u32[]{:S(2)}, u32[]{:S(2)}) collective-permute-start(bf16[2,192,128]{2,1,0:T(8,128)(2,1)S(1)} %across.3), channel_id=1, source_target_pairs={{0,4},{4,0},{8,12},{12,8},{1,5},{5,1},{9,13},{13,9},{2,6},{6,2},{1... | collective-permute-start | bytes 294920 | tf_op jit(solution)/shard_map/ppermute | solution.py:260
  27.6 0.0 collective-permute-done.4.refs_0_
  27.7 3.8 %collective-permute-done.5.refs_1_ = bf16[768,128]{1,0:T(8,128)(2,1)S(1)} collective-permute-done((bf16[768,128]{1,0:T(8,128)(2,1)S(1)}, bf16[768,128]{1,0:T(8,128)(2,1)S(1)}, u32[]{:S(2)}, u32[]{:S(2)}) %collective-permute-start.5) | collective-permute-done | bytes 196640 | tf_op jit(solution)/shard_map/ppermute | solution.py:260
  31.5 0.8 %finish_rows.1 = bf16[96,16,128]{2,1,0:T(8,128)(2,1)} custom-call(f32[2,768,128]{2,1,0:T(8,128)S(1)} %get-tuple-element.24.own_ref, f32[1,384,128]{2,1,0:T(8,128)S(1)} %far_dq.1.far_ref.after_ref, bf16[384,128]{1,0:T(8,128)(2,1)S(1)} %collective-permute-done.4.refs_0_, bf16[768,128]{1,0:T(8,128)(2,1)S(1)} %collective-permute-done.5.refs_1_), custom_call_target="tpu_custom_call" | custom-call | tf_op jit(solution)/shard_map/finish_rows/pallas_call | solution.py:376
  32.3 0.2 collective-permute-done.10.refs_3_
  32.6 1.0 %finish_keys.1 = (bf16[192,2,128]{2,1,0:T(2,128)(2,1)}, bf16[192,2,128]{2,1,0:T(2,128)(2,1)}) custom-call(bf16[4,192,128]{2,1,0:T(8,128)(2,1)S(1)} %get-tuple-element.28.refs_0_, bf16[4,192,128]{2,1,0:T(8,128)(2,1)S(1)} %collective-permute-done.6.refs_1_, bf16[2,192,128]{2,1,0:T(8,128)(2,1)S(1)} %collective-permute-done.8.refs_2_, ...), custom_call_target="tpu_custom_call" | custom-call | tf_op jit(solution)/shard_map/finish_keys/pallas_call | solution.py:384
  (7 shorter events, 0.1 us)
Async XLA Ops:
  2.0 11.1 %collective-permute-start = (bf16[400,128]{1,0:T(8,128)(2,1)S(1)}, bf16[400,128]{1,0:T(8,128)(2,1)S(1)}, u32[]{:S(2)}, u32[]{:S(2)}) collective-permute-start(bf16[400,128]{1,0:T(8,128)(2,1)S(1)} %get-tuple-element.20.refs_2_), channel_id=1, source_target_pairs={{0,8},{4,12},{8,0},{12,4},{1,9},{5,13},{9,1},{13,5},{2,10},{6,14},... | collective-permute-start | bytes 307208 | tf_op jit(solution)/shard_map/ppermute | solution.py:260
  6.1 7.0 %collective-permute-start.1 = (bf16[400,128]{1,0:T(8,128)(2,1)S(1)}, bf16[400,128]{1,0:T(8,128)(2,1)S(1)}, u32[]{:S(2)}, u32[]{:S(2)}) collective-permute-start(bf16[400,128]{1,0:T(8,128)(2,1)S(1)} %get-tuple-element.21.refs_3_), channel_id=1, source_target_pairs={{0,4},{4,0},{8,12},{12,8},{1,5},{5,1},{9,13},{13,9},{2,6},{6,2},{1... | collective-permute-start | bytes 307208 | tf_op jit(solution)/shard_map/ppermute | solution.py:260
  7.7 5.4 %collective-permute-start.2 = (f32[16,128]{1,0:T(8,128)S(1)}, f32[16,128]{1,0:T(8,128)S(1)}, u32[]{:S(2)}, u32[]{:S(2)}) collective-permute-start(f32[16,128]{1,0:T(8,128)S(1)} %get-tuple-element.22), channel_id=1, source_target_pairs={{0,12},{4,8},{8,4},{12,0},{1,13},{5,9},{9,5},{13,1},{2,14},{6,10},... | collective-permute-start | bytes 24584 | tf_op jit(solution)/shard_map/ppermute | solution.py:260
  14.3 8.0 %collective-permute-start.3 = (bf16[384,128]{1,0:T(8,128)(2,1)S(1)}, bf16[384,128]{1,0:T(8,128)(2,1)S(1)}, u32[]{:S(2)}, u32[]{:S(2)}) collective-permute-start(bf16[384,128]{1,0:T(8,128)(2,1)S(1)} %bitcast.8), channel_id=1, source_target_pairs={{0,8},{4,12},{8,0},{12,4},{1,9},{5,13},{9,1},{13,5},{2,10},{6,14},... | collective-permute-start | bytes 294920 | tf_op jit(solution)/shard_map/ppermute | solution.py:260
  18.3 5.6 %collective-permute-start.7 = (bf16[2,192,128]{2,1,0:T(8,128)(2,1)S(1)}, bf16[2,192,128]{2,1,0:T(8,128)(2,1)S(1)}, u32[]{:S(2)}, u32[]{:S(2)}) collective-permute-start(bf16[2,192,128]{2,1,0:T(8,128)(2,1)S(1)} %get-tuple-element.29.refs_0_), channel_id=1, source_target_pairs={{0,16},{16,0},{1,17},{17,1},{2,18},{18,2},{3,19},{19,3},{4,20},{20... | collective-permute-start | bytes 294920 | tf_op jit(solution)/shard_map/ppermute | solution.py:351
  19.8 6.5 %collective-permute-start.9 = (bf16[2,192,128]{2,1,0:T(8,128)(2,1)S(1)}, bf16[2,192,128]{2,1,0:T(8,128)(2,1)S(1)}, u32[]{:S(2)}, u32[]{:S(2)}) collective-permute-start(bf16[2,192,128]{2,1,0:T(8,128)(2,1)S(1)} %get-tuple-element.30.refs_0_), channel_id=1, source_target_pairs={{0,16},{16,0},{1,17},{17,1},{2,18},{18,2},{3,19},{19,3},{4,20},{20... | collective-permute-start | bytes 294920 | tf_op jit(solution)/shard_map/ppermute | solution.py:351
  20.4 7.3 %collective-permute-start.4 = (bf16[384,128]{1,0:T(8,128)(2,1)S(1)}, bf16[384,128]{1,0:T(8,128)(2,1)S(1)}, u32[]{:S(2)}, u32[]{:S(2)}) collective-permute-start(bf16[384,128]{1,0:T(8,128)(2,1)S(1)} %bitcast.7), channel_id=1, source_target_pairs={{0,8},{4,12},{8,0},{12,4},{1,9},{5,13},{9,1},{13,5},{2,10},{6,14},... | collective-permute-start | bytes 294920 | tf_op jit(solution)/shard_map/ppermute | solution.py:260
  22.3 9.2 %collective-permute-start.5 = (bf16[768,128]{1,0:T(8,128)(2,1)S(1)}, bf16[768,128]{1,0:T(8,128)(2,1)S(1)}, u32[]{:S(2)}, u32[]{:S(2)}) collective-permute-start(bf16[768,128]{1,0:T(8,128)(2,1)S(1)} %bitcast.6), channel_id=1, source_target_pairs={{0,4},{4,0},{8,12},{12,8},{1,5},{5,1},{9,13},{13,9},{2,6},{6,2},{1... | collective-permute-start | bytes 589832 | tf_op jit(solution)/shard_map/ppermute | solution.py:260
  22.3 10.3 %collective-permute-start.6 = (bf16[4,192,128]{2,1,0:T(8,128)(2,1)S(1)}, bf16[4,192,128]{2,1,0:T(8,128)(2,1)S(1)}, u32[]{:S(2)}, u32[]{:S(2)}) collective-permute-start(bf16[4,192,128]{2,1,0:T(8,128)(2,1)S(1)} %get-tuple-element.28.refs_0_), channel_id=1, source_target_pairs={{0,16},{16,0},{1,17},{17,1},{2,18},{18,2},{3,19},{19,3},{4,20},{20... | collective-permute-start | bytes 589832 | tf_op jit(solution)/shard_map/ppermute | solution.py:351
  24.0 8.4 %collective-permute-start.8 = (bf16[2,192,128]{2,1,0:T(8,128)(2,1)S(1)}, bf16[2,192,128]{2,1,0:T(8,128)(2,1)S(1)}, u32[]{:S(2)}, u32[]{:S(2)}) collective-permute-start(bf16[2,192,128]{2,1,0:T(8,128)(2,1)S(1)} %across.2), channel_id=1, source_target_pairs={{0,8},{4,12},{8,0},{12,4},{1,9},{5,13},{9,1},{13,5},{2,10},{6,14},... | collective-permute-start | bytes 294920 | tf_op jit(solution)/shard_map/ppermute | solution.py:260
  26.4 6.2 %collective-permute-start.10 = (bf16[2,192,128]{2,1,0:T(8,128)(2,1)S(1)}, bf16[2,192,128]{2,1,0:T(8,128)(2,1)S(1)}, u32[]{:S(2)}, u32[]{:S(2)}) collective-permute-start(bf16[2,192,128]{2,1,0:T(8,128)(2,1)S(1)} %across.3), channel_id=1, source_target_pairs={{0,4},{4,0},{8,12},{12,8},{1,5},{5,1},{9,13},{13,9},{2,6},{6,2},{1... | collective-permute-start | bytes 294920 | tf_op jit(solution)/shard_map/ppermute | solution.py:260

commit v5 on v4

--- a/solution.py
+++ b/solution.py
@@ -115,19 +115,15 @@
 def rows_kernel(key_devices, share, heads, partners, row_sets, tasks, first, *refs):
     kv_heads = len(partners)
     busy = [g for g in range(kv_heads) if tasks[g]]
-    pieces = 2 if first else 1
+    pieces = 1
     sending = [g for g in busy if any(tasks[g]) for _ in range(pieces)]
     ends = [g for g in range(kv_heads) if partners[g] != partners[0]]
     q_ref, do_ref, *refs = refs
     own_refs, got_refs, refs = refs[:kv_heads], refs[kv_heads : 2 * kv_heads], refs[2 * kv_heads :]
-    if first:
-        *sum_refs, acc_ref = refs[: -len(sending)]
-        send_refs = list(zip(sending, refs[-len(sending) :]))
-    else:
-        dq_ref, keep_ref = refs[-2 - kv_heads : -kv_heads]
-        cross_refs, refs = refs[-kv_heads:], refs[: -2 - kv_heads]
-        send_refs = list(zip(sending, refs[-len(sending) :]))
-        *sum_refs, acc_ref = refs[: -len(sending)]
+    dq_ref, keep_ref = refs[-2 - kv_heads : -kv_heads]
+    cross_refs, refs = refs[-kv_heads:], refs[: -2 - kv_heads]
+    send_refs = list(zip(sending, refs[-len(sending) :]))
+    sum_refs = refs[: -len(sending)]
     ka, pb = lax.axis_index("ka"), lax.axis_index("pb")
     cols, width = q_ref.shape[2], q_ref.shape[3] // 2
     key_count = (own_refs[0].shape[0] - SUM_ROWS) // 2
@@ -158,8 +154,6 @@
         base = jnp.where(line < key_count, ka * key_count, ((ka ^ partners[g]) - 1) * key_count)
         lead = line + base - step
         dk = dv = None
-        if not first and g in ends:
-            dk, dv = acc_ref[2 * ends.index(g)], acc_ref[2 * ends.index(g) + 1]
         for m in tasks[g]:
             at = row_sets[g].index(m)
             q, do = q_ref[g, at], do_ref[g, at]
@@ -182,63 +176,35 @@
                 for j, ref in enumerate(ref for to, ref in send_refs if to == g):
                     piece = dq[j * cols // pieces : (j + 1) * cols // pieces]
                     ref[others.index(m)] = piece.astype(jnp.bfloat16)
-        if first:
-            acc_ref[2 * ends.index(g)] = dk
-            acc_ref[2 * ends.index(g) + 1] = dv
-        else:
-            for j, grad in enumerate((dk * root, dv)):
-                keep_ref[2 * g + j] = grad[:key_count].astype(jnp.bfloat16)
-                cross_refs[g][j] = grad[key_count:].astype(jnp.bfloat16)
-
-
-def across_kernel(after_ref, *refs):
-    *in_refs, out_ref = refs
-    total = in_refs[0][...].astype(jnp.float32)
-    for ref in in_refs[1:]:
-        total = total + ref[...].astype(jnp.float32)
-    out_ref[...] = total.astype(jnp.bfloat16)
-
-
-def far_rows_kernel(ends, own_ref, *refs):
-    *back_refs, sum_ref = refs
-    for j, g in enumerate(ends):
-        dq = own_ref[g, : own_ref.shape[1] // 2]
-        for ref in back_refs[j :: len(ends)]:
-            dq = dq + ref[...].astype(jnp.float32)
-        sum_ref[j] = dq
-
-
-def finish_rows_kernel(ends, late_count, own_ref, far_ref, *refs):
-    *back_refs, dq_ref = refs
-    late_refs, back_refs = back_refs[:late_count], back_refs[late_count:]
+        for j, grad in enumerate((dk * root, dv)):
+            keep_ref[2 * g + j] = grad[:key_count]
+            cross_refs[g][j] = grad[key_count:].astype(jnp.bfloat16)
+
+
+def join_kernel(keep_ref, *refs):
+    *got_refs, out_ref = refs
+    for g, ref in enumerate(got_refs):
+        total = keep_ref[2 * g : 2 * g + 2] + ref[...].astype(jnp.float32)
+        out_ref[2 * g : 2 * g + 2] = total.astype(jnp.bfloat16)
+
+
+def finish_kernel(kept_count, own_ref, *refs):
+    *refs, dq_ref, dk_ref, dv_ref = refs
+    kept_refs, back_refs = refs[:kept_count], refs[kept_count:]
     share, heads, width = dq_ref.shape
     kv_heads = own_ref.shape[0]
-    near = [g for g in range(kv_heads) if g not in ends]
     outs = []
     for g in range(kv_heads):
-        if g in ends:
-            late = own_ref[g, own_ref.shape[1] // 2 :]
-            for ref in late_refs[ends.index(g) :: len(ends)]:
-                late = late + ref[...].astype(jnp.float32)
-            dq = jnp.concatenate([far_ref[ends.index(g)], late], axis=0)
-        else:
-            dq = own_ref[g]
-            for ref in back_refs[near.index(g) :: len(near)]:
-                dq = dq + ref[...].astype(jnp.float32)
+        dq = own_ref[g]
+        for ref in back_refs[kv_heads - 1 - g :: kv_heads]:
+            dq = dq + ref[...].astype(jnp.float32)
         outs.append(dq.reshape(share, heads // kv_heads, width))
     dq_ref[...] = jnp.concatenate(outs, axis=1).astype(jnp.bfloat16)
-
-
-def finish_keys_kernel(*refs):
-    *refs, dk_ref, dv_ref = refs
-    kv_heads = dk_ref.shape[1]
-    keep_refs, z_refs = refs[:-kv_heads], refs[-kv_heads:]
-    total = keep_refs[0][...].astype(jnp.float32)
-    for ref in keep_refs[1:]:
+    total = kept_refs[0][...].astype(jnp.float32)
+    for ref in kept_refs[1:]:
         total = total + ref[...].astype(jnp.float32)
-    total = total + jnp.concatenate([ref[...] for ref in z_refs], axis=0).astype(jnp.float32)
     for j, ref in enumerate((dk_ref, dv_ref)):
-        grads = jnp.stack([total[2 * g + j] for g in range(ref.shape[1])], axis=1)
+        grads = jnp.stack([total[2 * g + j] for g in range(kv_heads)], axis=1)
         ref[...] = grads.astype(jnp.bfloat16)
 
 
@@ -252,7 +218,7 @@
     cols = share * group
     params = pltpu.CompilerParams(vmem_limit_bytes=24 * 2**20)
     top = key_devices // 2
-    partners = [top if g < kv_heads // 2 else 1 for g in range(kv_heads)]
+    partners = [1 if g < kv_heads // 2 else top for g in range(kv_heads)]
     row_sets = [[m for m in range(key_devices) if not m & p] for p in partners]
     shape = jax.ShapeDtypeStruct
 
@@ -299,8 +265,9 @@
     )(pinned(queries), pinned(grad_out), pinned(log_totals.T), pinned(grad_dot.T))
 
     part = shape((2 * kv_heads, key_count, width), jnp.bfloat16)
+    whole_part = shape((2 * kv_heads, key_count, width), jnp.float32)
+    one = shape((2, key_count, width), jnp.bfloat16)
     sent = shape((key_devices // 2 - 1, cols, width), jnp.bfloat16)
-    half_sent = shape((key_devices // 2 - 1, cols // 2, width), jnp.bfloat16)
     near = [g for g in range(kv_heads) if partners[g] == partners[0]]
     ends = [g for g in range(kv_heads) if partners[g] != partners[0]]
     inputs = (rows_q, rows_do, *messages, *got, *others)
@@ -317,23 +284,15 @@
             name="far_rows" if first else "near_rows",
         )(*inputs, *extra)
 
-    acc, *far_sends = rows(
-        [[m for m in row_sets[g] if m] if g in ends else [] for g in range(kv_heads)],
-        True,
-        out_shape=(shape((2 * len(ends), 2 * key_count, width), jnp.float32),)
-        + (half_sent,) * (2 * len(ends)),
-    )
-    one = shape((2, key_count, width), jnp.bfloat16)
     results = rows(
-        [[0] if g in ends else row_sets[g] for g in range(kv_heads)],
+        row_sets,
         False,
-        acc,
-        out_shape=(sent,) * len(near)
-        + (shape((kv_heads, cols, width), jnp.float32), part)
+        out_shape=(sent,) * kv_heads
+        + (shape((kv_heads, cols, width), jnp.float32), whole_part)
         + (one,) * kv_heads,
     )
-    near_sends, crosses = results[: len(near)], results[len(near) + 2 :]
-    own_dq, keep = results[len(near) : len(near) + 2]
+    sends, crosses = results[:kv_heads], results[kv_heads + 2 :]
+    own_dq, keep = results[kv_heads : kv_heads + 2]
 
     def send_back(sends, heads):
         return [
@@ -342,57 +301,36 @@
             for send, g in zip(sends, heads)
         ]
 
-    far_back = send_back(far_sends[0::2], ends)
-    far_late = send_back(far_sends[1::2], ends)
-    near_back = send_back(near_sends, near)
+    back = send_back(sends[::-1], list(range(kv_heads))[::-1])
 
     def over_queries(x):
         if query_devices == 2:
             return [x, lax.ppermute(x, "pb", [(0, 1), (1, 0)])]
         return [lax.psum(x.astype(jnp.float32), "pb")]
 
-    far_dq = pl.pallas_call(
-        functools.partial(far_rows_kernel, ends),
-        out_shape=shape((len(ends), cols // 2, width), jnp.float32),
-        in_specs=[VMEM] * (1 + len(far_back)),
+    mine = pl.pallas_call(
+        join_kernel,
+        out_shape=part,
+        in_specs=[VMEM] * (1 + kv_heads),
         out_specs=VMEM,
         compiler_params=params,
         cost_estimate=pl.CostEstimate(flops=10**10, bytes_accessed=2**20, transcendentals=0),
-        name="far_dq",
-    )(own_dq, *far_back)
-    z = []
-    for cross, partner in zip(crosses, partners):
-        crossed = over_queries(cross)
-        summed = pl.pallas_call(
-            across_kernel,
-            out_shape=one,
-            in_specs=[pl.BlockSpec(memory_space=pl.ANY)] + [VMEM] * len(crossed),
-            out_specs=VMEM,
-            compiler_params=params,
-            name="across",
-        )(far_dq, *crossed)
-        z.append(swap(summed, partner))
-    kept = over_queries(keep)
-    dq = pl.pallas_call(
-        functools.partial(finish_rows_kernel, ends, len(far_late)),
-        out_shape=shape((share, head_count, width), jnp.bfloat16),
-        in_specs=[VMEM] * (2 + len(far_late) + len(near_back)),
-        out_specs=VMEM,
-        compiler_params=params,
-        name="finish_rows",
-    )(own_dq, far_dq, *far_late, *near_back)
-    dk, dv = pl.pallas_call(
-        finish_keys_kernel,
+        name="join",
+    )(keep, *[swap(cross, by) for cross, by in zip(crosses, partners)])
+    kept = over_queries(mine)
+    arrived = (own_dq, *kept, *back)
+    return pl.pallas_call(
+        functools.partial(finish_kernel, len(kept)),
         out_shape=(
+            shape((share, head_count, width), jnp.bfloat16),
             shape(key_codes.shape, jnp.bfloat16),
             shape(values.shape, jnp.bfloat16),
         ),
-        in_specs=[VMEM] * (len(kept) + len(z)),
-        out_specs=(VMEM, VMEM),
+        in_specs=[VMEM] * len(arrived),
+        out_specs=(VMEM,) * 3,
         compiler_params=params,
-        name="finish_keys",
-    )(*kept, *z)
-    return dq, dk, dv
+        name="finish",
+    )(*arrived)
 
 
 def solution(mesh):

time: 33.8 us -> 33 us (0.976)
  waiting for transfers between devices: 7.89 us -> 12 us
  starting transfers between devices: 15.9 us -> 12.2 us
  Pallas kernels: 9.08 us -> 7.89 us
    ppermute x8 -> x7, waiting for transfers between devices: 7.74 us -> 11.7 us  [swap(): return lax.ppermute(x, 'ka', [(i, i ^ by) for i in range(key_devices)])]
    ppermute x3 -> x1, starting transfers between devices: 3.59 us -> 1.51 us  [over_queries(): return [x, lax.ppermute(x, 'pb', [(0, 1), (1, 0)])]]
    ppermute x8 -> x7, starting transfers between devices: 12.3 us -> 10.7 us  [swap(): return lax.ppermute(x, 'ka', [(i, i ^ by) for i in range(key_devices)])]
    pallas_call x5 -> x2, Pallas kernels: 1.93 us -> 1.14 us  [the longest x1 1.09 us: per_device(): pl.pallas_call(functools.partial(finish_kernel, len(kept)), out_shape=(sh...]
    pallas_call x2 -> x1, Pallas kernels: 4.05 us -> 3.65 us  [rows(): pl.pallas_call(functools.partial(rows_kernel, key_devices, share, head_co...]
  transfers between devices with their start and end apart: 11 -> 8, of which waited for: 4 -> 5; matrix products, arithmetic and copies ran while one was open for 0% -> 0% of each run, Pallas kernels for 16% -> 6%
where the time goes in v5:
time: 33 us; the launch traced here: 32.8 us
  starting transfers between devices  12.2 us (37%)
  waiting for transfers between devices  12 us (36%)
  Pallas kernels  7.89 us (24%)
  between operations  0.67 us (2%)
    ppermute x7, waiting for transfers between devices, swap(): return lax.ppermute(x, 'ka', [(i, i ^ by) for i in range(key_devices)])  11.7 us
    ppermute x7, starting transfers between devices, swap(): return lax.ppermute(x, 'ka', [(i, i ^ by) for i in range(key_devices)])  10.7 us
    pallas_call x1, Pallas kernels, rows(): pl.pallas_call(functools.partial(rows_kernel, key_devices, share, head_co...  3.65 us
    pallas_call x1, Pallas kernels, per_device(): pl.pallas_call(functools.partial(gather_kernel, row_sets, share), out_sha...  1.76 us
    ppermute x1, starting transfers between devices, over_queries(): return [x, lax.ppermute(x, 'pb', [(0, 1), (1, 0)])]  1.51 us
    pallas_call x1, Pallas kernels, per_device(): pl.pallas_call(prep_kernel, out_shape=(shape((2 * key_count + SUM_ROWS, w...  1.34 us
    pallas_call x1, Pallas kernels, per_device(): pl.pallas_call(functools.partial(finish_kernel, len(kept)), out_shape=(sh...  1.09 us
  transfers between devices with their start and end apart: 8, of which 5 were waited for; matrix products, arithmetic and copies ran while one was open for 0% of the time, Pallas kernels for 6%

profile of v5, /device:TPU:0, one launch (start us, length us, event | category | flops | bytes accessed | tf_op | source)
XLA Modules:
  0.0 32.8 jit_solution(13946540560361234651)
XLA Ops:
  0.6 1.3 %prep.1 = (bf16[400,128]{1,0:T(8,128)(2,1)S(1)}, bf16[400,128]{1,0:T(8,128)(2,1)S(1)}, f32[16,128]{1,0:T(8,128)S(1)}) custom-call(s32[2,3]{1,0:T(2,128)} %bitcast.9, bf16[192,2,128]{2,1,0:T(2,128)(2,1)} %codes_hbm.1, bf16[192,2,128]{2,1,0:T(2,128)(2,1)} %values_hbm.1), custom_call_target="tpu_custom_call" | custom-call | tf_op jit(solution)/shard_map/prep/pallas_call | solution.py:231
  2.0 3.1 %collective-permute-start = (bf16[400,128]{1,0:T(8,128)(2,1)S(1)}, bf16[400,128]{1,0:T(8,128)(2,1)S(1)}, u32[]{:S(2)}, u32[]{:S(2)}) collective-permute-start(bf16[400,128]{1,0:T(8,128)(2,1)S(1)} %get-tuple-element.16.refs_2_), channel_id=1, source_target_pairs={{0,4},{4,0},{8,12},{12,8},{1,5},{5,1},{9,13},{13,9},{2,6},{6,2},{1... | collective-permute-start | bytes 307208 | tf_op jit(solution)/shard_map/ppermute | solution.py:226
  5.1 2.6 %collective-permute-start.1 = (bf16[400,128]{1,0:T(8,128)(2,1)S(1)}, bf16[400,128]{1,0:T(8,128)(2,1)S(1)}, u32[]{:S(2)}, u32[]{:S(2)}) collective-permute-start(bf16[400,128]{1,0:T(8,128)(2,1)S(1)} %get-tuple-element.17.refs_3_), channel_id=1, source_target_pairs={{0,8},{4,12},{8,0},{12,4},{1,9},{5,13},{9,1},{13,5},{2,10},{6,14},... | collective-permute-start | bytes 307208 | tf_op jit(solution)/shard_map/ppermute | solution.py:226
  7.7 0.0 collective-permute-start.2
  7.7 1.8 %gather.1 = (bf16[2,2,768,256]{3,2,1,0:T(8,128)(2,1)S(1)}, bf16[2,2,768,256]{3,2,1,0:T(8,128)(2,1)S(1)}) custom-call(bf16[384,16,128]{2,1,0:T(8,128)(2,1)} %q_hbm.1, bf16[384,16,128]{2,1,0:T(8,128)(2,1)} %do_hbm.1, f32[16,384]{1,0:T(8,128)} %bitcast.7, f32[16,384]{1,0:T(8,128)} %bitcast.8), custom_call_target="tpu_custom_call" | custom-call | tf_op jit(solution)/shard_map/gather/pallas_call | solution.py:251
  9.4 3.7 %collective-permute-done.2.refs_6_ = f32[16,128]{1,0:T(8,128)S(1)} collective-permute-done((f32[16,128]{1,0:T(8,128)S(1)}, f32[16,128]{1,0:T(8,128)S(1)}, u32[]{:S(2)}, u32[]{:S(2)}) %collective-permute-start.2) | collective-permute-done | bytes 8224 | tf_op jit(solution)/shard_map/ppermute | solution.py:226
  13.1 0.0 collective-permute-done.refs_4_
  13.1 0.0 collective-permute-done.1.refs_5_
  13.1 3.7 %near_rows.1 = (bf16[1,768,128]{2,1,0:T(8,128)(2,1)S(1)}, bf16[1,768,128]{2,1,0:T(8,128)(2,1)S(1)}, f32[2,768,128]{2,1,0:T(8,128)S(1)}, f32[4,192,128]{2,1,0:T(8...) custom-call(bf16[2,2,768,256]{3,2,1,0:T(8,128)(2,1)S(1)} %get-tuple-element.14.refs_0_, ...), custom_call_target="tpu_custom_call" | custom-call | tf_op jit(solution)/shard_map/near_rows/pallas_call | solution.py:276
  16.8 0.3 collective-permute-start.3
  17.1 2.5 %collective-permute-start.4 = (bf16[2,192,128]{2,1,0:T(8,128)(2,1)S(1)}, bf16[2,192,128]{2,1,0:T(8,128)(2,1)S(1)}, u32[]{:S(2)}, u32[]{:S(2)}) collective-permute-start(bf16[2,192,128]{2,1,0:T(8,128)(2,1)S(1)} %get-tuple-element.22), channel_id=1, source_target_pairs={{0,8},{4,12},{8,0},{12,4},{1,9},{5,13},{9,1},{13,5},{2,10},{6,14},... | collective-permute-start | bytes 294920 | tf_op jit(solution)/shard_map/ppermute | solution.py:226
  19.5 0.7 %collective-permute-start.6 = (bf16[768,128]{1,0:T(8,128)(2,1)S(1)}, bf16[768,128]{1,0:T(8,128)(2,1)S(1)}, u32[]{:S(2)}, u32[]{:S(2)}) collective-permute-start(bf16[768,128]{1,0:T(8,128)(2,1)S(1)} %bitcast.6), channel_id=1, source_target_pairs={{0,4},{4,0},{8,12},{12,8},{1,5},{5,1},{9,13},{13,9},{2,6},{6,2},{1... | collective-permute-start | bytes 589832 | tf_op jit(solution)/shard_map/ppermute | solution.py:226
  20.2 1.6 %collective-permute-start.7 = (bf16[768,128]{1,0:T(8,128)(2,1)S(1)}, bf16[768,128]{1,0:T(8,128)(2,1)S(1)}, u32[]{:S(2)}, u32[]{:S(2)}) collective-permute-start(bf16[768,128]{1,0:T(8,128)(2,1)S(1)} %bitcast.5), channel_id=1, source_target_pairs={{0,8},{4,12},{8,0},{12,4},{1,9},{5,13},{9,1},{13,5},{2,10},{6,14},... | collective-permute-start | bytes 589832 | tf_op jit(solution)/shard_map/ppermute | solution.py:226
  21.8 4.1 %collective-permute-done.3.refs_0_ = bf16[2,192,128]{2,1,0:T(8,128)(2,1)S(1)} collective-permute-done((bf16[2,192,128]{2,1,0:T(8,128)(2,1)S(1)}, bf16[2,192,128]{2,1,0:T(8,128)(2,1)S(1)}, u32[]{:S(2)}, u32[]{:S(2)}) %collective-permute-start.3) | collective-permute-done | bytes 98336 | tf_op jit(solution)/shard_map/ppermute | solution.py:226
  25.9 0.0 collective-permute-done.4.refs_1_
  26.0 1.5 %collective-permute-start.5 = (bf16[4,192,128]{2,1,0:T(8,128)(2,1)S(1)}, bf16[4,192,128]{2,1,0:T(8,128)(2,1)S(1)}, u32[]{:S(2)}, u32[]{:S(2)}) collective-permute-start(bf16[4,192,128]{2,1,0:T(8,128)(2,1)S(1)} %join.1.refs_0_), channel_id=1, source_target_pairs={{0,16},{16,0},{1,17},{17,1},{2,18},{18,2},{3,19},{19,3},{4,20},{20... | collective-permute-start | bytes 589832 | tf_op jit(solution)/shard_map/ppermute | solution.py:308
  27.5 2.8 %collective-permute-done.6.refs_2_ = bf16[768,128]{1,0:T(8,128)(2,1)S(1)} collective-permute-done((bf16[768,128]{1,0:T(8,128)(2,1)S(1)}, bf16[768,128]{1,0:T(8,128)(2,1)S(1)}, u32[]{:S(2)}, u32[]{:S(2)}) %collective-permute-start.6) | collective-permute-done | bytes 196640 | tf_op jit(solution)/shard_map/ppermute | solution.py:226
  30.3 1.1 %collective-permute-done.7.refs_3_ = bf16[768,128]{1,0:T(8,128)(2,1)S(1)} collective-permute-done((bf16[768,128]{1,0:T(8,128)(2,1)S(1)}, bf16[768,128]{1,0:T(8,128)(2,1)S(1)}, u32[]{:S(2)}, u32[]{:S(2)}) %collective-permute-start.7) | collective-permute-done | bytes 196640 | tf_op jit(solution)/shard_map/ppermute | solution.py:226
  31.4 0.3 collective-permute-done.5.refs_1_
  31.7 1.1 %finish.1 = (bf16[96,16,128]{2,1,0:T(8,128)(2,1)}, bf16[192,2,128]{2,1,0:T(2,128)(2,1)}, bf16[192,2,128]{2,1,0:T(2,128)(2,1)}) custom-call(f32[2,768,128]{2,1,0:T(8,128)S(1)} %get-tuple-element.19.own_ref, bf16[4,192,128]{2,1,0:T(8,128)(2,1)S(1)} %join.1.refs_0_, bf16[4,192,128]{2,1,0:T(8,128)(2,1)S(1)} %collective-permute-done.5.refs_1_, ...), custom_call_target="tpu_custom_call" | custom-call | tf_op jit(solution)/shard_map/finish/pallas_call | solution.py:322
  (1 shorter events, 0.0 us)
Async XLA Ops:
  2.0 11.1 %collective-permute-start = (bf16[400,128]{1,0:T(8,128)(2,1)S(1)}, bf16[400,128]{1,0:T(8,128)(2,1)S(1)}, u32[]{:S(2)}, u32[]{:S(2)}) collective-permute-start(bf16[400,128]{1,0:T(8,128)(2,1)S(1)} %get-tuple-element.16.refs_2_), channel_id=1, source_target_pairs={{0,4},{4,0},{8,12},{12,8},{1,5},{5,1},{9,13},{13,9},{2,6},{6,2},{1... | collective-permute-start | bytes 307208 | tf_op jit(solution)/shard_map/ppermute | solution.py:226
  5.1 8.0 %collective-permute-start.1 = (bf16[400,128]{1,0:T(8,128)(2,1)S(1)}, bf16[400,128]{1,0:T(8,128)(2,1)S(1)}, u32[]{:S(2)}, u32[]{:S(2)}) collective-permute-start(bf16[400,128]{1,0:T(8,128)(2,1)S(1)} %get-tuple-element.17.refs_3_), channel_id=1, source_target_pairs={{0,8},{4,12},{8,0},{12,4},{1,9},{5,13},{9,1},{13,5},{2,10},{6,14},... | collective-permute-start | bytes 307208 | tf_op jit(solution)/shard_map/ppermute | solution.py:226
  7.7 5.4 %collective-permute-start.2 = (f32[16,128]{1,0:T(8,128)S(1)}, f32[16,128]{1,0:T(8,128)S(1)}, u32[]{:S(2)}, u32[]{:S(2)}) collective-permute-start(f32[16,128]{1,0:T(8,128)S(1)} %get-tuple-element.18), channel_id=1, source_target_pairs={{0,12},{4,8},{8,4},{12,0},{1,13},{5,9},{9,5},{13,1},{2,14},{6,10},... | collective-permute-start | bytes 24584 | tf_op jit(solution)/shard_map/ppermute | solution.py:226
  16.8 9.1 %collective-permute-start.3 = (bf16[2,192,128]{2,1,0:T(8,128)(2,1)S(1)}, bf16[2,192,128]{2,1,0:T(8,128)(2,1)S(1)}, u32[]{:S(2)}, u32[]{:S(2)}) collective-permute-start(bf16[2,192,128]{2,1,0:T(8,128)(2,1)S(1)} %get-tuple-element.21), channel_id=1, source_target_pairs={{0,4},{4,0},{8,12},{12,8},{1,5},{5,1},{9,13},{13,9},{2,6},{6,2},{1... | collective-permute-start | bytes 294920 | tf_op jit(solution)/shard_map/ppermute | solution.py:226
  17.1 8.9 %collective-permute-start.4 = (bf16[2,192,128]{2,1,0:T(8,128)(2,1)S(1)}, bf16[2,192,128]{2,1,0:T(8,128)(2,1)S(1)}, u32[]{:S(2)}, u32[]{:S(2)}) collective-permute-start(bf16[2,192,128]{2,1,0:T(8,128)(2,1)S(1)} %get-tuple-element.22), channel_id=1, source_target_pairs={{0,8},{4,12},{8,0},{12,4},{1,9},{5,13},{9,1},{13,5},{2,10},{6,14},... | collective-permute-start | bytes 294920 | tf_op jit(solution)/shard_map/ppermute | solution.py:226
  19.5 10.8 %collective-permute-start.6 = (bf16[768,128]{1,0:T(8,128)(2,1)S(1)}, bf16[768,128]{1,0:T(8,128)(2,1)S(1)}, u32[]{:S(2)}, u32[]{:S(2)}) collective-permute-start(bf16[768,128]{1,0:T(8,128)(2,1)S(1)} %bitcast.6), channel_id=1, source_target_pairs={{0,4},{4,0},{8,12},{12,8},{1,5},{5,1},{9,13},{13,9},{2,6},{6,2},{1... | collective-permute-start | bytes 589832 | tf_op jit(solution)/shard_map/ppermute | solution.py:226
  20.2 11.2 %collective-permute-start.7 = (bf16[768,128]{1,0:T(8,128)(2,1)S(1)}, bf16[768,128]{1,0:T(8,128)(2,1)S(1)}, u32[]{:S(2)}, u32[]{:S(2)}) collective-permute-start(bf16[768,128]{1,0:T(8,128)(2,1)S(1)} %bitcast.5), channel_id=1, source_target_pairs={{0,8},{4,12},{8,0},{12,4},{1,9},{5,13},{9,1},{13,5},{2,10},{6,14},... | collective-permute-start | bytes 589832 | tf_op jit(solution)/shard_map/ppermute | solution.py:226
  26.0 5.7 %collective-permute-start.5 = (bf16[4,192,128]{2,1,0:T(8,128)(2,1)S(1)}, bf16[4,192,128]{2,1,0:T(8,128)(2,1)S(1)}, u32[]{:S(2)}, u32[]{:S(2)}) collective-permute-start(bf16[4,192,128]{2,1,0:T(8,128)(2,1)S(1)} %join.1.refs_0_), channel_id=1, source_target_pairs={{0,16},{16,0},{1,17},{17,1},{2,18},{18,2},{3,19},{19,3},{4,20},{20... | collective-permute-start | bytes 589832 | tf_op jit(solution)/shard_map/ppermute | solution.py:308

commit v6 on v5

--- a/solution.py
+++ b/solution.py
@@ -112,26 +112,24 @@
                     dst[g, to, :, width:] = extra.reshape(cols, width).astype(jnp.bfloat16)
 
 
-def rows_kernel(key_devices, share, heads, partners, row_sets, tasks, first, *refs):
+def rows_kernel(key_devices, share, heads, partners, row_sets, first, *refs):
     kv_heads = len(partners)
-    busy = [g for g in range(kv_heads) if tasks[g]]
-    pieces = 1
-    sending = [g for g in busy if any(tasks[g]) for _ in range(pieces)]
-    ends = [g for g in range(kv_heads) if partners[g] != partners[0]]
     q_ref, do_ref, *refs = refs
     own_refs, got_refs, refs = refs[:kv_heads], refs[kv_heads : 2 * kv_heads], refs[2 * kv_heads :]
-    dq_ref, keep_ref = refs[-2 - kv_heads : -kv_heads]
-    cross_refs, refs = refs[-kv_heads:], refs[: -2 - kv_heads]
-    send_refs = list(zip(sending, refs[-len(sending) :]))
-    sum_refs = refs[: -len(sending)]
+    if first:
+        part_ref, *cross_refs = refs[-1 - kv_heads :]
+        sum_refs = refs[: -1 - kv_heads]
+    else:
+        *sum_refs, part_ref = refs[: -2 - kv_heads]
+        *send_refs, dq_ref, keep_ref = refs[-2 - kv_heads :]
     ka, pb = lax.axis_index("ka"), lax.axis_index("pb")
     cols, width = q_ref.shape[2], q_ref.shape[3] // 2
     key_count = (own_refs[0].shape[0] - SUM_ROWS) // 2
     group = cols // share
     root = width**-0.5
-    line = lax.broadcasted_iota(jnp.int32, (2 * key_count, cols), 0)
-    step = lax.broadcasted_iota(jnp.int32, (2 * key_count, cols), 1) // group
-    lane = lax.broadcasted_iota(jnp.int32, (2 * key_count, width), 1)
+    lead = lax.broadcasted_iota(jnp.int32, (key_count, cols), 0)
+    lead = lead - lax.broadcasted_iota(jnp.int32, (key_count, cols), 1) // group
+    lane = lax.broadcasted_iota(jnp.int32, (key_count, width), 1)
     minus = jnp.where(lane < 6 * heads, -1.0, 0.0).astype(jnp.bfloat16)
     parts = own_refs[0][2 * key_count :].astype(jnp.float32)
     for partner in dict(zip(partners, range(kv_heads))).values():
@@ -139,25 +137,19 @@
     whole = jnp.zeros((SUM_ROWS, width), jnp.float32)
     for ref in sum_refs:
         whole = whole + ref[...]
-    for g in busy:
-        own, got = own_refs[g], got_refs[g]
+    for g in range(kv_heads):
+        message = got_refs[g] if first else own_refs[g]
         total = jnp.sum(parts[3 * g : 3 * g + 3], axis=0, keepdims=True) + whole[g : g + 1]
         mean = total / (key_count * key_devices)
-        k = jnp.concatenate([own[0:key_count], got[0:key_count]], axis=0).astype(jnp.float32)
-        k = (k - mean).astype(jnp.bfloat16)
+        k = (message[0:key_count].astype(jnp.float32) - mean).astype(jnp.bfloat16)
         turned = k.astype(jnp.float32).T.astype(jnp.bfloat16)
         k = jnp.concatenate([k, minus], axis=1)
-        v = jnp.concatenate(
-            [own[key_count : 2 * key_count], got[key_count : 2 * key_count]], axis=0
-        )
-        v = jnp.concatenate([v, minus], axis=1)
-        base = jnp.where(line < key_count, ka * key_count, ((ka ^ partners[g]) - 1) * key_count)
-        lead = line + base - step
+        v = jnp.concatenate([message[key_count : 2 * key_count], minus], axis=1)
+        base = (ka ^ partners[g] if first else ka) * key_count
         dk = dv = None
-        for m in tasks[g]:
-            at = row_sets[g].index(m)
+        for at, m in enumerate(row_sets[g]):
             q, do = q_ref[g, at], do_ref[g, at]
-            visible = lead <= pb * (share * key_devices) + (ka ^ m) * share
+            visible = lead <= pb * (share * key_devices) + (ka ^ m) * share - base
             scores = lax.dot_general(k, q, NT, preferred_element_type=jnp.float32)
             weights = jnp.where(visible, jnp.exp2(scores * (root * LOG2E)), 0.0)
             dp = lax.dot_general(v, do, NT, preferred_element_type=jnp.float32)
@@ -168,17 +160,21 @@
             dk_now = jnp.dot(ds, q[:, :width], preferred_element_type=jnp.float32)
             dv = dv_now if dv is None else dv + dv_now
             dk = dk_now if dk is None else dk + dk_now
-            dq = jnp.dot(turned, ds, preferred_element_type=jnp.float32).T * root
+            dq = jnp.dot(turned, ds, preferred_element_type=jnp.float32)
+            if first:
+                part_ref[g, at] = dq
+                continue
+            dq = (dq + part_ref[g, at]).T * root
             if m == 0:
                 dq_ref[g] = dq
             else:
                 others = [other for other in row_sets[g] if other]
-                for j, ref in enumerate(ref for to, ref in send_refs if to == g):
-                    piece = dq[j * cols // pieces : (j + 1) * cols // pieces]
-                    ref[others.index(m)] = piece.astype(jnp.bfloat16)
+                send_refs[g][others.index(m)] = dq.astype(jnp.bfloat16)
         for j, grad in enumerate((dk * root, dv)):
-            keep_ref[2 * g + j] = grad[:key_count]
-            cross_refs[g][j] = grad[key_count:].astype(jnp.bfloat16)
+            if first:
+                cross_refs[g][j] = grad.astype(jnp.bfloat16)
+            else:
+                keep_ref[2 * g + j] = grad
 
 
 def join_kernel(keep_ref, *refs):
@@ -196,7 +192,7 @@
     outs = []
     for g in range(kv_heads):
         dq = own_ref[g]
-        for ref in back_refs[kv_heads - 1 - g :: kv_heads]:
+        for ref in back_refs[g::kv_heads]:
             dq = dq + ref[...].astype(jnp.float32)
         outs.append(dq.reshape(share, heads // kv_heads, width))
     dq_ref[...] = jnp.concatenate(outs, axis=1).astype(jnp.bfloat16)
@@ -272,27 +268,28 @@
     ends = [g for g in range(kv_heads) if partners[g] != partners[0]]
     inputs = (rows_q, rows_do, *messages, *got, *others)
 
-    def rows(tasks, first, *extra, out_shape):
+    def rows(first, *extra, out_shape):
         return pl.pallas_call(
             functools.partial(
-                rows_kernel, key_devices, share, head_count, partners, row_sets, tasks, first
+                rows_kernel, key_devices, share, head_count, partners, row_sets, first
             ),
             out_shape=out_shape,
             in_specs=[VMEM] * (len(inputs) + len(extra)),
             out_specs=(VMEM,) * len(out_shape),
             compiler_params=params,
-            name="far_rows" if first else "near_rows",
+            name="partner_keys" if first else "own_keys",
         )(*inputs, *extra)
 
-    results = rows(
-        row_sets,
+    handed, *crosses = rows(
+        True,
+        out_shape=(shape((kv_heads, key_devices // 2, width, cols), jnp.float32),)
+        + (one,) * kv_heads,
+    )
+    *sends, own_dq, keep = rows(
         False,
-        out_shape=(sent,) * kv_heads
-        + (shape((kv_heads, cols, width), jnp.float32), whole_part)
-        + (one,) * kv_heads,
-    )
-    sends, crosses = results[:kv_heads], results[kv_heads + 2 :]
-    own_dq, keep = results[kv_heads : kv_heads + 2]
+        handed,
+        out_shape=(sent,) * kv_heads + (shape((kv_heads, cols, width), jnp.float32), whole_part),
+    )
 
     def send_back(sends, heads):
         return [
@@ -301,7 +298,7 @@
             for send, g in zip(sends, heads)
         ]
 
-    back = send_back(sends[::-1], list(range(kv_heads))[::-1])
+    back = send_back(sends, list(range(kv_heads)))
 
     def over_queries(x):
         if query_devices == 2:

time: 33 us -> 32 us (0.970)
  waiting for transfers between devices: 12 us -> 9.78 us
  Pallas kernels: 7.89 us -> 9.08 us
    ppermute x7, waiting for transfers between devices: 11.7 us -> 9.78 us  [swap(): return lax.ppermute(x, 'ka', [(i, i ^ by) for i in range(key_devices)])]
    pallas_call x1 -> x2, Pallas kernels: 3.65 us -> 4.84 us  [rows(): pl.pallas_call(functools.partial(rows_kernel, key_devices, share, head_co...]
  transfers between devices with their start and end apart: 8 -> 8, of which waited for: 5 -> 2; matrix products, arithmetic and copies ran while one was open for 0% -> 0% of each run, Pallas kernels for 6% -> 14%
where the time goes in v6:
time: 32 us; the launch traced here: 31.8 us
  starting transfers between devices  12.3 us (38%)
  waiting for transfers between devices  9.78 us (31%)
  Pallas kernels  9.08 us (28%)
  between operations  0.67 us (2%)
    ppermute x7, starting transfers between devices, swap(): return lax.ppermute(x, 'ka', [(i, i ^ by) for i in range(key_devices)])  10.8 us
    ppermute x7, waiting for transfers between devices, swap(): return lax.ppermute(x, 'ka', [(i, i ^ by) for i in range(key_devices)])  9.78 us
    pallas_call x2, Pallas kernels, rows(): pl.pallas_call(functools.partial(rows_kernel, key_devices, share, head_co...  4.84 us
    pallas_call x1, Pallas kernels, per_device(): pl.pallas_call(functools.partial(gather_kernel, row_sets, share), out_sha...  1.76 us
    ppermute x1, starting transfers between devices, over_queries(): return [x, lax.ppermute(x, 'pb', [(0, 1), (1, 0)])]  1.55 us
    pallas_call x1, Pallas kernels, per_device(): pl.pallas_call(prep_kernel, out_shape=(shape((2 * key_count + SUM_ROWS, w...  1.34 us
    pallas_call x1, Pallas kernels, per_device(): pl.pallas_call(functools.partial(finish_kernel, len(kept)), out_shape=(sh...  1.09 us
  transfers between devices with their start and end apart: 8, of which 2 were waited for; matrix products, arithmetic and copies ran while one was open for 0% of the time, Pallas kernels for 14%

profile of v6, /device:TPU:0, one launch (start us, length us, event | category | flops | bytes accessed | tf_op | source)
XLA Modules:
  0.0 31.8 jit_solution(1734581708176446719)
XLA Ops:
  0.6 1.3 %prep.1 = (bf16[400,128]{1,0:T(8,128)(2,1)S(1)}, bf16[400,128]{1,0:T(8,128)(2,1)S(1)}, f32[16,128]{1,0:T(8,128)S(1)}) custom-call(s32[2,3]{1,0:T(2,128)} %bitcast.9, bf16[192,2,128]{2,1,0:T(2,128)(2,1)} %codes_hbm.1, bf16[192,2,128]{2,1,0:T(2,128)(2,1)} %values_hbm.1), custom_call_target="tpu_custom_call" | custom-call | tf_op jit(solution)/shard_map/prep/pallas_call | solution.py:227
  2.0 3.1 %collective-permute-start = (bf16[400,128]{1,0:T(8,128)(2,1)S(1)}, bf16[400,128]{1,0:T(8,128)(2,1)S(1)}, u32[]{:S(2)}, u32[]{:S(2)}) collective-permute-start(bf16[400,128]{1,0:T(8,128)(2,1)S(1)} %get-tuple-element.17.refs_2_), channel_id=1, source_target_pairs={{0,4},{4,0},{8,12},{12,8},{1,5},{5,1},{9,13},{13,9},{2,6},{6,2},{1... | collective-permute-start | bytes 307208 | tf_op jit(solution)/shard_map/ppermute | solution.py:222
  5.1 2.6 %collective-permute-start.1 = (bf16[400,128]{1,0:T(8,128)(2,1)S(1)}, bf16[400,128]{1,0:T(8,128)(2,1)S(1)}, u32[]{:S(2)}, u32[]{:S(2)}) collective-permute-start(bf16[400,128]{1,0:T(8,128)(2,1)S(1)} %get-tuple-element.18.refs_3_), channel_id=1, source_target_pairs={{0,8},{4,12},{8,0},{12,4},{1,9},{5,13},{9,1},{13,5},{2,10},{6,14},... | collective-permute-start | bytes 307208 | tf_op jit(solution)/shard_map/ppermute | solution.py:222
  7.7 0.0 collective-permute-start.2
  7.7 1.8 %gather.1 = (bf16[2,2,768,256]{3,2,1,0:T(8,128)(2,1)S(1)}, bf16[2,2,768,256]{3,2,1,0:T(8,128)(2,1)S(1)}) custom-call(bf16[384,16,128]{2,1,0:T(8,128)(2,1)} %q_hbm.1, bf16[384,16,128]{2,1,0:T(8,128)(2,1)} %do_hbm.1, f32[16,384]{1,0:T(8,128)} %bitcast.7, f32[16,384]{1,0:T(8,128)} %bitcast.8), custom_call_target="tpu_custom_call" | custom-call | tf_op jit(solution)/shard_map/gather/pallas_call | solution.py:247
  9.4 3.7 %collective-permute-done.2.refs_6_ = f32[16,128]{1,0:T(8,128)S(1)} collective-permute-done((f32[16,128]{1,0:T(8,128)S(1)}, f32[16,128]{1,0:T(8,128)S(1)}, u32[]{:S(2)}, u32[]{:S(2)}) %collective-permute-start.2) | collective-permute-done | bytes 8224 | tf_op jit(solution)/shard_map/ppermute | solution.py:222
  13.1 0.0 collective-permute-done.refs_4_
  13.1 0.0 collective-permute-done.1.refs_5_
  13.1 2.4 %partner_keys.1 = (f32[2,2,128,768]{3,2,1,0:T(8,128)S(1)}, bf16[2,192,128]{2,1,0:T(8,128)(2,1)S(1)}, bf16[2,192,128]{2,1,0:T(8,128)(2,1)S(1)}) custom-call(bf16[2,2,768,256]{3,2,1,0:T(8,128)(2,1)S(1)} %get-tuple-element.15.refs_0_, bf16[2,2,768,256]{3,2,1,0:T(8,128)(2,1)S(1)} %get-tuple-element.16.refs_1_, bf16[400,128]{1,0:T(8,128)(2,1)S(1)} %get-tuple-element.17.refs_2_, ...), custom_call_target="tpu_custom_call" | custom-call | tf_op jit(solution)/shard_map/partner_keys/pallas_call | solution.py:272
  15.5 0.3 collective-permute-start.3
  15.8 2.5 %collective-permute-start.4 = (bf16[2,192,128]{2,1,0:T(8,128)(2,1)S(1)}, bf16[2,192,128]{2,1,0:T(8,128)(2,1)S(1)}, u32[]{:S(2)}, u32[]{:S(2)}) collective-permute-start(bf16[2,192,128]{2,1,0:T(8,128)(2,1)S(1)} %get-tuple-element.24), channel_id=1, source_target_pairs={{0,8},{4,12},{8,0},{12,4},{1,9},{5,13},{9,1},{13,5},{2,10},{6,14},... | collective-permute-start | bytes 294920 | tf_op jit(solution)/shard_map/ppermute | solution.py:222
  18.2 2.5 %own_keys.1 = (bf16[1,768,128]{2,1,0:T(8,128)(2,1)S(1)}, bf16[1,768,128]{2,1,0:T(8,128)(2,1)S(1)}, f32[2,768,128]{2,1,0:T(8,128)S(1)}, f32[4,192,128]{2,1,0:T(8,128)S(1)}) custom-call(bf16[2,2,768,256]{3,2,1,0:T(8,128)(2,1)S(1)} %get-tuple-element.15.refs_0_, bf16[2,2,768,256]{3,2,1,0:T(8,128)(2,1)S(1)} %get-tuple-element.16.refs_1_, ...), custom_call_target="tpu_custom_call" | custom-call | tf_op jit(solution)/shard_map/own_keys/pallas_call | solution.py:272
  20.7 0.5 %collective-permute-start.6 = (bf16[768,128]{1,0:T(8,128)(2,1)S(1)}, bf16[768,128]{1,0:T(8,128)(2,1)S(1)}, u32[]{:S(2)}, u32[]{:S(2)}) collective-permute-start(bf16[768,128]{1,0:T(8,128)(2,1)S(1)} %bitcast.6), channel_id=1, source_target_pairs={{0,8},{4,12},{8,0},{12,4},{1,9},{5,13},{9,1},{13,5},{2,10},{6,14},... | collective-permute-start | bytes 589832 | tf_op jit(solution)/shard_map/ppermute | solution.py:222
  21.2 1.8 %collective-permute-start.7 = (bf16[768,128]{1,0:T(8,128)(2,1)S(1)}, bf16[768,128]{1,0:T(8,128)(2,1)S(1)}, u32[]{:S(2)}, u32[]{:S(2)}) collective-permute-start(bf16[768,128]{1,0:T(8,128)(2,1)S(1)} %bitcast.5), channel_id=1, source_target_pairs={{0,4},{4,0},{8,12},{12,8},{1,5},{5,1},{9,13},{13,9},{2,6},{6,2},{1... | collective-permute-start | bytes 589832 | tf_op jit(solution)/shard_map/ppermute | solution.py:222
  23.0 0.0 collective-permute-done.3.refs_0_
  23.0 0.0 collective-permute-done.4.refs_1_
  23.0 0.1 join.1.refs_0_
  23.1 1.6 %collective-permute-start.5 = (bf16[4,192,128]{2,1,0:T(8,128)(2,1)S(1)}, bf16[4,192,128]{2,1,0:T(8,128)(2,1)S(1)}, u32[]{:S(2)}, u32[]{:S(2)}) collective-permute-start(bf16[4,192,128]{2,1,0:T(8,128)(2,1)S(1)} %join.1.refs_0_), channel_id=1, source_target_pairs={{0,16},{16,0},{1,17},{17,1},{2,18},{18,2},{3,19},{19,3},{4,20},{20... | collective-permute-start | bytes 589832 | tf_op jit(solution)/shard_map/ppermute | solution.py:305
  24.7 6.1 %collective-permute-done.6.refs_2_ = bf16[768,128]{1,0:T(8,128)(2,1)S(1)} collective-permute-done((bf16[768,128]{1,0:T(8,128)(2,1)S(1)}, bf16[768,128]{1,0:T(8,128)(2,1)S(1)}, u32[]{:S(2)}, u32[]{:S(2)}) %collective-permute-start.6) | collective-permute-done | bytes 196640 | tf_op jit(solution)/shard_map/ppermute | solution.py:222
  30.7 0.0 collective-permute-done.7.refs_3_
  30.8 0.0 collective-permute-done.5.refs_1_
  30.8 1.1 %finish.1 = (bf16[96,16,128]{2,1,0:T(8,128)(2,1)}, bf16[192,2,128]{2,1,0:T(2,128)(2,1)}, bf16[192,2,128]{2,1,0:T(2,128)(2,1)}) custom-call(f32[2,768,128]{2,1,0:T(8,128)S(1)} %get-tuple-element.21.own_ref, bf16[4,192,128]{2,1,0:T(8,128)(2,1)S(1)} %join.1.refs_0_, bf16[4,192,128]{2,1,0:T(8,128)(2,1)S(1)} %collective-permute-done.5.refs_1_, ...), custom_call_target="tpu_custom_call" | custom-call | tf_op jit(solution)/shard_map/finish/pallas_call | solution.py:319
Async XLA Ops:
  2.0 11.1 %collective-permute-start = (bf16[400,128]{1,0:T(8,128)(2,1)S(1)}, bf16[400,128]{1,0:T(8,128)(2,1)S(1)}, u32[]{:S(2)}, u32[]{:S(2)}) collective-permute-start(bf16[400,128]{1,0:T(8,128)(2,1)S(1)} %get-tuple-element.17.refs_2_), channel_id=1, source_target_pairs={{0,4},{4,0},{8,12},{12,8},{1,5},{5,1},{9,13},{13,9},{2,6},{6,2},{1... | collective-permute-start | bytes 307208 | tf_op jit(solution)/shard_map/ppermute | solution.py:222
  5.1 8.0 %collective-permute-start.1 = (bf16[400,128]{1,0:T(8,128)(2,1)S(1)}, bf16[400,128]{1,0:T(8,128)(2,1)S(1)}, u32[]{:S(2)}, u32[]{:S(2)}) collective-permute-start(bf16[400,128]{1,0:T(8,128)(2,1)S(1)} %get-tuple-element.18.refs_3_), channel_id=1, source_target_pairs={{0,8},{4,12},{8,0},{12,4},{1,9},{5,13},{9,1},{13,5},{2,10},{6,14},... | collective-permute-start | bytes 307208 | tf_op jit(solution)/shard_map/ppermute | solution.py:222
  7.7 5.4 %collective-permute-start.2 = (f32[16,128]{1,0:T(8,128)S(1)}, f32[16,128]{1,0:T(8,128)S(1)}, u32[]{:S(2)}, u32[]{:S(2)}) collective-permute-start(f32[16,128]{1,0:T(8,128)S(1)} %get-tuple-element.19), channel_id=1, source_target_pairs={{0,12},{4,8},{8,4},{12,0},{1,13},{5,9},{9,5},{13,1},{2,14},{6,10},... | collective-permute-start | bytes 24584 | tf_op jit(solution)/shard_map/ppermute | solution.py:222
  15.5 7.6 %collective-permute-start.3 = (bf16[2,192,128]{2,1,0:T(8,128)(2,1)S(1)}, bf16[2,192,128]{2,1,0:T(8,128)(2,1)S(1)}, u32[]{:S(2)}, u32[]{:S(2)}) collective-permute-start(bf16[2,192,128]{2,1,0:T(8,128)(2,1)S(1)} %get-tuple-element.23), channel_id=1, source_target_pairs={{0,4},{4,0},{8,12},{12,8},{1,5},{5,1},{9,13},{13,9},{2,6},{6,2},{1... | collective-permute-start | bytes 294920 | tf_op jit(solution)/shard_map/ppermute | solution.py:222
  15.8 7.3 %collective-permute-start.4 = (bf16[2,192,128]{2,1,0:T(8,128)(2,1)S(1)}, bf16[2,192,128]{2,1,0:T(8,128)(2,1)S(1)}, u32[]{:S(2)}, u32[]{:S(2)}) collective-permute-start(bf16[2,192,128]{2,1,0:T(8,128)(2,1)S(1)} %get-tuple-element.24), channel_id=1, source_target_pairs={{0,8},{4,12},{8,0},{12,4},{1,9},{5,13},{9,1},{13,5},{2,10},{6,14},... | collective-permute-start | bytes 294920 | tf_op jit(solution)/shard_map/ppermute | solution.py:222
  20.7 10.0 %collective-permute-start.6 = (bf16[768,128]{1,0:T(8,128)(2,1)S(1)}, bf16[768,128]{1,0:T(8,128)(2,1)S(1)}, u32[]{:S(2)}, u32[]{:S(2)}) collective-permute-start(bf16[768,128]{1,0:T(8,128)(2,1)S(1)} %bitcast.6), channel_id=1, source_target_pairs={{0,8},{4,12},{8,0},{12,4},{1,9},{5,13},{9,1},{13,5},{2,10},{6,14},... | collective-permute-start | bytes 589832 | tf_op jit(solution)/shard_map/ppermute | solution.py:222
  21.2 9.5 %collective-permute-start.7 = (bf16[768,128]{1,0:T(8,128)(2,1)S(1)}, bf16[768,128]{1,0:T(8,128)(2,1)S(1)}, u32[]{:S(2)}, u32[]{:S(2)}) collective-permute-start(bf16[768,128]{1,0:T(8,128)(2,1)S(1)} %bitcast.5), channel_id=1, source_target_pairs={{0,4},{4,0},{8,12},{12,8},{1,5},{5,1},{9,13},{13,9},{2,6},{6,2},{1... | collective-permute-start | bytes 589832 | tf_op jit(solution)/shard_map/ppermute | solution.py:222
  23.1 7.7 %collective-permute-start.5 = (bf16[4,192,128]{2,1,0:T(8,128)(2,1)S(1)}, bf16[4,192,128]{2,1,0:T(8,128)(2,1)S(1)}, u32[]{:S(2)}, u32[]{:S(2)}) collective-permute-start(bf16[4,192,128]{2,1,0:T(8,128)(2,1)S(1)} %join.1.refs_0_), channel_id=1, source_target_pairs={{0,16},{16,0},{1,17},{17,1},{2,18},{18,2},{3,19},{19,3},{4,20},{20... | collective-permute-start | bytes 589832 | tf_op jit(solution)/shard_map/ppermute | solution.py:305

commit v7 on v6

--- a/solution.py
+++ b/solution.py
@@ -177,11 +177,9 @@
                 keep_ref[2 * g + j] = grad
 
 
-def join_kernel(keep_ref, *refs):
-    *got_refs, out_ref = refs
-    for g, ref in enumerate(got_refs):
-        total = keep_ref[2 * g : 2 * g + 2] + ref[...].astype(jnp.float32)
-        out_ref[2 * g : 2 * g + 2] = total.astype(jnp.bfloat16)
+def join_kernel(g, keep_ref, got_ref, out_ref):
+    total = keep_ref[2 * g : 2 * g + 2] + got_ref[...].astype(jnp.float32)
+    out_ref[...] = total.astype(jnp.bfloat16)
 
 
 def finish_kernel(kept_count, own_ref, *refs):
@@ -196,11 +194,15 @@
             dq = dq + ref[...].astype(jnp.float32)
         outs.append(dq.reshape(share, heads // kv_heads, width))
     dq_ref[...] = jnp.concatenate(outs, axis=1).astype(jnp.bfloat16)
-    total = kept_refs[0][...].astype(jnp.float32)
-    for ref in kept_refs[1:]:
-        total = total + ref[...].astype(jnp.float32)
+    each = kept_count // kv_heads
+    totals = []
+    for g in range(kv_heads):
+        total = kept_refs[g * each][...].astype(jnp.float32)
+        for ref in kept_refs[g * each + 1 : (g + 1) * each]:
+            total = total + ref[...].astype(jnp.float32)
+        totals.append(total)
     for j, ref in enumerate((dk_ref, dv_ref)):
-        grads = jnp.stack([total[2 * g + j] for g in range(kv_heads)], axis=1)
+        grads = jnp.stack([total[j] for total in totals], axis=1)
         ref[...] = grads.astype(jnp.bfloat16)
 
 
@@ -260,7 +262,6 @@
         name="gather",
     )(pinned(queries), pinned(grad_out), pinned(log_totals.T), pinned(grad_dot.T))
 
-    part = shape((2 * kv_heads, key_count, width), jnp.bfloat16)
     whole_part = shape((2 * kv_heads, key_count, width), jnp.float32)
     one = shape((2, key_count, width), jnp.bfloat16)
     sent = shape((key_devices // 2 - 1, cols, width), jnp.bfloat16)
@@ -305,16 +306,20 @@
             return [x, lax.ppermute(x, "pb", [(0, 1), (1, 0)])]
         return [lax.psum(x.astype(jnp.float32), "pb")]
 
-    mine = pl.pallas_call(
-        join_kernel,
-        out_shape=part,
-        in_specs=[VMEM] * (1 + kv_heads),
-        out_specs=VMEM,
-        compiler_params=params,
-        cost_estimate=pl.CostEstimate(flops=10**10, bytes_accessed=2**20, transcendentals=0),
-        name="join",
-    )(keep, *[swap(cross, by) for cross, by in zip(crosses, partners)])
-    kept = over_queries(mine)
+    kept = []
+    for g, (cross, partner) in enumerate(zip(crosses, partners)):
+        mine = pl.pallas_call(
+            functools.partial(join_kernel, g),
+            out_shape=one,
+            in_specs=[VMEM] * 2,
+            out_specs=VMEM,
+            compiler_params=params,
+            cost_estimate=pl.CostEstimate(
+                flops=10**10, bytes_accessed=2**20, transcendentals=0
+            ),
+            name="join",
+        )(keep, swap(cross, partner))
+        kept += over_queries(mine)
     arrived = (own_dq, *kept, *back)
     return pl.pallas_call(
         functools.partial(finish_kernel, len(kept)),

time: 32 us -> 32 us (level)
  waiting for transfers between devices: 9.78 us -> 9.17 us
  starting transfers between devices: 12.3 us -> 12.9 us
    ppermute x7, waiting for transfers between devices: 9.78 us -> 5.09 us  [swap(): return lax.ppermute(x, 'ka', [(i, i ^ by) for i in range(key_devices)])]
    ppermute x1 -> x2, waiting for transfers between devices: 0.01 us -> 4.08 us  [over_queries(): return [x, lax.ppermute(x, 'pb', [(0, 1), (1, 0)])]]
    ppermute x1 -> x2, starting transfers between devices: 1.55 us -> 2.16 us  [over_queries(): return [x, lax.ppermute(x, 'pb', [(0, 1), (1, 0)])]]
  transfers between devices with their start and end apart: 8 -> 9, of which waited for: 2 -> 4; matrix products, arithmetic and copies ran while one was open for 0% -> 0% of each run, Pallas kernels for 14% -> 14%
where the time goes in v7:
time: 32 us; the launch traced here: 31.8 us
  starting transfers between devices  12.9 us (40%)
  waiting for transfers between devices  9.17 us (29%)
  Pallas kernels  9.07 us (28%)
  between operations  0.67 us (2%)
    ppermute x7, starting transfers between devices, swap(): return lax.ppermute(x, 'ka', [(i, i ^ by) for i in range(key_devices)])  10.8 us
    ppermute x7, waiting for transfers between devices, swap(): return lax.ppermute(x, 'ka', [(i, i ^ by) for i in range(key_devices)])  5.09 us
    pallas_call x2, Pallas kernels, rows(): pl.pallas_call(functools.partial(rows_kernel, key_devices, share, head_co...  4.84 us
    ppermute x2, waiting for transfers between devices, over_queries(): return [x, lax.ppermute(x, 'pb', [(0, 1), (1, 0)])]  4.08 us
    ppermute x2, starting transfers between devices, over_queries(): return [x, lax.ppermute(x, 'pb', [(0, 1), (1, 0)])]  2.16 us
    pallas_call x1, Pallas kernels, per_device(): pl.pallas_call(functools.partial(gather_kernel, row_sets, share), out_sha...  1.76 us
    pallas_call x1, Pallas kernels, per_device(): pl.pallas_call(prep_kernel, out_shape=(shape((2 * key_count + SUM_ROWS, w...  1.34 us
    pallas_call x1, Pallas kernels, per_device(): pl.pallas_call(functools.partial(finish_kernel, len(kept)), out_shape=(sh...  1.09 us
  transfers between devices with their start and end apart: 9, of which 4 were waited for; matrix products, arithmetic and copies ran while one was open for 0% of the time, Pallas kernels for 14%

profile of v7, /device:TPU:0, one launch (start us, length us, event | category | flops | bytes accessed | tf_op | source)
XLA Modules:
  0.0 31.8 jit_solution(6878229794710564763)
XLA Ops:
  0.6 1.3 %prep.1 = (bf16[400,128]{1,0:T(8,128)(2,1)S(1)}, bf16[400,128]{1,0:T(8,128)(2,1)S(1)}, f32[16,128]{1,0:T(8,128)S(1)}) custom-call(s32[2,3]{1,0:T(2,128)} %bitcast.9, bf16[192,2,128]{2,1,0:T(2,128)(2,1)} %codes_hbm.1, bf16[192,2,128]{2,1,0:T(2,128)(2,1)} %values_hbm.1), custom_call_target="tpu_custom_call" | custom-call | tf_op jit(solution)/shard_map/prep/pallas_call | solution.py:229
  2.0 3.1 %collective-permute-start = (bf16[400,128]{1,0:T(8,128)(2,1)S(1)}, bf16[400,128]{1,0:T(8,128)(2,1)S(1)}, u32[]{:S(2)}, u32[]{:S(2)}) collective-permute-start(bf16[400,128]{1,0:T(8,128)(2,1)S(1)} %get-tuple-element.17.refs_2_), channel_id=1, source_target_pairs={{0,4},{4,0},{8,12},{12,8},{1,5},{5,1},{9,13},{13,9},{2,6},{6,2},{1... | collective-permute-start | bytes 307208 | tf_op jit(solution)/shard_map/ppermute | solution.py:224
  5.1 2.6 %collective-permute-start.1 = (bf16[400,128]{1,0:T(8,128)(2,1)S(1)}, bf16[400,128]{1,0:T(8,128)(2,1)S(1)}, u32[]{:S(2)}, u32[]{:S(2)}) collective-permute-start(bf16[400,128]{1,0:T(8,128)(2,1)S(1)} %get-tuple-element.18.refs_3_), channel_id=1, source_target_pairs={{0,8},{4,12},{8,0},{12,4},{1,9},{5,13},{9,1},{13,5},{2,10},{6,14},... | collective-permute-start | bytes 307208 | tf_op jit(solution)/shard_map/ppermute | solution.py:224
  7.7 0.0 collective-permute-start.2
  7.7 1.8 %gather.1 = (bf16[2,2,768,256]{3,2,1,0:T(8,128)(2,1)S(1)}, bf16[2,2,768,256]{3,2,1,0:T(8,128)(2,1)S(1)}) custom-call(bf16[384,16,128]{2,1,0:T(8,128)(2,1)} %q_hbm.1, bf16[384,16,128]{2,1,0:T(8,128)(2,1)} %do_hbm.1, f32[16,384]{1,0:T(8,128)} %bitcast.7, f32[16,384]{1,0:T(8,128)} %bitcast.8), custom_call_target="tpu_custom_call" | custom-call | tf_op jit(solution)/shard_map/gather/pallas_call | solution.py:249
  9.4 3.7 %collective-permute-done.2.refs_6_ = f32[16,128]{1,0:T(8,128)S(1)} collective-permute-done((f32[16,128]{1,0:T(8,128)S(1)}, f32[16,128]{1,0:T(8,128)S(1)}, u32[]{:S(2)}, u32[]{:S(2)}) %collective-permute-start.2) | collective-permute-done | bytes 8224 | tf_op jit(solution)/shard_map/ppermute | solution.py:224
  13.1 0.0 collective-permute-done.refs_4_
  13.1 0.0 collective-permute-done.1.refs_5_
  13.1 2.4 %partner_keys.1 = (f32[2,2,128,768]{3,2,1,0:T(8,128)S(1)}, bf16[2,192,128]{2,1,0:T(8,128)(2,1)S(1)}, bf16[2,192,128]{2,1,0:T(8,128)(2,1)S(1)}) custom-call(bf16[2,2,768,256]{3,2,1,0:T(8,128)(2,1)S(1)} %get-tuple-element.15.refs_0_, bf16[2,2,768,256]{3,2,1,0:T(8,128)(2,1)S(1)} %get-tuple-element.16.refs_1_, bf16[400,128]{1,0:T(8,128)(2,1)S(1)} %get-tuple-element.17.refs_2_, ...), custom_call_target="tpu_custom_call" | custom-call | tf_op jit(solution)/shard_map/partner_keys/pallas_call | solution.py:273
  15.5 0.3 collective-permute-start.3
  15.8 2.5 %collective-permute-start.5 = (bf16[2,192,128]{2,1,0:T(8,128)(2,1)S(1)}, bf16[2,192,128]{2,1,0:T(8,128)(2,1)S(1)}, u32[]{:S(2)}, u32[]{:S(2)}) collective-permute-start(bf16[2,192,128]{2,1,0:T(8,128)(2,1)S(1)} %get-tuple-element.24), channel_id=1, source_target_pairs={{0,8},{4,12},{8,0},{12,4},{1,9},{5,13},{9,1},{13,5},{2,10},{6,14},... | collective-permute-start | bytes 294920 | tf_op jit(solution)/shard_map/ppermute | solution.py:224
  18.2 2.5 %own_keys.1 = (bf16[1,768,128]{2,1,0:T(8,128)(2,1)S(1)}, bf16[1,768,128]{2,1,0:T(8,128)(2,1)S(1)}, f32[2,768,128]{2,1,0:T(8,128)S(1)}, f32[4,192,128]{2,1,0:T(8,128)S(1)}) custom-call(bf16[2,2,768,256]{3,2,1,0:T(8,128)(2,1)S(1)} %get-tuple-element.15.refs_0_, bf16[2,2,768,256]{3,2,1,0:T(8,128)(2,1)S(1)} %get-tuple-element.16.refs_1_, ...), custom_call_target="tpu_custom_call" | custom-call | tf_op jit(solution)/shard_map/own_keys/pallas_call | solution.py:273
  20.7 0.5 %collective-permute-start.7 = (bf16[768,128]{1,0:T(8,128)(2,1)S(1)}, bf16[768,128]{1,0:T(8,128)(2,1)S(1)}, u32[]{:S(2)}, u32[]{:S(2)}) collective-permute-start(bf16[768,128]{1,0:T(8,128)(2,1)S(1)} %bitcast.6), channel_id=1, source_target_pairs={{0,8},{4,12},{8,0},{12,4},{1,9},{5,13},{9,1},{13,5},{2,10},{6,14},... | collective-permute-start | bytes 589832 | tf_op jit(solution)/shard_map/ppermute | solution.py:224
  21.2 1.8 %collective-permute-start.8 = (bf16[768,128]{1,0:T(8,128)(2,1)S(1)}, bf16[768,128]{1,0:T(8,128)(2,1)S(1)}, u32[]{:S(2)}, u32[]{:S(2)}) collective-permute-start(bf16[768,128]{1,0:T(8,128)(2,1)S(1)} %bitcast.5), channel_id=1, source_target_pairs={{0,4},{4,0},{8,12},{12,8},{1,5},{5,1},{9,13},{13,9},{2,6},{6,2},{1... | collective-permute-start | bytes 589832 | tf_op jit(solution)/shard_map/ppermute | solution.py:224
  23.0 0.0 collective-permute-done.3.got_ref
  23.1 1.6 %collective-permute-start.4 = (bf16[2,192,128]{2,1,0:T(8,128)(2,1)S(1)}, bf16[2,192,128]{2,1,0:T(8,128)(2,1)S(1)}, u32[]{:S(2)}, u32[]{:S(2)}) collective-permute-start(bf16[2,192,128]{2,1,0:T(8,128)(2,1)S(1)} %join.2.refs_0_), channel_id=1, source_target_pairs={{0,16},{16,0},{1,17},{17,1},{2,18},{18,2},{3,19},{19,3},{4,20},{20... | collective-permute-start | bytes 294920 | tf_op jit(solution)/shard_map/ppermute | solution.py:306
  24.6 0.0 collective-permute-done.5.got_ref
  24.7 0.6 %collective-permute-start.6 = (bf16[2,192,128]{2,1,0:T(8,128)(2,1)S(1)}, bf16[2,192,128]{2,1,0:T(8,128)(2,1)S(1)}, u32[]{:S(2)}, u32[]{:S(2)}) collective-permute-start(bf16[2,192,128]{2,1,0:T(8,128)(2,1)S(1)} %join.3.refs_2_), channel_id=1, source_target_pairs={{0,16},{16,0},{1,17},{17,1},{2,18},{18,2},{3,19},{19,3},{4,20},{20... | collective-permute-start | bytes 294920 | tf_op jit(solution)/shard_map/ppermute | solution.py:306
  25.3 2.5 %collective-permute-done.4.refs_1_ = bf16[2,192,128]{2,1,0:T(8,128)(2,1)S(1)} collective-permute-done((bf16[2,192,128]{2,1,0:T(8,128)(2,1)S(1)}, bf16[2,192,128]{2,1,0:T(8,128)(2,1)S(1)}, u32[]{:S(2)}, u32[]{:S(2)}) %collective-permute-start.4) | collective-permute-done | bytes 98336 | tf_op jit(solution)/shard_map/ppermute | solution.py:306
  27.8 1.6 %collective-permute-done.6.refs_3_ = bf16[2,192,128]{2,1,0:T(8,128)(2,1)S(1)} collective-permute-done((bf16[2,192,128]{2,1,0:T(8,128)(2,1)S(1)}, bf16[2,192,128]{2,1,0:T(8,128)(2,1)S(1)}, u32[]{:S(2)}, u32[]{:S(2)}) %collective-permute-start.6) | collective-permute-done | bytes 98336 | tf_op jit(solution)/shard_map/ppermute | solution.py:306
  29.3 1.4 %collective-permute-done.7.refs_4_ = bf16[768,128]{1,0:T(8,128)(2,1)S(1)} collective-permute-done((bf16[768,128]{1,0:T(8,128)(2,1)S(1)}, bf16[768,128]{1,0:T(8,128)(2,1)S(1)}, u32[]{:S(2)}, u32[]{:S(2)}) %collective-permute-start.7) | collective-permute-done | bytes 196640 | tf_op jit(solution)/shard_map/ppermute | solution.py:224
  30.7 0.0 collective-permute-done.8.refs_5_
  30.8 1.1 %finish.1 = (bf16[96,16,128]{2,1,0:T(8,128)(2,1)}, bf16[192,2,128]{2,1,0:T(2,128)(2,1)}, bf16[192,2,128]{2,1,0:T(2,128)(2,1)}) custom-call(f32[2,768,128]{2,1,0:T(8,128)S(1)} %get-tuple-element.21.own_ref, bf16[2,192,128]{2,1,0:T(8,128)(2,1)S(1)} %join.2.refs_0_, bf16[2,192,128]{2,1,0:T(8,128)(2,1)S(1)} %collective-permute-done.4.refs_1_, ...), custom_call_target="tpu_custom_call" | custom-call | tf_op jit(solution)/shard_map/finish/pallas_call | solution.py:324
  (2 shorter events, 0.0 us)
Async XLA Ops:
  2.0 11.1 %collective-permute-start = (bf16[400,128]{1,0:T(8,128)(2,1)S(1)}, bf16[400,128]{1,0:T(8,128)(2,1)S(1)}, u32[]{:S(2)}, u32[]{:S(2)}) collective-permute-start(bf16[400,128]{1,0:T(8,128)(2,1)S(1)} %get-tuple-element.17.refs_2_), channel_id=1, source_target_pairs={{0,4},{4,0},{8,12},{12,8},{1,5},{5,1},{9,13},{13,9},{2,6},{6,2},{1... | collective-permute-start | bytes 307208 | tf_op jit(solution)/shard_map/ppermute | solution.py:224
  5.1 8.0 %collective-permute-start.1 = (bf16[400,128]{1,0:T(8,128)(2,1)S(1)}, bf16[400,128]{1,0:T(8,128)(2,1)S(1)}, u32[]{:S(2)}, u32[]{:S(2)}) collective-permute-start(bf16[400,128]{1,0:T(8,128)(2,1)S(1)} %get-tuple-element.18.refs_3_), channel_id=1, source_target_pairs={{0,8},{4,12},{8,0},{12,4},{1,9},{5,13},{9,1},{13,5},{2,10},{6,14},... | collective-permute-start | bytes 307208 | tf_op jit(solution)/shard_map/ppermute | solution.py:224
  7.7 5.4 %collective-permute-start.2 = (f32[16,128]{1,0:T(8,128)S(1)}, f32[16,128]{1,0:T(8,128)S(1)}, u32[]{:S(2)}, u32[]{:S(2)}) collective-permute-start(f32[16,128]{1,0:T(8,128)S(1)} %get-tuple-element.19), channel_id=1, source_target_pairs={{0,12},{4,8},{8,4},{12,0},{1,13},{5,9},{9,5},{13,1},{2,14},{6,10},... | collective-permute-start | bytes 24584 | tf_op jit(solution)/shard_map/ppermute | solution.py:224
  15.5 7.6 %collective-permute-start.3 = (bf16[2,192,128]{2,1,0:T(8,128)(2,1)S(1)}, bf16[2,192,128]{2,1,0:T(8,128)(2,1)S(1)}, u32[]{:S(2)}, u32[]{:S(2)}) collective-permute-start(bf16[2,192,128]{2,1,0:T(8,128)(2,1)S(1)} %get-tuple-element.23), channel_id=1, source_target_pairs={{0,4},{4,0},{8,12},{12,8},{1,5},{5,1},{9,13},{13,9},{2,6},{6,2},{1... | collective-permute-start | bytes 294920 | tf_op jit(solution)/shard_map/ppermute | solution.py:224
  15.8 8.9 %collective-permute-start.5 = (bf16[2,192,128]{2,1,0:T(8,128)(2,1)S(1)}, bf16[2,192,128]{2,1,0:T(8,128)(2,1)S(1)}, u32[]{:S(2)}, u32[]{:S(2)}) collective-permute-start(bf16[2,192,128]{2,1,0:T(8,128)(2,1)S(1)} %get-tuple-element.24), channel_id=1, source_target_pairs={{0,8},{4,12},{8,0},{12,4},{1,9},{5,13},{9,1},{13,5},{2,10},{6,14},... | collective-permute-start | bytes 294920 | tf_op jit(solution)/shard_map/ppermute | solution.py:224
  20.7 10.0 %collective-permute-start.7 = (bf16[768,128]{1,0:T(8,128)(2,1)S(1)}, bf16[768,128]{1,0:T(8,128)(2,1)S(1)}, u32[]{:S(2)}, u32[]{:S(2)}) collective-permute-start(bf16[768,128]{1,0:T(8,128)(2,1)S(1)} %bitcast.6), channel_id=1, source_target_pairs={{0,8},{4,12},{8,0},{12,4},{1,9},{5,13},{9,1},{13,5},{2,10},{6,14},... | collective-permute-start | bytes 589832 | tf_op jit(solution)/shard_map/ppermute | solution.py:224
  21.2 9.5 %collective-permute-start.8 = (bf16[768,128]{1,0:T(8,128)(2,1)S(1)}, bf16[768,128]{1,0:T(8,128)(2,1)S(1)}, u32[]{:S(2)}, u32[]{:S(2)}) collective-permute-start(bf16[768,128]{1,0:T(8,128)(2,1)S(1)} %bitcast.5), channel_id=1, source_target_pairs={{0,4},{4,0},{8,12},{12,8},{1,5},{5,1},{9,13},{13,9},{2,6},{6,2},{1... | collective-permute-start | bytes 589832 | tf_op jit(solution)/shard_map/ppermute | solution.py:224
  23.1 4.7 %collective-permute-start.4 = (bf16[2,192,128]{2,1,0:T(8,128)(2,1)S(1)}, bf16[2,192,128]{2,1,0:T(8,128)(2,1)S(1)}, u32[]{:S(2)}, u32[]{:S(2)}) collective-permute-start(bf16[2,192,128]{2,1,0:T(8,128)(2,1)S(1)} %join.2.refs_0_), channel_id=1, source_target_pairs={{0,16},{16,0},{1,17},{17,1},{2,18},{18,2},{3,19},{19,3},{4,20},{20... | collective-permute-start | bytes 294920 | tf_op jit(solution)/shard_map/ppermute | solution.py:306
  24.7 4.7 %collective-permute-start.6 = (bf16[2,192,128]{2,1,0:T(8,128)(2,1)S(1)}, bf16[2,192,128]{2,1,0:T(8,128)(2,1)S(1)}, u32[]{:S(2)}, u32[]{:S(2)}) collective-permute-start(bf16[2,192,128]{2,1,0:T(8,128)(2,1)S(1)} %join.3.refs_2_), channel_id=1, source_target_pairs={{0,16},{16,0},{1,17},{17,1},{2,18},{18,2},{3,19},{19,3},{4,20},{20... | collective-permute-start | bytes 294920 | tf_op jit(solution)/shard_map/ppermute | solution.py:306
